TPU v7x, 32 devices: a whole 2x2x4 slice. The times are simulated.
32 devices in a mesh: section: 4 (over y, core), dp: 8 (over z, x).
Axes of the slice: x: 2, y: 2, z: 4, core: 2. Of those that a mesh axis runs over, the one named last changes fastest.
Arguments:
- entry_states: bfloat16 [5, 256, 4608], P(None, 'dp'), may hold values from -6 to 6
- down_proj: bfloat16 [4, 4, 4608, 128], P('section'), may hold values from -0.09375 to 0.09375
- up_proj: bfloat16 [4, 4, 4608, 128], P('section'), may hold values from -0.5 to 0.5
- label_rows: bfloat16 [256, 4608], replicated, may hold values from -0.375 to 0.375
- sampled_labels: int32 [4, 5, 256], P(None, None, 'dp'), may hold values from 0 to 255
- eval_states: bfloat16 [256, 4608], P('dp'), may hold values from -6 to 6
Outputs:
- eval_out: bfloat16 [4, 256, 4608], P('section', 'dp')
- label_logprob: float32 [4, 5, 256], P('section', None, 'dp')
- fisher_log: float32 [4, 2, 4608, 128], P('section', None, 'dp')
All inputs are finite; a program needn't handle non-finite values.
Results may differ from a plain program's by a relative error of at most 0.0065.
Values may be sent and summed in bfloat16 or wider, within the bound.
No kernel may reach another device: no remote copies, remote signals or barrier semaphores. Data moves between devices by JAX's collectives and lax.ppermute only.
A program may use at most 128 MiB of HBM per device.

v0:
```python
import functools

import jax
import jax.numpy as jnp
from jax import lax
from jax.experimental import pallas as pl
from jax.experimental.pallas import tpu as pltpu
from jax.sharding import PartitionSpec as P

norm_eps = 1e-06
merge_eps = 1e-06
soft_cap = 30.0
gelu_coef = 0.7978845608028654
vmem_bytes = 56 * 1024 * 1024
bf16 = jnp.bfloat16
f32 = jnp.float32


def nt_dot(lhs, rhs):
    return lax.dot_general(lhs, rhs, (((1,), (1,)), ((), ())), preferred_element_type=f32)


def nn_dot(lhs, rhs):
    return lax.dot_general(lhs, rhs, (((1,), (0,)), ((), ())), preferred_element_type=f32)


def tn_dot(lhs, rhs):
    return lax.dot_general(lhs, rhs, (((0,), (0,)), ((), ())), preferred_element_type=f32)


def gelu_value(hidden):
    inner = gelu_coef * (hidden + 0.044715 * hidden * hidden * hidden)
    return 0.5 * hidden * (1.0 + jnp.tanh(inner))


def gelu_slope(hidden):
    inner = gelu_coef * (hidden + 0.044715 * hidden * hidden * hidden)
    tanh_value = jnp.tanh(inner)
    return 0.5 * (1.0 + tanh_value) + 0.5 * hidden * (1.0 - tanh_value * tanh_value) * gelu_coef * (
        1.0 + 3.0 * 0.044715 * hidden * hidden
    )


def tiled(width):
    count = max(n for n in (1, 2, 3) if width % (128 * n) == 0)
    size = width // count

    def loop(body, start=None):
        def step(index, carry):
            return body(pl.ds(pl.multiple_of(index * size, 128), size), carry)

        return lax.fori_loop(0, count, step, start)

    return loop


def row_scale(total, width):
    return lax.rsqrt(total / width + norm_eps)


def row_sum(values):
    return jnp.sum(values, axis=-1, keepdims=True)


def square(values):
    wide = values.astype(f32)
    return (wide * wide).astype(bf16)


def zeros(*shape):
    return jnp.zeros(shape, f32)


def label_head(states, labels, label_rows, grads):
    tasks, rows, width = states.shape
    loop, words = tiled(width), label_rows.shape[0]

    def joined(cols):
        return jnp.concatenate([states[task, :, cols] for task in range(tasks)], axis=0)

    def score(cols, carry):
        total, logits = carry
        part = joined(cols)
        wide = part.astype(f32)
        return total + row_sum(wide * wide), logits + nt_dot(part, label_rows[:, cols])

    total, logits = loop(score, (zeros(tasks * rows, 1), zeros(tasks * rows, words)))
    scale = row_scale(total, width)
    bent = jnp.tanh(logits * scale / soft_cap)
    capped = soft_cap * bent
    logprob = capped - jnp.log(row_sum(jnp.exp(capped)))
    one_hot = (labels == lax.broadcasted_iota(jnp.int32, logprob.shape, 1)).astype(f32)
    slope = ((jnp.exp(logprob) - one_hot) * (1.0 - bent * bent)).astype(bf16)

    def product(cols, total):
        return total + row_sum(nn_dot(slope, label_rows[:, cols]) * joined(cols).astype(f32))

    mean = loop(product, zeros(tasks * rows, 1)) * scale / width

    def finish(cols, carry):
        wide = joined(cols).astype(f32)
        grad = (scale * (nn_dot(slope, label_rows[:, cols]) - wide * (scale * mean))).astype(bf16)
        for task in range(tasks):
            grads[task, :, cols] = grad[task * rows:(task + 1) * rows]
        return carry

    loop(finish, 0)
    return row_sum(logprob * one_hot)


class Copies:
    def __init__(self, sems):
        self.sems, self.used = sems, 0

    def start(self, source, target):
        copy = pltpu.make_async_copy(source, target, self.sems.at[self.used])
        self.used += 1
        copy.start()
        return copy


class StageWeights:
    def __init__(self, member, own, other, held, sems):
        self.member, self.own, self.other = member, own, other
        self.held, self.sems = held, sems
        self.tasks = held[0].shape[1]

    def copy(self, kind, layer, task):
        return pltpu.make_async_copy(
            self.other[kind].at[task], self.held[kind].at[layer, task], self.sems.at[kind, layer, task]
        )

    def start(self, order):
        for kind, layer in order:
            @pl.when(self.member == layer)
            def _():
                for task in range(self.tasks):
                    pltpu.make_async_copy(
                        self.own[kind].at[layer * self.tasks + task],
                        self.held[kind].at[layer, task],
                        self.sems.at[kind, layer, task],
                    ).start()

            @pl.when(self.member != layer)
            def _():
                for task in range(self.tasks):
                    self.copy(kind, layer, task).start()

    def wait(self, kind, layer, task):
        self.copy(kind, layer, task).wait()


def forward_loop(levels, hidden, scales, weights, held_down, held_up, done):
    tasks, (rows, width), rank = range(levels.shape[1]), levels.shape[2:], held_down.shape[-1]
    loop = tiled(width)

    @pl.loop(0, 2)
    def _(layer):
        for task in tasks:
            weights.wait(0, layer, task)

        def down(cols, carry):
            result = []
            for task in tasks:
                part = levels[layer, task, :, cols]
                wide = part.astype(f32)
                total, pre = carry[task]
                result.append((total + row_sum(wide * wide), pre + nn_dot(part, held_down[layer, task, cols])))
            return tuple(result)

        found = loop(down, tuple((zeros(rows, 1), zeros(rows, rank)) for _ in tasks))
        active = []
        for task in tasks:
            scale = row_scale(found[task][0], width)
            pre = found[task][1] * scale
            scales[layer, task] = jnp.broadcast_to(scale, (rows, 128))
            hidden[layer, task] = pre
            active.append(gelu_value(pre).astype(bf16))
        for task in tasks:
            weights.wait(1, layer, task)

        def up(cols, carry):
            update = [nt_dot(active[task], held_up[layer, task, cols]) for task in tasks]
            for task in tasks:
                levels[layer + 1, task, :, cols] = (
                    levels[layer, task, :, cols].astype(f32) + update[task]
                ).astype(bf16)
            return carry

        loop(up, 0)
        done(layer)


class Squares:
    def __init__(self, wide, narrow, wide_out, narrow_out, sems):
        self.pairs = ((wide, wide_out), (narrow, narrow_out))
        self.sems = sems

    def copy(self, width, layer, kind, task):
        source, target = self.pairs[width]
        return pltpu.make_async_copy(
            source.at[layer, kind, task], target.at[layer, kind, task], self.sems.at[width, layer, kind, task]
        )

    def set_wide(self, layer, kind, task, cols, value):
        self.pairs[0][0][layer, kind, task, :, cols] = value

    def set_narrow(self, layer, kind, task, value):
        self.pairs[1][0][layer, kind, task] = value

    def start(self, layer, kind, task):
        for width in range(2):
            self.copy(width, layer, kind, task).start()

    def wait(self):
        tasks = self.pairs[0][0].shape[2]

        @pl.loop(0, 2 * tasks)
        def _(index):
            for kind in range(2):
                for width in range(2):
                    self.copy(width, index // tasks, kind, index % tasks).wait()


def backward_step(layer, levels, grads, hidden, scales, weights, held_down, held_up, squares, pass_on):
    tasks, (rows, width), rank = range(levels.shape[1]), levels.shape[2:], held_down.shape[-1]
    loop = tiled(width)
    if weights is not None:
        for task in tasks:
            weights.wait(1, layer, task)
    scale = [scales[layer, task][:, :1] for task in tasks]

    def up(cols, carry):
        result = []
        for task in tasks:
            grad = grads[layer + 1, task, :, cols]
            result.append(carry[task] + nn_dot(grad, held_up[layer, task, cols]))
            norm = (levels[layer, task, :, cols].astype(f32) * scale[task]).astype(bf16)
            squares.set_wide(layer, 0, task, cols, square(norm))
            squares.set_wide(layer, 1, task, cols, square(grad))
        return tuple(result)

    grad_act = loop(up, tuple(zeros(rows, rank) for _ in tasks))
    grad_hidden = []
    for task in tasks:
        pre = hidden[layer, task]
        grad_hidden.append((grad_act[task] * gelu_slope(pre)).astype(bf16))
        squares.set_narrow(layer, 0, task, square(grad_hidden[task]))
        squares.set_narrow(layer, 1, task, square(gelu_value(pre).astype(bf16)))
    for task in tasks:
        for kind in range(2):
            squares.start(layer, kind, task)
    if not pass_on:
        return
    if weights is not None:
        for task in tasks:
            weights.wait(0, layer, task)

    def product(cols, carry):
        grad_norm = [nt_dot(grad_hidden[task], held_down[layer, task, cols]) for task in tasks]
        return tuple(
            carry[task] + row_sum(grad_norm[task] * levels[layer, task, :, cols].astype(f32)) for task in tasks
        )

    found = loop(product, tuple(zeros(rows, 1) for _ in tasks))
    pull = [scale[task] * scale[task] * found[task] / width for task in tasks]

    def finish(cols, carry):
        grad_norm = [nt_dot(grad_hidden[task], held_down[layer, task, cols]) for task in tasks]
        for task in tasks:
            wide = levels[layer, task, :, cols].astype(f32)
            grads[layer, task, :, cols] = (
                grads[layer + 1, task, :, cols].astype(f32) + scale[task] * (grad_norm[task] - wide * pull[task])
            ).astype(bf16)
        return carry

    loop(finish, 0)


def first_forward_kernel(turn, place, entry, down, up, down_other, up_other, out, middle, hidden, scales_out,
                         levels, pre, scales, sems, held_down, held_up, weight_sems):
    @pl.when(place[0] == 0)
    def _():
        tasks = out.shape[0]
        copies = Copies(sems)
        loads = [copies.start(entry.at[turn], levels.at[0, task]) for task in range(tasks)]
        weights = StageWeights(place[1], (down, up), (down_other, up_other), (held_down, held_up), weight_sems)
        weights.start([(0, 0), (1, 0), (0, 1), (1, 1)])
        for load in loads:
            load.wait()
        base = copies.used

        def leave(layer, task):
            return pltpu.make_async_copy(
                levels.at[layer + 1, task], (middle, out)[layer].at[task], sems.at[base + layer * tasks + task]
            )

        def done(layer):
            for fixed in range(2):
                @pl.when(layer == fixed)
                def _():
                    for task in range(tasks):
                        leave(fixed, task).start()

        forward_loop(levels, pre, scales, weights, held_down, held_up, done)
        last = [pltpu.make_async_copy(pre, hidden, sems.at[0]), pltpu.make_async_copy(scales, scales_out, sems.at[1])]
        for copy in last:
            copy.start()
        for layer in range(2):
            for task in range(tasks):
                leave(layer, task).wait()
        for copy in last:
            copy.wait()


def first_backward_kernel(turn, place, grad, entry, middle, hidden, scales_in, wide_in, narrow_in, down, up, down_other, up_other,
                          wide_out, narrow_out, grads, levels, pre, scales, wide, narrow, square_sems, sems,
                          held_down, held_up, weight_sems):
    del wide_in, narrow_in

    @pl.when(place[0] == 0)
    def _():
        tasks = middle.shape[0]
        copies = Copies(sems)
        loads = [copies.start(grad, grads.at[2]), copies.start(hidden, pre), copies.start(middle, levels.at[1])]
        loads.append(copies.start(scales_in, scales))
        weights = StageWeights(place[1], (down, up), (down_other, up_other), (held_down, held_up), weight_sems)
        weights.start([(1, 1), (0, 1), (1, 0)])
        loads += [copies.start(entry.at[turn], levels.at[0, task]) for task in range(tasks)]
        squares = Squares(wide, narrow, wide_out, narrow_out, square_sems)
        for load in loads:
            load.wait()
        for layer in (1, 0):
            backward_step(layer, levels, grads, pre, scales, weights, held_down, held_up, squares, layer == 1)
        squares.wait()


def last_stage_kernel(turn, place, states, labels, label_rows, down, up, down_other, up_other,
                      grad_out, picked, wide_out, narrow_out,
                      levels, words, marks, chosen, pre, scales, grads, wide, narrow, square_sems, sems,
                      held_down, held_up, weight_sems):
    @pl.when(place[0] == 1)
    def _():
        tasks, rows = states.shape[0], states.shape[1]
        copies = Copies(sems)
        loaded = copies.start(states, levels.at[0])
        weights = StageWeights(place[1], (down, up), (down_other, up_other), (held_down, held_up), weight_sems)
        weights.start([(0, 0), (1, 0), (0, 1), (1, 1)])
        later = [copies.start(label_rows, words), copies.start(labels.at[turn], marks)]
        loaded.wait()
        forward_loop(levels, pre, scales, weights, held_down, held_up, lambda layer: None)
        for copy in later:
            copy.wait()

        values = label_head(levels.at[2], marks[...], words, grads.at[2])
        for task in range(tasks):
            part = slice(task * rows, (task + 1) * rows)
            chosen[task] = jnp.broadcast_to(values[part], (rows, 128)).T[0:8]

        out_copy = copies.start(chosen, picked)
        squares = Squares(wide, narrow, wide_out, narrow_out, square_sems)

        @pl.loop(0, 2)
        def _(index):
            backward_step(1 - index, levels, grads, pre, scales, None, held_down, held_up, squares, True)

        last = copies.start(grads.at[0], grad_out)
        squares.wait()
        out_copy.wait()
        last.wait()


def eval_kernel(step, offsets, place, states, before, *refs):
    *pieces, out, base, top, held, sems = refs
    copies = Copies(sems)
    rows = pieces[0].shape[1]

    @pl.when(place[2] == step)
    def _():
        loads = [[copies.start(states, base)], [], []]
        for kind in range(2):
            for index, piece in enumerate(pieces):
                block = block_at(place[3], offsets[index], len(pieces))
                spot = pl.ds(pl.multiple_of(block * rows, 16), rows)
                loads[1 + kind].append(copies.start(piece.at[kind], held.at[kind, spot]))
        for load in loads[0]:
            load.wait()
        total_rows, width = base.shape
        loop = tiled(width)

        def squared(cols, total):
            wide = base[:, cols].astype(f32)
            return total + row_sum(wide * wide)

        scale = row_scale(loop(squared, zeros(total_rows, 1)), width)
        for load in loads[1]:
            load.wait()
        pre = loop(lambda cols, sums: sums + nn_dot(base[:, cols], held[0, cols]), zeros(total_rows, held.shape[-1]))
        active = gelu_value(pre * scale).astype(bf16)
        for load in loads[2]:
            load.wait()

        def up(cols, carry):
            top[:, cols] = (base[:, cols].astype(f32) + nt_dot(active, held[1, cols])).astype(bf16)
            return carry

        loop(up, 0)
        copies.start(top, out).wait()

    @pl.when(place[2] != step)
    def _():
        copies.start(before, base).wait()
        copies.start(base, out).wait()


def fisher_kernel(turns, place, *refs):
    wides, narrows = refs[:turns], refs[turns:2 * turns]
    weights, outs = refs[2 * turns:2 * turns + 2], refs[2 * turns + 2:]
    del place
    for kind in range(2):
        top, total = None, None
        for task in range(weights[0].shape[0]):
            left = jnp.concatenate([ref[0, kind, task] for ref in wides], axis=0)
            right = jnp.concatenate([ref[0, kind, task] for ref in narrows], axis=0)
            term = tn_dot(left, right)
            scaled = term * weights[kind][task].astype(f32)
            top = scaled if top is None else top + scaled
            total = term if total is None else total + term
        outs[0][kind] = top.astype(bf16)
        outs[1][kind] = total.astype(bf16)


def block_size(width):
    return max(size for size in range(128, 513, 128) if width % size == 0)


smem = pl.BlockSpec(memory_space=pltpu.SMEM)
anywhere = pl.BlockSpec(memory_space=pl.ANY)
hbm = pl.BlockSpec(memory_space=pltpu.HBM)


def send(block, axis, route):
    return lax.ppermute(block, axis, route)


def walk(spot, count):
    if count % 2:
        return spot
    return jnp.where(spot < count // 2, 2 * spot, 2 * (count - 1 - spot) + 1)


def spot_of(device, count):
    if count % 2:
        return device
    return jnp.where(lax.rem(device, 2) == 0, lax.div(device, 2), count - 1 - lax.div(device, 2))


def block_at(spot, offset, count):
    return walk(lax.rem(spot + offset + 2 * count, count), count)


def ring_routes(axis):
    count = lax.axis_size(axis)
    order = list(range(count)) if count % 2 else list(range(0, count, 2)) + list(range(count - 1, 0, -2))
    ahead = [(order[i], order[(i + 1) % count]) for i in range(count)]
    return count, ahead, [(j, i) for i, j in ahead]


def ring_scatter(own, other, spot, axis):
    count, ahead, back = ring_routes(axis)
    rows = own[0].shape[1] // count

    def part(index, offset):
        start = block_at(spot, offset, count) * rows
        return sum(
            lax.dynamic_slice_in_dim(array[index], start, rows, 1).astype(f32) for array in (own, other)
        )

    moving = [part(0, -1).astype(bf16), part(1, 1).astype(bf16)]
    for step in range(count - 1):
        last = step == count - 2
        landed = [send(moving[0], axis, ahead), send(moving[1], axis, back)]
        sums = [landed[0].astype(f32) + part(0, -2 - step), landed[1].astype(f32) + part(1, 2 + step)]
        moving = sums if last else [value.astype(bf16) for value in sums]
    return moving


def ring_gather(own, axis):
    count, ahead, back = ring_routes(axis)
    pieces, offsets = [own], [0]
    down = up = own
    for step in range(1, count // 2 + 1):
        down = send(down, axis, ahead)
        pieces.append(down)
        offsets.append(-step)
        if len(pieces) < count:
            up = send(up, axis, back)
            pieces.append(up)
            offsets.append(step)
    return pieces, offsets


def after(value, done):
    return lax.optimization_barrier((value, done))[0]


def local(entry_states, down_proj, up_proj, label_rows, sampled_labels, eval_states):
    section_count = lax.axis_size("section")
    section = lax.axis_index("section")
    stage, member = section // 2, section % 2
    w_down, w_up = down_proj[0], up_proj[0]
    all_tasks, width, rank = w_down.shape
    tasks = all_tasks // 2
    micro, rows, _ = entry_states.shape
    label_count = label_rows.shape[0]
    spot = spot_of(lax.axis_index("dp"), lax.axis_size("dp"))
    place = jnp.stack([stage, member, section, spot]).astype(jnp.int32)
    sections = range(section_count)
    swap = [(i, i ^ 1) for i in sections]
    upward = [(i, i + 2) for i in sections if i + 2 < section_count]
    downward = [(i, i - 2) for i in sections if i - 2 >= 0]

    away = (1 - member) * tasks
    down_other = send(lax.dynamic_slice_in_dim(w_down, away, tasks, 0), "section", swap)
    up_other = send(lax.dynamic_slice_in_dim(w_up, away, tasks, 0), "section", swap)
    weights = (w_down, w_up, down_other, up_other)

    held = [
        pltpu.VMEM((2, tasks, width, rank), bf16),
        pltpu.VMEM((2, tasks, width, rank), bf16),
        pltpu.SemaphoreType.DMA((2, 2, tasks)),
    ]
    params = pltpu.CompilerParams(vmem_limit_bytes=vmem_bytes)
    state_shape, hidden_shape = (tasks, rows, width), (2, tasks, rows, rank)
    wide_shape, narrow_shape = (2, 2, tasks, rows, width), (2, 2, tasks, rows, rank)
    state_type = jax.ShapeDtypeStruct(state_shape, bf16)
    square_types = (jax.ShapeDtypeStruct(wide_shape, bf16), jax.ShapeDtypeStruct(narrow_shape, bf16))
    square_scratch = [
        pltpu.VMEM(wide_shape, bf16),
        pltpu.VMEM(narrow_shape, bf16),
        pltpu.SemaphoreType.DMA((2, 2, 2, tasks)),
    ]
    layer_flops = 4 * tasks * rows * width * rank
    weight_bytes = 8 * tasks * width * rank

    def stage_call(kernel, turn, name, operands, outputs, scratch, flops, hbm_in=(), hbm_out=(), **more):
        return pl.pallas_call(
            functools.partial(kernel, turn),
            out_shape=outputs,
            in_specs=[smem] + [hbm if index in hbm_in else anywhere for index in range(1, operands + 1)],
            out_specs=tuple(hbm if index in hbm_out else anywhere for index in range(len(outputs))),
            scratch_shapes=scratch + held,
            compiler_params=params,
            cost_estimate=pl.CostEstimate(flops=flops, bytes_accessed=weight_bytes, transcendentals=0),
            name=name,
            **more,
        )

    own_labels = lax.dynamic_slice_in_dim(sampled_labels, member * tasks, tasks, 0)
    label_columns = own_labels.transpose(1, 0, 2).reshape(micro, tasks * rows, 1)
    saved, crossing, returned, picked = {}, {}, {}, {}
    squares = {}
    token = place

    levels, pre = pltpu.VMEM((3,) + state_shape, bf16), pltpu.VMEM(hidden_shape, f32)
    scale_shape = (2, tasks, rows, 128)
    scales, scale_type = pltpu.VMEM(scale_shape, f32), jax.ShapeDtypeStruct(scale_shape, f32)

    def first_forward(turn):
        nonlocal token
        call = stage_call(
            first_forward_kernel, turn, "first_forward", 5,
            (state_type, state_type, jax.ShapeDtypeStruct(hidden_shape, f32), scale_type),
            [levels, pre, scales, pltpu.SemaphoreType.DMA((3 * tasks,))],
            2 * layer_flops, hbm_in=(1, 2, 3, 4, 5), hbm_out=(1, 2, 3),
        )
        out, middle, hidden, scale = call(token, entry_states, *weights)
        saved[turn] = (entry_states, middle, hidden, scale)
        crossing[turn] = out
        token = after(place, scale)

    def cross(turn):
        nonlocal token
        out = lax.optimization_barrier((crossing[turn], token))[0]
        crossing[turn] = send(out, "section", upward)

    def last_stage(turn):
        nonlocal token
        call = stage_call(
            last_stage_kernel, turn, "last_stage", 7,
            (state_type, jax.ShapeDtypeStruct((tasks, 8, rows), f32)) + square_types,
            [
                levels, pltpu.VMEM(label_rows.shape, bf16),
                pltpu.VMEM((tasks * rows, 1), jnp.int32), pltpu.VMEM((tasks, 8, rows), f32),
                pre, scales, levels,
            ] + square_scratch + [pltpu.SemaphoreType.DMA((5,))],
            4 * layer_flops + 4 * tasks * rows * width * label_count,
            hbm_in=(3, 4, 5, 6, 7), hbm_out=(2, 3),
        )
        grad, picked[turn], *squares[turn] = call(
            token, crossing[turn], label_columns, label_rows, *weights
        )
        returned[turn] = send(grad, "section", downward)
        token = after(place, picked[turn])

    def first_backward(turn):
        nonlocal token
        call = stage_call(
            first_backward_kernel, turn, "first_backward", 11, square_types,
            [levels, levels, pre, scales] + square_scratch + [pltpu.SemaphoreType.DMA((4 + tasks,))],
            2 * layer_flops,
            hbm_in=range(2, 12), hbm_out=(0, 1),
            input_output_aliases={6: 0, 7: 1},
        )
        squares[turn] = call(token, returned[turn], *saved[turn], *squares[turn], *weights)
        token = after(place, squares[turn][1])

    ahead, behind = min(3, micro), 2
    for turn in range(ahead):
        first_forward(turn)
        cross(turn)
    for turn in range(micro):
        if turn + ahead < micro:
            first_forward(turn + ahead)
        if turn >= behind:
            first_backward(turn - behind)
            if turn + 1 in crossing:
                token = after(token, crossing[turn + 1])
        last_stage(turn)
        if turn + ahead < micro:
            cross(turn + ahead)
    for turn in range(max(micro - behind, 0), micro - 1):
        first_backward(turn)
    picked_all = jnp.stack([picked[turn][:, 0] for turn in range(micro)], axis=0)
    label_logprob = jnp.zeros((micro, rows), f32)
    for index in range(tasks):
        route = [(section_count - 2 + m, m * tasks + index) for m in range(2)]
        landed = send(picked_all[:, index], "section", route)
        label_logprob = jnp.where(section % tasks == index, landed, label_logprob)

    token = after(place, label_logprob)
    first_backward(micro - 1)

    block = block_size(width)

    def fisher(away, order):
        turns = len(squares)

        def layer_of(s):
            return 1 - s[1] if away else s[1]

        call = pl.pallas_call(
            functools.partial(fisher_kernel, turns),
            out_shape=(jax.ShapeDtypeStruct((2, width, rank), bf16),) * 2,
            grid_spec=pltpu.PrefetchScalarGridSpec(
                num_scalar_prefetch=1,
                grid=(width // block,),
                in_specs=[pl.BlockSpec((1, 2, tasks, rows, block), lambda i, s: (layer_of(s), 0, 0, 0, i))] * turns
                + [pl.BlockSpec((1, 2, tasks, rows, rank), lambda i, s: (layer_of(s), 0, 0, 0, 0))] * turns
                + [pl.BlockSpec((tasks, block, rank), lambda i, s: (0 if away else s[1], i, 0))] * 2,
                out_specs=(pl.BlockSpec((2, block, rank), lambda i, s: (0, i, 0)),) * 2,
            ),
            compiler_params=pltpu.CompilerParams(vmem_limit_bytes=vmem_bytes),
            cost_estimate=pl.CostEstimate(
                flops=4 * tasks * turns * rows * width * rank,
                bytes_accessed=turns * 8 * tasks * rows * width,
                transcendentals=0,
            ),
            name="fisher_away" if away else "fisher_own",
        )
        return call(
            order, *[squares[turn][0] for turn in range(turns)], *[squares[turn][1] for turn in range(turns)],
            *(weights[2:] if away else weights[:2]),
        )

    away_sums = fisher(True, token)
    other_sums = [send(value, "section", swap) for value in away_sums]
    sums = fisher(False, after(place, away_sums[0]))
    shares = ring_scatter(sums, other_sums, spot, "dp")
    numerator, denominator = shares
    merged_part = (numerator / (denominator + merge_eps)).astype(bf16)
    pieces, offsets = ring_gather(merged_part, "dp")
    fisher_log = jnp.log(denominator + merge_eps)

    current, result = eval_states, eval_states
    for step in range(section_count):
        result = pl.pallas_call(
            functools.partial(eval_kernel, step, offsets),
            out_shape=jax.ShapeDtypeStruct(eval_states.shape, bf16),
            in_specs=[smem] + [anywhere] * (2 + len(pieces)),
            out_specs=anywhere,
            scratch_shapes=[
                pltpu.VMEM(eval_states.shape, bf16), pltpu.VMEM(eval_states.shape, bf16),
                pltpu.VMEM((2, width, rank), bf16), pltpu.SemaphoreType.DMA((4 + 2 * len(pieces),)),
            ],
            compiler_params=pltpu.CompilerParams(vmem_limit_bytes=vmem_bytes // 4),
            cost_estimate=pl.CostEstimate(
                flops=4 * eval_states.size * rank, bytes_accessed=4 * width * rank, transcendentals=0
            ),
            name="eval_block",
        )(place, current, result, *pieces)
        if step + 1 < section_count:
            current = send(result, "section", [(step, step + 1)])
    return (result[None], label_logprob[None], fisher_log[None])


def solution(mesh):
    placed = (
        P(None, "dp", None),
        P("section", None, None, None),
        P("section", None, None, None),
        P(),
        P(None, None, "dp"),
        P("dp", None),
    )
    return jax.shard_map(
        local,
        mesh=mesh,
        in_specs=placed,
        out_specs=(
            P("section", "dp", None),
            P("section", None, "dp"),
            P("section", None, "dp", None),
        ),
        check_vma=False,
    )
```

profile of v0, /device:TPU:23, one launch (start us, length us, event | category | flops | bytes accessed | tf_op | source)
XLA Modules:
  0.0 338.9 jit_solution(6029527251829751894)
XLA Ops:
  0.7 3.4 %dynamic-slice_bitcast_fusion.1 = bf16[2,4608,128]{2,1,0:T(8,128)(2,1)} fusion(bf16[1,4,4608,128]{3,2,1,0:T(8,128)(2,1)} %param.7, s32[]{:T(128)S(6)} %select_n.155), kind=kLoop, calls=%fused_computation.1 | loop fusion | bytes 4718596 | tf_op jit(solution)/shard_map/dynamic_slice | solution.py:524
  4.8 1.6 dynamic-slice_bitcast_fusion
  7.0 2.1 collective-permute-done.down_other.refs_10_
  9.1 3.5 %collective-permute-done.1.up_other.refs_11_ = bf16[2,4608,128]{2,1,0:T(8,128)(2,1)} collective-permute-done((bf16[2,4608,128]{2,1,0:T(8,128)(2,1)}, bf16[2,4608,128]{2,1,0:T(8,128)(2,1)}, u32[]{:S(2)}, u32[]{:S(2)}) %collective-permute-start.1) | collective-permute-done | bytes 2359328 | tf_op jit(solution)/shard_map/ppermute | solution.py:443
  13.4 1.3 collective-permute-start.2
  15.5 1.3 collective-permute-start.3
  19.4 17.6 %collective-permute-done.2.states = bf16[2,32,4608]{2,1,0:T(8,128)(2,1)S(1)} collective-permute-done((bf16[2,32,4608]{2,1,0:T(8,128)(2,1)}, bf16[2,32,4608]{2,1,0:T(8,128)(2,1)S(1)}, u32[]{:S(2)}, u32[]{:S(2)}) %collective-permute-start.2) | collective-permute-done | bytes 589856 | tf_op jit(solution)/shard_map/ppermute | solution.py:443
  37.8 18.8 %last_stage.5 = (bf16[2,32,4608]{2,1,0:T(8,128)(2,1)}, f32[2,8,32]{2,1,0:T(8,128)}, bf16[2,2,2,32,4608]{4,3,2,1,0:T(8,128)(2,1)}, bf16[2,2,2,32,128]{4,3,2,1,0:T(8,128)(2,1)}) custom-call(s32[4]{0:T(128)} %pad_add_fusion.place, bf16[2,32,4608]{2,1,0:T(8,128)(2,1)} %copy-done.15, s32[5,64,1]{2,1,0:T(8,128)} %reshape.12.labels, bf16[256,4608]{1,0:T(8,128)(2,1)} %label_rows.9, ...), custom_call_target="tpu_custom_call" | custom-call | flops 905969664 | bytes 9437184 | tf_op jit(solution)/shard_map/last_stage/pallas_call | solution.py:600
  56.6 1.3 collective-permute-start.4
  58.0 1.3 collective-permute-start.5
  59.3 1.3 collective-permute-start.6
  62.2 18.8 %last_stage.6 = (bf16[2,32,4608]{2,1,0:T(8,128)(2,1)}, f32[2,8,32]{2,1,0:T(8,128)}, bf16[2,2,2,32,4608]{4,3,2,1,0:T(8,128)(2,1)}, bf16[2,2,2,32,128]{4,3,2,1,0:T(8,128)(2,1)}) custom-call(s32[4]{0:T(128)} %pad_add_fusion.place, bf16[2,32,4608]{2,1,0:T(8,128)(2,1)} %copy-done.12, s32[5,64,1]{2,1,0:T(8,128)} %reshape.12.labels, bf16[256,4608]{1,0:T(8,128)(2,1)} %label_rows.9, ...), custom_call_target="tpu_custom_call" | custom-call | flops 905969664 | bytes 9437184 | tf_op jit(solution)/shard_map/last_stage/pallas_call | solution.py:600
  81.1 1.3 collective-permute-start.7
  82.4 1.3 collective-permute-start.8
  87.1 18.8 %last_stage.7 = (bf16[2,32,4608]{2,1,0:T(8,128)(2,1)}, f32[2,8,32]{2,1,0:T(8,128)}, bf16[2,2,2,32,4608]{4,3,2,1,0:T(8,128)(2,1)}, bf16[2,2,2,32,128]{4,3,2,1,0:T(8,128)(2,1)}) custom-call(s32[4]{0:T(128)} %pad_add_fusion.place, bf16[2,32,4608]{2,1,0:T(8,128)(2,1)} %copy-done.13, s32[5,64,1]{2,1,0:T(8,128)} %reshape.12.labels, bf16[256,4608]{1,0:T(8,128)(2,1)} %label_rows.9, ...), custom_call_target="tpu_custom_call" | custom-call | flops 905969664 | bytes 9437184 | tf_op jit(solution)/shard_map/last_stage/pallas_call | solution.py:600
  106.0 1.3 collective-permute-start.9
  111.2 19.0 %last_stage.8 = (bf16[2,32,4608]{2,1,0:T(8,128)(2,1)}, f32[2,8,32]{2,1,0:T(8,128)}, bf16[2,2,2,32,4608]{4,3,2,1,0:T(8,128)(2,1)}, bf16[2,2,2,32,128]{4,3,2,1,0:T(8,128)(2,1)}) custom-call(s32[4]{0:T(128)} %pad_add_fusion.place, bf16[2,32,4608]{2,1,0:T(8,128)(2,1)} %copy-done.7, s32[5,64,1]{2,1,0:T(8,128)} %reshape.12.labels, bf16[256,4608]{1,0:T(8,128)(2,1)} %label_rows.9, ...), custom_call_target="tpu_custom_call" | custom-call | flops 905969664 | bytes 9437184 | tf_op jit(solution)/shard_map/last_stage/pallas_call | solution.py:600
  130.2 1.3 collective-permute-start.13
  134.1 18.8 %last_stage.9 = (bf16[2,32,4608]{2,1,0:T(8,128)(2,1)}, f32[2,8,32]{2,1,0:T(8,128)}, bf16[2,2,2,32,4608]{4,3,2,1,0:T(8,128)(2,1)}, bf16[2,2,2,32,128]{4,3,2,1,0:T(8,128)(2,1)}) custom-call(s32[4]{0:T(128)} %pad_add_fusion.place, bf16[2,32,4608]{2,1,0:T(8,128)(2,1)} %copy-done.6, s32[5,64,1]{2,1,0:T(8,128)} %reshape.12.labels, bf16[256,4608]{1,0:T(8,128)(2,1)} %label_rows.9, ...), custom_call_target="tpu_custom_call" | custom-call | flops 905969664 | bytes 9437184 | tf_op jit(solution)/shard_map/last_stage/pallas_call | solution.py:600
  153.6 1.3 collective-permute-start.12
  155.6 4.3 %collective-permute-start.11 = (f32[5,32]{1,0:T(8,128)S(1)}, f32[5,32]{1,0:T(8,128)S(1)}, u32[]{:S(2)}, u32[]{:S(2)}) collective-permute-start(f32[5,32]{1,0:T(8,128)S(1)} %bitcast.67), channel_id=1, source_target_pairs={{16,0},{24,16},{17,1},{25,17},{18,2},{26,18},{19,3},{27,19},{20,4}... | collective-permute-start | bytes 1928 | tf_op jit(solution)/shard_map/ppermute | solution.py:443
  162.4 3.9 %collective-permute-done.12.grad = bf16[2,32,4608]{2,1,0:T(8,128)(2,1)S(1)} collective-permute-done((bf16[2,32,4608]{2,1,0:T(8,128)(2,1)}, bf16[2,32,4608]{2,1,0:T(8,128)(2,1)S(1)}, u32[]{:S(2)}, u32[]{:S(2)}) %collective-permute-start.12) | collective-permute-done | bytes 589856 | tf_op jit(solution)/shard_map/ppermute | solution.py:443
  168.1 11.3 %fisher_away.1 = (bf16[2,4608,128]{2,1,0:T(8,128)(2,1)}, bf16[2,4608,128]{2,1,0:T(8,128)(2,1)}) custom-call(s32[4]{0:T(128)} %pad_add_fusion.place, bf16[2,2,2,32,4608]{4,3,2,1,0:T(8,128)(2,1)} %get-tuple-element.140.refs_0_, bf16[2,2,2,32,4608]{4,3,2,1,0:T(8,128)(2,1)} %get-tuple-element.141.refs_1_, ...), custom_call_target="tpu_custom_call" | custom-call | flops 754974720 | bytes 11796480 | tf_op jit(solution)/shard_map/fisher_away/pallas_call | solution.py:671
  179.4 3.1 collective-permute-start.22
  182.5 11.3 %fisher_own.1 = (bf16[2,4608,128]{2,1,0:T(8,128)(2,1)}, bf16[2,4608,128]{2,1,0:T(8,128)(2,1)}) custom-call(s32[4]{0:T(128)} %pad_add_fusion.place, bf16[2,2,2,32,4608]{4,3,2,1,0:T(8,128)(2,1)} %get-tuple-element.140.refs_0_, bf16[2,2,2,32,4608]{4,3,2,1,0:T(8,128)(2,1)} %get-tuple-element.141.refs_1_, ...), custom_call_target="tpu_custom_call" | custom-call | flops 754974720 | bytes 11796480 | tf_op jit(solution)/shard_map/fisher_own/pallas_call | solution.py:671
  194.9 1.4 collective-permute-start.23
  196.3 1.1 add_convert_fusion.13
  197.6 5.5 %collective-permute-done.23 = bf16[2,576,128]{2,1,0:T(8,128)(2,1)S(1)} collective-permute-done((bf16[2,576,128]{2,1,0:T(8,128)(2,1)S(1)}, bf16[2,576,128]{2,1,0:T(8,128)(2,1)S(1)}, u32[]{:S(2)}, u32[]{:S(2)}) %collective-permute-start.23) | collective-permute-done | bytes 294944 | tf_op jit(solution)/shard_map/ppermute | solution.py:443
  203.1 1.1 add_convert_fusion.5
  204.2 1.4 collective-permute-start.24
  205.5 1.2 add_convert_fusion.12
  206.9 4.5 %collective-permute-done.24 = bf16[2,576,128]{2,1,0:T(8,128)(2,1)S(1)} collective-permute-done((bf16[2,576,128]{2,1,0:T(8,128)(2,1)S(1)}, bf16[2,576,128]{2,1,0:T(8,128)(2,1)S(1)}, u32[]{:S(2)}, u32[]{:S(2)}) %collective-permute-start.24) | collective-permute-done | bytes 294944 | tf_op jit(solution)/shard_map/ppermute | solution.py:443
  211.4 1.1 add_convert_fusion.4
  212.5 1.4 collective-permute-start.25
  213.9 1.2 add_convert_fusion.11
  215.3 3.6 %collective-permute-done.25 = bf16[2,576,128]{2,1,0:T(8,128)(2,1)S(1)} collective-permute-done((bf16[2,576,128]{2,1,0:T(8,128)(2,1)S(1)}, bf16[2,576,128]{2,1,0:T(8,128)(2,1)S(1)}, u32[]{:S(2)}, u32[]{:S(2)}) %collective-permute-start.25) | collective-permute-done | bytes 294944 | tf_op jit(solution)/shard_map/ppermute | solution.py:443
  218.9 1.1 add_convert_fusion.3
  219.9 1.4 collective-permute-start.26
  221.3 1.2 add_convert_fusion.10
  222.7 2.9 collective-permute-done.26
  225.6 1.1 add_convert_fusion.2
  226.6 1.4 collective-permute-start.27
  228.4 1.2 add_convert_fusion.9
  229.8 2.6 collective-permute-done.27
  232.4 1.2 add_convert_fusion.1
  233.6 1.4 collective-permute-start.28
  235.6 1.9 add_convert_fusion.8
  237.6 2.6 collective-permute-done.28
  240.3 1.2 add_convert_fusion
  241.4 1.4 collective-permute-start.29
  243.7 2.0 add_convert_fusion.7
  245.8 3.7 %collective-permute-done.29 = bf16[2,576,128]{2,1,0:T(8,128)(2,1)S(1)} collective-permute-done((bf16[2,576,128]{2,1,0:T(8,128)(2,1)S(1)}, bf16[2,576,128]{2,1,0:T(8,128)(2,1)S(1)}, u32[]{:S(2)}, u32[]{:S(2)}) %collective-permute-start.29) | collective-permute-done | bytes 294944 | tf_op jit(solution)/shard_map/ppermute | solution.py:443
  249.5 3.3 collective-permute-done.21
  252.8 2.3 log_bitcast_fusion
  255.2 1.3 collective-permute-start.31
  256.5 6.6 %collective-permute-done.30.refs_1_ = bf16[2,576,128]{2,1,0:T(8,128)(2,1)S(1)} collective-permute-done((bf16[2,576,128]{2,1,0:T(8,128)(2,1)S(1)}, bf16[2,576,128]{2,1,0:T(8,128)(2,1)S(1)}, u32[]{:S(2)}, u32[]{:S(2)}) %collective-permute-start.30) | collective-permute-done | bytes 294944 | tf_op jit(solution)/shard_map/ppermute | solution.py:443
  263.3 1.3 collective-permute-start.33
  264.6 4.7 %collective-permute-done.32.refs_3_ = bf16[2,576,128]{2,1,0:T(8,128)(2,1)S(1)} collective-permute-done((bf16[2,576,128]{2,1,0:T(8,128)(2,1)S(1)}, bf16[2,576,128]{2,1,0:T(8,128)(2,1)S(1)}, u32[]{:S(2)}, u32[]{:S(2)}) %collective-permute-start.32) | collective-permute-done | bytes 294944 | tf_op jit(solution)/shard_map/ppermute | solution.py:443
  269.5 1.3 collective-permute-start.35
  270.8 4.3 %collective-permute-done.34.refs_5_ = bf16[2,576,128]{2,1,0:T(8,128)(2,1)S(1)} collective-permute-done((bf16[2,576,128]{2,1,0:T(8,128)(2,1)S(1)}, bf16[2,576,128]{2,1,0:T(8,128)(2,1)S(1)}, u32[]{:S(2)}, u32[]{:S(2)}) %collective-permute-start.34) | collective-permute-done | bytes 294944 | tf_op jit(solution)/shard_map/ppermute | solution.py:443
  275.2 6.7 %collective-permute-done.36.refs_7_ = bf16[2,576,128]{2,1,0:T(8,128)(2,1)S(1)} collective-permute-done((bf16[2,576,128]{2,1,0:T(8,128)(2,1)S(1)}, bf16[2,576,128]{2,1,0:T(8,128)(2,1)S(1)}, u32[]{:S(2)}, u32[]{:S(2)}) %collective-permute-start.36) | collective-permute-done | bytes 294944 | tf_op jit(solution)/shard_map/ppermute | solution.py:443
  285.9 1.3 collective-permute-start.39
  287.8 44.6 %collective-permute-done.39.states = bf16[32,4608]{1,0:T(8,128)(2,1)S(1)} collective-permute-done((bf16[32,4608]{1,0:T(8,128)(2,1)S(1)}, bf16[32,4608]{1,0:T(8,128)(2,1)S(1)}, u32[]{:S(2)}, u32[]{:S(2)}) %collective-permute-start.39) | collective-permute-done | bytes 294944 | tf_op jit(solution)/shard_map/ppermute | solution.py:443
  332.3 6.4 %eval_block.7 = bf16[32,4608]{1,0:T(8,128)(2,1)} custom-call(s32[4]{0:T(128)S(1)} %copy-done.3, bf16[32,4608]{1,0:T(8,128)(2,1)S(1)} %collective-permute-done.39.states, bf16[32,4608]{1,0:T(8,128)(2,1)S(1)} %eval_block.6.before, bf16[2,576,128]{2,1,0:T(8,128)(2,1)S(1)} %get-tuple-element.164.refs_0_, ...), custom_call_target="tpu_custom_call" | custom-call | flops 75497472 | bytes 2359296 | tf_op jit(solution)/shard_map/eval_block/pallas_call | solution.py:687
  (112 shorter events, 32.4 us)
Async XLA Ops:
  0.6 16.2 %copy-start = (s32[4,5,32]{2,0,1:T(4,128)S(1)}, s32[4,5,32]{2,0,1:T(4,128)}, u32[]{:S(2)}) copy-start(s32[4,5,32]{2,0,1:T(4,128)} %param.10) | copy-start | bytes 7684
  0.7 4.1 %copy-start.4 = (bf16[1,4,4608,128]{3,2,1,0:T(8,128)(2,1)S(1)}, bf16[1,4,4608,128]{3,2,1,0:T(8,128)(2,1)}, u32[]{:S(2)}) copy-start(bf16[1,4,4608,128]{3,2,1,0:T(8,128)(2,1)} %param.8) | copy-start | bytes 14155780
  4.1 5.0 %collective-permute-start = (bf16[2,4608,128]{2,1,0:T(8,128)(2,1)}, bf16[2,4608,128]{2,1,0:T(8,128)(2,1)S(1)}, u32[]{:S(2)}, u32[]{:S(2)}) collective-permute-start(bf16[2,4608,128]{2,1,0:T(8,128)(2,1)} %dynamic-slice_bitcast_fusion.1), channel_id=1, source_target_pairs={{0,8},{8,0},{16,24},{24,16},{1,9},{9,1},{17,25},{25,17},{2,10},{10... | collective-permute-start | bytes 7077896 | tf_op jit(solution)/shard_map/ppermute | solution.py:443
  6.3 6.3 %collective-permute-start.1 = (bf16[2,4608,128]{2,1,0:T(8,128)(2,1)}, bf16[2,4608,128]{2,1,0:T(8,128)(2,1)}, u32[]{:S(2)}, u32[]{:S(2)}) collective-permute-start(bf16[2,4608,128]{2,1,0:T(8,128)(2,1)} %dynamic-slice_bitcast_fusion), channel_id=1, source_target_pairs={{0,8},{8,0},{16,24},{24,16},{1,9},{9,1},{17,25},{25,17},{2,10},{10... | collective-permute-start | bytes 7077896 | tf_op jit(solution)/shard_map/ppermute | solution.py:443
  9.1 3.5 %copy-start.5 = (bf16[2,4608,128]{2,1,0:T(8,128)(2,1)}, bf16[2,4608,128]{2,1,0:T(8,128)(2,1)S(1)}, u32[]{:S(2)}) copy-start(bf16[2,4608,128]{2,1,0:T(8,128)(2,1)S(1)} %collective-permute-done.down_other.refs_10_) | copy-start | bytes 7077892
  13.4 23.5 %collective-permute-start.2 = (bf16[2,32,4608]{2,1,0:T(8,128)(2,1)}, bf16[2,32,4608]{2,1,0:T(8,128)(2,1)S(1)}, u32[]{:S(2)}, u32[]{:S(2)}) collective-permute-start(bf16[2,32,4608]{2,1,0:T(8,128)(2,1)} %get-tuple-element.89), channel_id=1, source_target_pairs={{0,16},{8,24},{1,17},{9,25},{2,18},{10,26},{3,19},{11,27},{4,20},{... | collective-permute-start | bytes 1769480 | tf_op jit(solution)/shard_map/ppermute | solution.py:443
  15.5 45.9 %collective-permute-start.3 = (bf16[2,32,4608]{2,1,0:T(8,128)(2,1)}, bf16[2,32,4608]{2,1,0:T(8,128)(2,1)S(1)}, u32[]{:S(2)}, u32[]{:S(2)}) collective-permute-start(bf16[2,32,4608]{2,1,0:T(8,128)(2,1)} %get-tuple-element.95), channel_id=1, source_target_pairs={{0,16},{8,24},{1,17},{9,25},{2,18},{10,26},{3,19},{11,27},{4,20},{... | collective-permute-start | bytes 1769480 | tf_op jit(solution)/shard_map/ppermute | solution.py:443
  19.3 38.7 %copy-start.19 = (bf16[2,32,4608]{2,1,0:T(8,128)(2,1)S(1)}, bf16[2,32,4608]{2,1,0:T(8,128)(2,1)}, u32[]{:S(2)}) copy-start(bf16[2,32,4608]{2,1,0:T(8,128)(2,1)} %get-tuple-element.106) | copy-start | bytes 1769476
  19.3 40.0 %copy-start.18 = (bf16[2,32,4608]{2,1,0:T(8,128)(2,1)S(1)}, bf16[2,32,4608]{2,1,0:T(8,128)(2,1)}, u32[]{:S(2)}) copy-start(bf16[2,32,4608]{2,1,0:T(8,128)(2,1)} %get-tuple-element.109) | copy-start | bytes 1769476
  37.0 0.8 copy-start.15
  56.6 27.1 %collective-permute-start.4 = (bf16[2,32,4608]{2,1,0:T(8,128)(2,1)}, bf16[2,32,4608]{2,1,0:T(8,128)(2,1)S(1)}, u32[]{:S(2)}, u32[]{:S(2)}) collective-permute-start(bf16[2,32,4608]{2,1,0:T(8,128)(2,1)} %get-tuple-element.98), channel_id=1, source_target_pairs={{16,0},{24,8},{17,1},{25,9},{18,2},{26,10},{19,3},{27,11},{20,4},{... | collective-permute-start | bytes 1769480 | tf_op jit(solution)/shard_map/ppermute | solution.py:443
  58.0 27.5 %collective-permute-start.5 = (bf16[2,32,4608]{2,1,0:T(8,128)(2,1)S(1)}, bf16[2,32,4608]{2,1,0:T(8,128)(2,1)S(1)}, u32[]{:S(2)}, u32[]{:S(2)}) collective-permute-start(bf16[2,32,4608]{2,1,0:T(8,128)(2,1)S(1)} %copy-done.19), channel_id=1, source_target_pairs={{0,16},{8,24},{1,17},{9,25},{2,18},{10,26},{3,19},{11,27},{4,20},{... | collective-permute-start | bytes 1769480 | tf_op jit(solution)/shard_map/ppermute | solution.py:443
  59.3 27.0 %collective-permute-start.6 = (bf16[2,32,4608]{2,1,0:T(8,128)(2,1)S(1)}, bf16[2,32,4608]{2,1,0:T(8,128)(2,1)S(1)}, u32[]{:S(2)}, u32[]{:S(2)}) collective-permute-start(bf16[2,32,4608]{2,1,0:T(8,128)(2,1)S(1)} %copy-done.18), channel_id=1, source_target_pairs={{0,16},{8,24},{1,17},{9,25},{2,18},{10,26},{3,19},{11,27},{4,20},{... | collective-permute-start | bytes 1769480 | tf_op jit(solution)/shard_map/ppermute | solution.py:443
  61.4 21.0 %copy-start.17 = (bf16[2,32,4608]{2,1,0:T(8,128)(2,1)S(1)}, bf16[2,32,4608]{2,1,0:T(8,128)(2,1)}, u32[]{:S(2)}) copy-start(bf16[2,32,4608]{2,1,0:T(8,128)(2,1)} %get-tuple-element.120) | copy-start | bytes 1769476
  61.4 0.8 copy-start.12
  81.1 28.3 %collective-permute-start.7 = (bf16[2,32,4608]{2,1,0:T(8,128)(2,1)}, bf16[2,32,4608]{2,1,0:T(8,128)(2,1)S(1)}, u32[]{:S(2)}, u32[]{:S(2)}) collective-permute-start(bf16[2,32,4608]{2,1,0:T(8,128)(2,1)} %get-tuple-element.112), channel_id=1, source_target_pairs={{16,0},{24,8},{17,1},{25,9},{18,2},{26,10},{19,3},{27,11},{20,4},{... | collective-permute-start | bytes 1769480 | tf_op jit(solution)/shard_map/ppermute | solution.py:443
  82.4 28.8 %collective-permute-start.8 = (bf16[2,32,4608]{2,1,0:T(8,128)(2,1)S(1)}, bf16[2,32,4608]{2,1,0:T(8,128)(2,1)S(1)}, u32[]{:S(2)}, u32[]{:S(2)}) collective-permute-start(bf16[2,32,4608]{2,1,0:T(8,128)(2,1)S(1)} %copy-done.17), channel_id=1, source_target_pairs={{0,16},{8,24},{1,17},{9,25},{2,18},{10,26},{3,19},{11,27},{4,20},{... | collective-permute-start | bytes 1769480 | tf_op jit(solution)/shard_map/ppermute | solution.py:443
  83.7 0.8 copy-start.14
  85.5 20.4 %copy-start.7 = (bf16[2,32,4608]{2,1,0:T(8,128)(2,1)}, bf16[2,32,4608]{2,1,0:T(8,128)(2,1)S(1)}, u32[]{:S(2)}) copy-start(bf16[2,32,4608]{2,1,0:T(8,128)(2,1)S(1)} %collective-permute-done.5.states) | copy-start | bytes 1769476
  86.3 0.8 copy-start.13
  106.0 26.3 %collective-permute-start.9 = (bf16[2,32,4608]{2,1,0:T(8,128)(2,1)}, bf16[2,32,4608]{2,1,0:T(8,128)(2,1)S(1)}, u32[]{:S(2)}, u32[]{:S(2)}) collective-permute-start(bf16[2,32,4608]{2,1,0:T(8,128)(2,1)} %get-tuple-element.124), channel_id=1, source_target_pairs={{16,0},{24,8},{17,1},{25,9},{18,2},{26,10},{19,3},{27,11},{20,4},{... | collective-permute-start | bytes 1769480 | tf_op jit(solution)/shard_map/ppermute | solution.py:443
  109.4 0.8 copy-start.9
  111.2 19.0 %copy-start.6 = (bf16[2,32,4608]{2,1,0:T(8,128)(2,1)}, bf16[2,32,4608]{2,1,0:T(8,128)(2,1)S(1)}, u32[]{:S(2)}) copy-start(bf16[2,32,4608]{2,1,0:T(8,128)(2,1)S(1)} %collective-permute-done.8.states) | copy-start | bytes 1769476
  130.2 29.7 %collective-permute-start.13 = (bf16[2,32,4608]{2,1,0:T(8,128)(2,1)}, bf16[2,32,4608]{2,1,0:T(8,128)(2,1)S(1)}, u32[]{:S(2)}, u32[]{:S(2)}) collective-permute-start(bf16[2,32,4608]{2,1,0:T(8,128)(2,1)} %get-tuple-element.144), channel_id=1, source_target_pairs={{16,0},{24,8},{17,1},{25,9},{18,2},{26,10},{19,3},{27,11},{20,4},{... | collective-permute-start | bytes 1769480 | tf_op jit(solution)/shard_map/ppermute | solution.py:443
  132.3 0.8 copy-start.10
  153.6 12.7 %collective-permute-start.12 = (bf16[2,32,4608]{2,1,0:T(8,128)(2,1)}, bf16[2,32,4608]{2,1,0:T(8,128)(2,1)S(1)}, u32[]{:S(2)}, u32[]{:S(2)}) collective-permute-start(bf16[2,32,4608]{2,1,0:T(8,128)(2,1)} %get-tuple-element.133), channel_id=1, source_target_pairs={{16,0},{24,8},{17,1},{25,9},{18,2},{26,10},{19,3},{27,11},{20,4},{... | collective-permute-start | bytes 1769480 | tf_op jit(solution)/shard_map/ppermute | solution.py:443
  155.0 6.8 %collective-permute-start.10 = (f32[5,32]{1,0:T(8,128)S(1)}, f32[5,32]{1,0:T(8,128)S(1)}, u32[]{:S(2)}, u32[]{:S(2)}) collective-permute-start(f32[5,32]{1,0:T(8,128)S(1)} %bitcast.66), channel_id=1, source_target_pairs={{16,8},{24,24},{17,9},{25,25},{18,10},{26,26},{19,11},{27,27},{20,... | collective-permute-start | bytes 1928 | tf_op jit(solution)/shard_map/ppermute | solution.py:443
  155.6 6.1 %collective-permute-start.11 = (f32[5,32]{1,0:T(8,128)S(1)}, f32[5,32]{1,0:T(8,128)S(1)}, u32[]{:S(2)}, u32[]{:S(2)}) collective-permute-start(f32[5,32]{1,0:T(8,128)S(1)} %bitcast.67), channel_id=1, source_target_pairs={{16,0},{24,16},{17,1},{25,17},{18,2},{26,18},{19,3},{27,19},{20,4}... | collective-permute-start | bytes 1928 | tf_op jit(solution)/shard_map/ppermute | solution.py:443
  160.0 0.8 copy-start.8
  166.3 0.8 copy-start.11
  179.4 14.5 %collective-permute-start.22 = (bf16[2,4608,128]{2,1,0:T(8,128)(2,1)}, bf16[2,4608,128]{2,1,0:T(8,128)(2,1)S(1)}, u32[]{:S(2)}, u32[]{:S(2)}) collective-permute-start(bf16[2,4608,128]{2,1,0:T(8,128)(2,1)} %get-tuple-element.156), channel_id=1, source_target_pairs={{0,8},{8,0},{16,24},{24,16},{1,9},{9,1},{17,25},{25,17},{2,10},{10... | collective-permute-start | bytes 7077896 | tf_op jit(solution)/shard_map/ppermute | solution.py:443
  182.4 13.8 %collective-permute-start.14 = (bf16[2,4608,128]{2,1,0:T(8,128)(2,1)}, bf16[2,4608,128]{2,1,0:T(8,128)(2,1)}, u32[]{:S(2)}, u32[]{:S(2)}) collective-permute-start(bf16[2,4608,128]{2,1,0:T(8,128)(2,1)} %get-tuple-element.152), channel_id=1, source_target_pairs={{0,8},{8,0},{16,24},{24,16},{1,9},{9,1},{17,25},{25,17},{2,10},{10... | collective-permute-start | bytes 7077896 | tf_op jit(solution)/shard_map/ppermute | solution.py:443
  194.9 8.2 %collective-permute-start.23 = (bf16[2,576,128]{2,1,0:T(8,128)(2,1)S(1)}, bf16[2,576,128]{2,1,0:T(8,128)(2,1)S(1)}, u32[]{:S(2)}, u32[]{:S(2)}) collective-permute-start(bf16[2,576,128]{2,1,0:T(8,128)(2,1)S(1)} %add_convert_fusion.6), channel_id=1, source_target_pairs={{2,0},{4,2},{6,4},{7,6},{5,7},{3,5},{1,3},{0,1},{10,8},{12,10},{14... | collective-permute-start | bytes 884744 | tf_op jit(solution)/shard_map/ppermute | solution.py:443
  197.4 8.1 %collective-permute-start.15 = (bf16[2,576,128]{2,1,0:T(8,128)(2,1)S(1)}, bf16[2,576,128]{2,1,0:T(8,128)(2,1)S(1)}, u32[]{:S(2)}, u32[]{:S(2)}) collective-permute-start(bf16[2,576,128]{2,1,0:T(8,128)(2,1)S(1)} %add_convert_fusion.13), channel_id=1, source_target_pairs={{0,2},{2,4},{4,6},{6,7},{7,5},{5,3},{3,1},{1,0},{8,10},{10,12},{12... | collective-permute-start | bytes 884744 | tf_op jit(solution)/shard_map/ppermute | solution.py:443
  204.2 7.3 %collective-permute-start.24 = (bf16[2,576,128]{2,1,0:T(8,128)(2,1)S(1)}, bf16[2,576,128]{2,1,0:T(8,128)(2,1)S(1)}, u32[]{:S(2)}, u32[]{:S(2)}) collective-permute-start(bf16[2,576,128]{2,1,0:T(8,128)(2,1)S(1)} %add_convert_fusion.5), channel_id=1, source_target_pairs={{2,0},{4,2},{6,4},{7,6},{5,7},{3,5},{1,3},{0,1},{10,8},{12,10},{14... | collective-permute-start | bytes 884744 | tf_op jit(solution)/shard_map/ppermute | solution.py:443
  206.7 7.2 %collective-permute-start.16 = (bf16[2,576,128]{2,1,0:T(8,128)(2,1)S(1)}, bf16[2,576,128]{2,1,0:T(8,128)(2,1)S(1)}, u32[]{:S(2)}, u32[]{:S(2)}) collective-permute-start(bf16[2,576,128]{2,1,0:T(8,128)(2,1)S(1)} %add_convert_fusion.12), channel_id=1, source_target_pairs={{0,2},{2,4},{4,6},{6,7},{7,5},{5,3},{3,1},{1,0},{8,10},{10,12},{12... | collective-permute-start | bytes 884744 | tf_op jit(solution)/shard_map/ppermute | solution.py:443
  212.5 6.3 %collective-permute-start.25 = (bf16[2,576,128]{2,1,0:T(8,128)(2,1)S(1)}, bf16[2,576,128]{2,1,0:T(8,128)(2,1)S(1)}, u32[]{:S(2)}, u32[]{:S(2)}) collective-permute-start(bf16[2,576,128]{2,1,0:T(8,128)(2,1)S(1)} %add_convert_fusion.4), channel_id=1, source_target_pairs={{2,0},{4,2},{6,4},{7,6},{5,7},{3,5},{1,3},{0,1},{10,8},{12,10},{14... | collective-permute-start | bytes 884744 | tf_op jit(solution)/shard_map/ppermute | solution.py:443
  215.1 6.3 %collective-permute-start.17 = (bf16[2,576,128]{2,1,0:T(8,128)(2,1)S(1)}, bf16[2,576,128]{2,1,0:T(8,128)(2,1)S(1)}, u32[]{:S(2)}, u32[]{:S(2)}) collective-permute-start(bf16[2,576,128]{2,1,0:T(8,128)(2,1)S(1)} %add_convert_fusion.11), channel_id=1, source_target_pairs={{0,2},{2,4},{4,6},{6,7},{7,5},{5,3},{3,1},{1,0},{8,10},{10,12},{12... | collective-permute-start | bytes 884744 | tf_op jit(solution)/shard_map/ppermute | solution.py:443
  219.9 5.6 %collective-permute-start.26 = (bf16[2,576,128]{2,1,0:T(8,128)(2,1)S(1)}, bf16[2,576,128]{2,1,0:T(8,128)(2,1)S(1)}, u32[]{:S(2)}, u32[]{:S(2)}) collective-permute-start(bf16[2,576,128]{2,1,0:T(8,128)(2,1)S(1)} %add_convert_fusion.3), channel_id=1, source_target_pairs={{2,0},{4,2},{6,4},{7,6},{5,7},{3,5},{1,3},{0,1},{10,8},{12,10},{14... | collective-permute-start | bytes 884744 | tf_op jit(solution)/shard_map/ppermute | solution.py:443
  222.5 5.9 %collective-permute-start.18 = (bf16[2,576,128]{2,1,0:T(8,128)(2,1)S(1)}, bf16[2,576,128]{2,1,0:T(8,128)(2,1)S(1)}, u32[]{:S(2)}, u32[]{:S(2)}) collective-permute-start(bf16[2,576,128]{2,1,0:T(8,128)(2,1)S(1)} %add_convert_fusion.10), channel_id=1, source_target_pairs={{0,2},{2,4},{4,6},{6,7},{7,5},{5,3},{3,1},{1,0},{8,10},{10,12},{12... | collective-permute-start | bytes 884744 | tf_op jit(solution)/shard_map/ppermute | solution.py:443
  226.6 5.8 %collective-permute-start.27 = (bf16[2,576,128]{2,1,0:T(8,128)(2,1)S(1)}, bf16[2,576,128]{2,1,0:T(8,128)(2,1)}, u32[]{:S(2)}, u32[]{:S(2)}) collective-permute-start(bf16[2,576,128]{2,1,0:T(8,128)(2,1)S(1)} %add_convert_fusion.2), channel_id=1, source_target_pairs={{2,0},{4,2},{6,4},{7,6},{5,7},{3,5},{1,3},{0,1},{10,8},{12,10},{14... | collective-permute-start | bytes 884744 | tf_op jit(solution)/shard_map/ppermute | solution.py:443
  229.6 6.0 %collective-permute-start.19 = (bf16[2,576,128]{2,1,0:T(8,128)(2,1)S(1)}, bf16[2,576,128]{2,1,0:T(8,128)(2,1)S(1)}, u32[]{:S(2)}, u32[]{:S(2)}) collective-permute-start(bf16[2,576,128]{2,1,0:T(8,128)(2,1)S(1)} %add_convert_fusion.9), channel_id=1, source_target_pairs={{0,2},{2,4},{4,6},{6,7},{7,5},{5,3},{3,1},{1,0},{8,10},{10,12},{12... | collective-permute-start | bytes 884744 | tf_op jit(solution)/shard_map/ppermute | solution.py:443
  233.6 6.7 %collective-permute-start.28 = (bf16[2,576,128]{2,1,0:T(8,128)(2,1)S(1)}, bf16[2,576,128]{2,1,0:T(8,128)(2,1)}, u32[]{:S(2)}, u32[]{:S(2)}) collective-permute-start(bf16[2,576,128]{2,1,0:T(8,128)(2,1)S(1)} %add_convert_fusion.1), channel_id=1, source_target_pairs={{2,0},{4,2},{6,4},{7,6},{5,7},{3,5},{1,3},{0,1},{10,8},{12,10},{14... | collective-permute-start | bytes 884744 | tf_op jit(solution)/shard_map/ppermute | solution.py:443
  237.5 6.2 %collective-permute-start.20 = (bf16[2,576,128]{2,1,0:T(8,128)(2,1)}, bf16[2,576,128]{2,1,0:T(8,128)(2,1)}, u32[]{:S(2)}, u32[]{:S(2)}) collective-permute-start(bf16[2,576,128]{2,1,0:T(8,128)(2,1)} %add_convert_fusion.8), channel_id=1, source_target_pairs={{0,2},{2,4},{4,6},{6,7},{7,5},{5,3},{3,1},{1,0},{8,10},{10,12},{12... | collective-permute-start | bytes 884744 | tf_op jit(solution)/shard_map/ppermute | solution.py:443
  237.6 44.2 %copy-start.2 = (bf16[32,4608]{1,0:T(8,128)(2,1)S(1)}, bf16[32,4608]{1,0:T(8,128)(2,1)}, u32[]{:S(2)}) copy-start(bf16[32,4608]{1,0:T(8,128)(2,1)} %before.1) | copy-start | bytes 884740
  237.6 44.2 %copy-start.3 = (s32[4]{0:T(128)S(1)}, s32[4]{0:T(128)}, u32[]{:S(2)}) copy-start(s32[4]{0:T(128)} %pad_add_fusion.place) | copy-start | bytes 52
  241.4 8.1 %collective-permute-start.29 = (bf16[2,576,128]{2,1,0:T(8,128)(2,1)S(1)}, bf16[2,576,128]{2,1,0:T(8,128)(2,1)S(1)}, u32[]{:S(2)}, u32[]{:S(2)}) collective-permute-start(bf16[2,576,128]{2,1,0:T(8,128)(2,1)S(1)} %add_convert_fusion), channel_id=1, source_target_pairs={{2,0},{4,2},{6,4},{7,6},{5,7},{3,5},{1,3},{0,1},{10,8},{12,10},{14... | collective-permute-start | bytes 884744 | tf_op jit(solution)/shard_map/ppermute | solution.py:443
  245.6 7.2 %collective-permute-start.21 = (bf16[2,576,128]{2,1,0:T(8,128)(2,1)}, bf16[2,576,128]{2,1,0:T(8,128)(2,1)S(1)}, u32[]{:S(2)}, u32[]{:S(2)}) collective-permute-start(bf16[2,576,128]{2,1,0:T(8,128)(2,1)} %add_convert_fusion.7), channel_id=1, source_target_pairs={{0,2},{2,4},{4,6},{6,7},{7,5},{5,3},{3,1},{1,0},{8,10},{10,12},{12... | collective-permute-start | bytes 884744 | tf_op jit(solution)/shard_map/ppermute | solution.py:443
  255.1 8.1 %collective-permute-start.30 = (bf16[2,576,128]{2,1,0:T(8,128)(2,1)S(1)}, bf16[2,576,128]{2,1,0:T(8,128)(2,1)S(1)}, u32[]{:S(2)}, u32[]{:S(2)}) collective-permute-start(bf16[2,576,128]{2,1,0:T(8,128)(2,1)S(1)} %get-tuple-element.164.refs_0_), channel_id=1, source_target_pairs={{0,2},{2,4},{4,6},{6,7},{7,5},{5,3},{3,1},{1,0},{8,10},{10,12},{12... | collective-permute-start | bytes 884744 | tf_op jit(solution)/shard_map/ppermute | solution.py:443
  255.2 8.1 %collective-permute-start.31 = (bf16[2,576,128]{2,1,0:T(8,128)(2,1)S(1)}, bf16[2,576,128]{2,1,0:T(8,128)(2,1)S(1)}, u32[]{:S(2)}, u32[]{:S(2)}) collective-permute-start(bf16[2,576,128]{2,1,0:T(8,128)(2,1)S(1)} %get-tuple-element.164.refs_0_), channel_id=1, source_target_pairs={{2,0},{4,2},{6,4},{7,6},{5,7},{3,5},{1,3},{0,1},{10,8},{12,10},{14... | collective-permute-start | bytes 884744 | tf_op jit(solution)/shard_map/ppermute | solution.py:443
  263.1 6.2 %collective-permute-start.32 = (bf16[2,576,128]{2,1,0:T(8,128)(2,1)S(1)}, bf16[2,576,128]{2,1,0:T(8,128)(2,1)S(1)}, u32[]{:S(2)}, u32[]{:S(2)}) collective-permute-start(bf16[2,576,128]{2,1,0:T(8,128)(2,1)S(1)} %collective-permute-done.30.refs_1_), channel_id=1, source_target_pairs={{0,2},{2,4},{4,6},{6,7},{7,5},{5,3},{3,1},{1,0},{8,10},{10,12},{12... | collective-permute-start | bytes 884744 | tf_op jit(solution)/shard_map/ppermute | solution.py:443
  263.3 6.2 %collective-permute-start.33 = (bf16[2,576,128]{2,1,0:T(8,128)(2,1)S(1)}, bf16[2,576,128]{2,1,0:T(8,128)(2,1)S(1)}, u32[]{:S(2)}, u32[]{:S(2)}) collective-permute-start(bf16[2,576,128]{2,1,0:T(8,128)(2,1)S(1)} %collective-permute-done.31.refs_2_), channel_id=1, source_target_pairs={{2,0},{4,2},{6,4},{7,6},{5,7},{3,5},{1,3},{0,1},{10,8},{12,10},{14... | collective-permute-start | bytes 884744 | tf_op jit(solution)/shard_map/ppermute | solution.py:443
  269.3 5.7 %collective-permute-start.34 = (bf16[2,576,128]{2,1,0:T(8,128)(2,1)S(1)}, bf16[2,576,128]{2,1,0:T(8,128)(2,1)S(1)}, u32[]{:S(2)}, u32[]{:S(2)}) collective-permute-start(bf16[2,576,128]{2,1,0:T(8,128)(2,1)S(1)} %collective-permute-done.32.refs_3_), channel_id=1, source_target_pairs={{0,2},{2,4},{4,6},{6,7},{7,5},{5,3},{3,1},{1,0},{8,10},{10,12},{12... | collective-permute-start | bytes 884744 | tf_op jit(solution)/shard_map/ppermute | solution.py:443
  269.5 5.7 %collective-permute-start.35 = (bf16[2,576,128]{2,1,0:T(8,128)(2,1)S(1)}, bf16[2,576,128]{2,1,0:T(8,128)(2,1)S(1)}, u32[]{:S(2)}, u32[]{:S(2)}) collective-permute-start(bf16[2,576,128]{2,1,0:T(8,128)(2,1)S(1)} %collective-permute-done.33.refs_4_), channel_id=1, source_target_pairs={{2,0},{4,2},{6,4},{7,6},{5,7},{3,5},{1,3},{0,1},{10,8},{12,10},{14... | collective-permute-start | bytes 884744 | tf_op jit(solution)/shard_map/ppermute | solution.py:443
  275.0 6.8 %collective-permute-start.36 = (bf16[2,576,128]{2,1,0:T(8,128)(2,1)S(1)}, bf16[2,576,128]{2,1,0:T(8,128)(2,1)S(1)}, u32[]{:S(2)}, u32[]{:S(2)}) collective-permute-start(bf16[2,576,128]{2,1,0:T(8,128)(2,1)S(1)} %collective-permute-done.34.refs_5_), channel_id=1, source_target_pairs={{0,2},{2,4},{4,6},{6,7},{7,5},{5,3},{3,1},{1,0},{8,10},{10,12},{12... | collective-permute-start | bytes 884744 | tf_op jit(solution)/shard_map/ppermute | solution.py:443
  282.7 0.7 collective-permute-start.37
  284.3 2.9 copy-start.16
  284.3 0.7 collective-permute-start.38
  285.0 53.7 %copy-start.1 = (s32[4,5,32]{2,0,1:T(4,128)S(1)}, s32[4,5,32]{2,0,1:T(4,128)}, u32[]{:S(2)}) copy-start(s32[4,5,32]{2,0,1:T(4,128)} %param.10) | copy-start | bytes 7684
  285.9 46.5 %collective-permute-start.39 = (bf16[32,4608]{1,0:T(8,128)(2,1)S(1)}, bf16[32,4608]{1,0:T(8,128)(2,1)S(1)}, u32[]{:S(2)}, u32[]{:S(2)}) collective-permute-start(bf16[32,4608]{1,0:T(8,128)(2,1)S(1)} %eval_block.6.before), channel_id=1, source_target_pairs={{16,24},{17,25},{18,26},{19,27},{20,28},{21,29},{22,30},{23,31}} | collective-permute-start | bytes 884744 | tf_op jit(solution)/shard_map/ppermute | solution.py:443
where the time goes:
time: 340 us; the launch traced here: 339 us
  Pallas kernels  135 us (40%)
  waiting for transfers between devices  125 us (37%)
  starting transfers between devices  40 us (12%)
  other arithmetic  20.9 us (6%)
  local copies, waits for them, and re-layouts  16.5 us (5%)
    ppermute x40, waiting for transfers between devices, send(): return lax.ppermute(block, axis, route)  125 us
    pallas_call x5, Pallas kernels, last_stage(): call(token, crossing[turn], label_columns, label_rows, *weights)  94.4 us
    ppermute x40, starting transfers between devices, send(): return lax.ppermute(block, axis, route)  40 us
    pallas_call x2, Pallas kernels, fisher(): call(order, *[squares[turn][0] for turn in range(turns)], *[squares[turn]...  22.6 us
    convert_element_type x12, other arithmetic, ring_scatter(): moving = sums if last else [value.astype(bf16) for value in sums]  15.2 us
    pallas_call x4, Pallas kernels, local(): pl.pallas_call(functools.partial(eval_kernel, step, offsets), out_shape=j...  8.94 us
    unnamed x47, local copies, waits for them, and re-layouts  7.18 us
  transfers between devices with their start and end apart: 40, of which 21 were waited for; matrix products, arithmetic and copies ran while one was open for 7% of the time, Pallas kernels for 33%

commit v1 on v0

v1 whole, which is shorter than its diff:
```python
import functools

import jax
import jax.numpy as jnp
from jax import lax
from jax.experimental import pallas as pl
from jax.experimental.pallas import tpu as pltpu
from jax.sharding import PartitionSpec as P

norm_eps = 1e-06
merge_eps = 1e-06
soft_cap = 30.0
gelu_coef = 0.7978845608028654
vmem_bytes = 56 * 1024 * 1024
bf16 = jnp.bfloat16
f32 = jnp.float32


def nt_dot(lhs, rhs):
    return lax.dot_general(lhs, rhs, (((1,), (1,)), ((), ())), preferred_element_type=f32)


def nn_dot(lhs, rhs):
    return lax.dot_general(lhs, rhs, (((1,), (0,)), ((), ())), preferred_element_type=f32)


def tn_dot(lhs, rhs):
    return lax.dot_general(lhs, rhs, (((0,), (0,)), ((), ())), preferred_element_type=f32)


def gelu_value(hidden):
    inner = gelu_coef * (hidden + 0.044715 * hidden * hidden * hidden)
    return 0.5 * hidden * (1.0 + jnp.tanh(inner))


def gelu_slope(hidden):
    inner = gelu_coef * (hidden + 0.044715 * hidden * hidden * hidden)
    tanh_value = jnp.tanh(inner)
    return 0.5 * (1.0 + tanh_value) + 0.5 * hidden * (1.0 - tanh_value * tanh_value) * gelu_coef * (
        1.0 + 3.0 * 0.044715 * hidden * hidden
    )


def tiled(width):
    count = max(n for n in (1, 2, 3) if width % (128 * n) == 0)
    size = width // count

    def loop(body, start=None):
        def step(index, carry):
            return body(pl.ds(pl.multiple_of(index * size, 128), size), carry)

        return lax.fori_loop(0, count, step, start)

    return loop


def row_scale(total, width):
    return lax.rsqrt(total / width + norm_eps)


def row_sum(values):
    return jnp.sum(values, axis=-1, keepdims=True)


def square(values):
    wide = values.astype(f32)
    return (wide * wide).astype(bf16)


def zeros(*shape):
    return jnp.zeros(shape, f32)


def label_head(states, labels, label_rows, grads):
    rows, width = states.shape
    loop, words = tiled(width), label_rows.shape[0]

    def score(cols, carry):
        total, logits = carry
        part = states[:, cols]
        wide = part.astype(f32)
        return total + row_sum(wide * wide), logits + nt_dot(part, label_rows[:, cols])

    total, logits = loop(score, (zeros(rows, 1), zeros(rows, words)))
    scale = row_scale(total, width)
    logits = logits * scale
    bent = jnp.tanh(logits / soft_cap)
    capped = soft_cap * bent
    logprob = capped - jnp.log(row_sum(jnp.exp(capped)))
    one_hot = (labels == lax.broadcasted_iota(jnp.int32, logprob.shape, 1)).astype(f32)
    slope = ((jnp.exp(logprob) - one_hot) * (1.0 - bent * bent)).astype(bf16)
    pull = scale * row_sum(slope.astype(f32) * logits) / width

    def finish(cols, carry):
        wide = states[:, cols].astype(f32)
        grads[:, cols] = (scale * nn_dot(slope, label_rows[:, cols]) - scale * (wide * pull)).astype(bf16)
        return carry

    loop(finish, 0)
    return row_sum(logprob * one_hot)


class Copies:
    def __init__(self, sems):
        self.sems, self.used = sems, 0

    def start(self, source, target):
        copy = pltpu.make_async_copy(source, target, self.sems.at[self.used])
        self.used += 1
        copy.start()
        return copy


class StageWeights:
    def __init__(self, member, task, own, other, held, sems):
        self.member, self.task, self.own, self.other = member, task, own, other
        self.held, self.sems = held, sems

    def copy(self, kind, layer):
        return pltpu.make_async_copy(
            self.other[kind].at[self.task], self.held[kind].at[layer], self.sems.at[kind, layer]
        )

    def start(self, order):
        tasks = self.other[0].shape[0]
        for kind, layer in order:
            @pl.when(self.member == layer)
            def _():
                pltpu.make_async_copy(
                    self.own[kind].at[layer * tasks + self.task], self.held[kind].at[layer], self.sems.at[kind, layer]
                ).start()

            @pl.when(self.member != layer)
            def _():
                self.copy(kind, layer).start()

    def wait(self, kind, layer):
        self.copy(kind, layer).wait()


def forward_loop(levels, hidden, scales, weights, held_down, held_up, done):
    (rows, width), rank = levels.shape[1:], held_down.shape[-1]
    loop = tiled(width)

    @pl.loop(0, 2)
    def _(layer):
        weights.wait(0, layer)

        def down(cols, carry):
            total, pre = carry
            part = levels[layer, :, cols]
            wide = part.astype(f32)
            return total + row_sum(wide * wide), pre + nn_dot(part, held_down[layer, cols])

        total, pre = loop(down, (zeros(rows, 1), zeros(rows, rank)))
        scale = row_scale(total, width)
        pre = pre * scale
        scales[layer] = jnp.broadcast_to(scale, (rows, 128))
        hidden[layer] = pre
        active = gelu_value(pre).astype(bf16)
        weights.wait(1, layer)

        def up(cols, carry):
            update = nt_dot(active, held_up[layer, cols])
            levels[layer + 1, :, cols] = (levels[layer, :, cols].astype(f32) + update).astype(bf16)
            return carry

        loop(up, 0)
        done(layer)


class Squares:
    def __init__(self, wide, narrow, wide_out, narrow_out, sems):
        self.wide, self.narrow = wide, narrow
        self.pairs = ((wide, wide_out), (narrow, narrow_out))
        self.sems = sems

    def copy(self, which, layer, kind):
        source, target = self.pairs[which]
        return pltpu.make_async_copy(
            source.at[layer, kind], target.at[layer, kind], self.sems.at[which, layer, kind]
        )

    def start(self, layer):
        for kind in range(2):
            for which in range(2):
                self.copy(which, layer, kind).start()

    def wait(self):
        for layer in range(2):
            for kind in range(2):
                for which in range(2):
                    self.copy(which, layer, kind).wait()


def backward_step(layer, levels, grads, hidden, scales, weights, held_down, held_up, squares, pass_on):
    (rows, width), rank = levels.shape[1:], held_down.shape[-1]
    loop = tiled(width)
    if weights is not None:
        weights.wait(1, layer)
    scale = scales[layer][:, :1]
    pre = hidden[layer]

    def up(cols, total):
        grad = grads[layer + 1, :, cols]
        total = total + nn_dot(grad, held_up[layer, cols])
        norm = (levels[layer, :, cols].astype(f32) * scale).astype(bf16)
        squares.wide[layer, 0, :, cols] = square(norm)
        squares.wide[layer, 1, :, cols] = square(grad)
        return total

    grad_hidden = (loop(up, zeros(rows, rank)) * gelu_slope(pre)).astype(bf16)
    squares.narrow[layer, 0] = square(grad_hidden)
    squares.narrow[layer, 1] = square(gelu_value(pre).astype(bf16))
    squares.start(layer)
    if not pass_on:
        return
    if weights is not None:
        weights.wait(0, layer)
    pull = scale * row_sum(grad_hidden.astype(f32) * pre) / width

    def finish(cols, carry):
        grad_norm = nt_dot(grad_hidden, held_down[layer, cols])
        wide = levels[layer, :, cols].astype(f32)
        grads[layer, :, cols] = (
            grads[layer + 1, :, cols].astype(f32) + scale * (grad_norm - wide * pull)
        ).astype(bf16)
        return carry

    loop(finish, 0)


def first_forward_kernel(task, half, place, entry, down, up, down_other, up_other, out, middle, hidden, scales_out,
                         levels, pre, scales, sems, held_down, held_up, weight_sems):
    @pl.when(place[0] == 0)
    def _():
        rows = levels.shape[1]
        copies = Copies(sems)
        load = copies.start(entry.at[pl.ds(half * rows, rows)], levels.at[0])
        weights = StageWeights(
            place[1], task, (down, up), (down_other, up_other), (held_down, held_up), weight_sems
        )
        weights.start([(0, 0), (1, 0), (0, 1), (1, 1)])
        load.wait()

        def leave(layer):
            return pltpu.make_async_copy(levels.at[layer + 1], (middle, out)[layer], sems.at[1 + layer])

        def done(layer):
            for fixed in range(2):
                @pl.when(layer == fixed)
                def _():
                    leave(fixed).start()

        forward_loop(levels, pre, scales, weights, held_down, held_up, done)
        last = [
            pltpu.make_async_copy(pre, hidden, sems.at[0]),
            pltpu.make_async_copy(scales, scales_out, sems.at[3]),
        ]
        for copy in last:
            copy.start()
        for copy in [leave(0), leave(1)] + last:
            copy.wait()


def first_backward_kernel(task, half, place, grad, entry, middle, hidden, scales_in, wide_in, narrow_in,
                          down, up, down_other, up_other, wide_out, narrow_out,
                          grads, levels, pre, scales, wide, narrow, square_sems, sems,
                          held_down, held_up, weight_sems):
    del wide_in, narrow_in

    @pl.when(place[0] == 0)
    def _():
        rows = levels.shape[1]
        copies = Copies(sems)
        loads = [
            copies.start(source, target)
            for source, target in (
                (grad, grads.at[2]), (hidden, pre), (scales_in, scales), (middle, levels.at[1]),
                (entry.at[pl.ds(half * rows, rows)], levels.at[0]),
            )
        ]
        weights = StageWeights(
            place[1], task, (down, up), (down_other, up_other), (held_down, held_up), weight_sems
        )
        weights.start([(1, 1), (0, 1), (1, 0)])
        squares = Squares(wide, narrow, wide_out, narrow_out, square_sems)
        for load in loads:
            load.wait()
        for layer in (1, 0):
            backward_step(layer, levels, grads, pre, scales, weights, held_down, held_up, squares, layer == 1)
        squares.wait()


def last_stage_kernel(task, half, place, states, labels, label_rows, down, up, down_other, up_other,
                      grad_out, picked, wide_out, narrow_out,
                      levels, words, marks, chosen, pre, scales, grads, wide, narrow, square_sems, sems,
                      held_down, held_up, weight_sems):
    @pl.when(place[0] == 1)
    def _():
        rows = levels.shape[1]
        copies = Copies(sems)
        loaded = copies.start(states, levels.at[0])
        weights = StageWeights(
            place[1], task, (down, up), (down_other, up_other), (held_down, held_up), weight_sems
        )
        weights.start([(0, 0), (1, 0), (0, 1), (1, 1)])
        later = [copies.start(label_rows, words), copies.start(labels.at[task, half], marks)]
        loaded.wait()
        forward_loop(levels, pre, scales, weights, held_down, held_up, lambda layer: None)
        for copy in later:
            copy.wait()
        values = label_head(levels.at[2], marks[...], words, grads.at[2])
        lanes = 128 * ((rows + 127) // 128)
        spread = jnp.broadcast_to(values, (rows, 128))
        if lanes > rows:
            spread = jnp.concatenate([spread, zeros(lanes - rows, 128)], axis=0)
        chosen[...] = spread.T[0:8]
        out_copy = copies.start(chosen, picked)
        squares = Squares(wide, narrow, wide_out, narrow_out, square_sems)

        @pl.loop(0, 2)
        def _(index):
            backward_step(1 - index, levels, grads, pre, scales, None, held_down, held_up, squares, True)

        last = copies.start(grads.at[0], grad_out)
        squares.wait()
        out_copy.wait()
        last.wait()


def eval_kernel(step, offsets, place, states, before, *refs):
    *pieces, out, base, top, held, sems = refs
    copies = Copies(sems)
    rows = pieces[0].shape[1]

    @pl.when(place[2] == step)
    def _():
        loads = [[copies.start(states, base)], [], []]
        for kind in range(2):
            for index, piece in enumerate(pieces):
                block = block_at(place[3], offsets[index], len(pieces))
                spot = pl.ds(pl.multiple_of(block * rows, 16), rows)
                loads[1 + kind].append(copies.start(piece.at[kind], held.at[kind, spot]))
        for load in loads[0]:
            load.wait()
        total_rows, width = base.shape
        loop = tiled(width)

        def squared(cols, total):
            wide = base[:, cols].astype(f32)
            return total + row_sum(wide * wide)

        scale = row_scale(loop(squared, zeros(total_rows, 1)), width)
        for load in loads[1]:
            load.wait()
        pre = loop(lambda cols, sums: sums + nn_dot(base[:, cols], held[0, cols]), zeros(total_rows, held.shape[-1]))
        active = gelu_value(pre * scale).astype(bf16)
        for load in loads[2]:
            load.wait()

        def up(cols, carry):
            top[:, cols] = (base[:, cols].astype(f32) + nt_dot(active, held[1, cols])).astype(bf16)
            return carry

        loop(up, 0)
        copies.start(top, out).wait()

    @pl.when(place[2] != step)
    def _():
        copies.start(before, base).wait()
        copies.start(base, out).wait()


def fisher_kernel(halves, first, place, *refs):
    del place
    wides, narrows, weights = refs[:halves], refs[halves:2 * halves], refs[2 * halves:2 * halves + 2]
    before, outs = ((), refs[2 * halves + 2:]) if first else (refs[2 * halves + 2:-2], refs[-2:])
    for kind in range(2):
        left = jnp.concatenate([ref[0, kind] for ref in wides], axis=0)
        right = jnp.concatenate([ref[0, kind] for ref in narrows], axis=0)
        term = tn_dot(left, right)
        values = (term * weights[kind][0].astype(f32), term)
        for index, out in enumerate(outs):
            value = values[index] if first else values[index] + before[index][kind]
            out[kind] = value.astype(out.dtype)


def block_size(width):
    return max(size for size in range(128, 513, 128) if width % size == 0)


smem = pl.BlockSpec(memory_space=pltpu.SMEM)
anywhere = pl.BlockSpec(memory_space=pl.ANY)
hbm = pl.BlockSpec(memory_space=pltpu.HBM)


def send(block, axis, route):
    return lax.ppermute(block, axis, route)


def walk(spot, count):
    if count % 2:
        return spot
    return jnp.where(spot < count // 2, 2 * spot, 2 * (count - 1 - spot) + 1)


def spot_of(device, count):
    if count % 2:
        return device
    return jnp.where(lax.rem(device, 2) == 0, lax.div(device, 2), count - 1 - lax.div(device, 2))


def block_at(spot, offset, count):
    return walk(lax.rem(spot + offset + 2 * count, count), count)


def ring_routes(axis):
    count = lax.axis_size(axis)
    order = list(range(count)) if count % 2 else list(range(0, count, 2)) + list(range(count - 1, 0, -2))
    ahead = [(order[i], order[(i + 1) % count]) for i in range(count)]
    return count, ahead, [(j, i) for i, j in ahead]


def ring_scatter(own, other, spot, axis):
    count, ahead, back = ring_routes(axis)
    rows = own[0].shape[1] // count

    def part(index, offset):
        start = block_at(spot, offset, count) * rows
        return sum(
            lax.dynamic_slice_in_dim(array[index], start, rows, 1).astype(f32) for array in (own, other)
        )

    moving = [part(0, -1).astype(bf16), part(1, 1).astype(bf16)]
    for step in range(count - 1):
        last = step == count - 2
        landed = [send(moving[0], axis, ahead), send(moving[1], axis, back)]
        sums = [landed[0].astype(f32) + part(0, -2 - step), landed[1].astype(f32) + part(1, 2 + step)]
        moving = sums if last else [value.astype(bf16) for value in sums]
    return moving


def ring_gather(own, axis):
    count, ahead, back = ring_routes(axis)
    pieces, offsets = [own], [0]
    down = up = own
    for step in range(1, count // 2 + 1):
        down = send(down, axis, ahead)
        pieces.append(down)
        offsets.append(-step)
        if len(pieces) < count:
            up = send(up, axis, back)
            pieces.append(up)
            offsets.append(step)
    return pieces, offsets


def after(value, done):
    return lax.optimization_barrier((value, done))[0]


def local(entry_states, down_proj, up_proj, label_rows, sampled_labels, eval_states):
    section_count = lax.axis_size("section")
    section = lax.axis_index("section")
    stage, member = section // 2, section % 2
    w_down, w_up = down_proj[0], up_proj[0]
    all_tasks, width, rank = w_down.shape
    tasks = all_tasks // 2
    micro, rows, _ = entry_states.shape
    label_count = label_rows.shape[0]
    halves = 2
    chunks, part = tasks * halves, micro * rows // halves
    spot = spot_of(lax.axis_index("dp"), lax.axis_size("dp"))
    place = jnp.stack([stage, member, section, spot]).astype(jnp.int32)
    sections = range(section_count)
    swap = [(i, i ^ 1) for i in sections]
    upward = [(i, i + 2) for i in sections if i + 2 < section_count]
    downward = [(i, i - 2) for i in sections if i - 2 >= 0]

    away = (1 - member) * tasks
    down_other = send(lax.dynamic_slice_in_dim(w_down, away, tasks, 0), "section", swap)
    up_other = send(lax.dynamic_slice_in_dim(w_up, away, tasks, 0), "section", swap)
    weights = (w_down, w_up, down_other, up_other)

    held = [
        pltpu.VMEM((2, width, rank), bf16),
        pltpu.VMEM((2, width, rank), bf16),
        pltpu.SemaphoreType.DMA((2, 2)),
    ]
    params = pltpu.CompilerParams(vmem_limit_bytes=vmem_bytes)
    state_shape, hidden_shape = (part, width), (2, part, rank)
    wide_shape, narrow_shape = (2, 2, part, width), (2, 2, part, rank)
    state_type = jax.ShapeDtypeStruct(state_shape, bf16)
    square_types = (jax.ShapeDtypeStruct(wide_shape, bf16), jax.ShapeDtypeStruct(narrow_shape, bf16))
    square_scratch = [
        pltpu.VMEM(wide_shape, bf16),
        pltpu.VMEM(narrow_shape, bf16),
        pltpu.SemaphoreType.DMA((2, 2, 2)),
    ]
    layer_flops = 4 * part * width * rank
    weight_bytes = 8 * width * rank

    def stage_call(kernel, turn, name, operands, outputs, scratch, flops, hbm_in=(), hbm_out=(), **more):
        return pl.pallas_call(
            functools.partial(kernel, turn // halves, turn % halves),
            out_shape=outputs,
            in_specs=[smem] + [hbm if index in hbm_in else anywhere for index in range(1, operands + 1)],
            out_specs=tuple(hbm if index in hbm_out else anywhere for index in range(len(outputs))),
            scratch_shapes=scratch + held,
            compiler_params=params,
            cost_estimate=pl.CostEstimate(flops=flops, bytes_accessed=weight_bytes, transcendentals=0),
            name=name,
            **more,
        )

    own_labels = lax.dynamic_slice_in_dim(sampled_labels, member * tasks, tasks, 0)
    label_columns = own_labels.reshape(tasks, halves, part, 1)
    entry = entry_states.reshape(micro * rows, width)
    saved, crossing, returned, picked = {}, {}, {}, {}
    squares = {}
    token = place

    levels, pre = pltpu.VMEM((3,) + state_shape, bf16), pltpu.VMEM(hidden_shape, f32)
    scale_shape = (2, part, 128)
    lanes = 128 * ((part + 127) // 128)
    scales, scale_type = pltpu.VMEM(scale_shape, f32), jax.ShapeDtypeStruct(scale_shape, f32)

    def first_forward(turn):
        nonlocal token
        call = stage_call(
            first_forward_kernel, turn, "first_forward", 5,
            (state_type, state_type, jax.ShapeDtypeStruct(hidden_shape, f32), scale_type),
            [levels, pre, scales, pltpu.SemaphoreType.DMA((4,))],
            2 * layer_flops, hbm_in=(1, 2, 3, 4, 5), hbm_out=(1, 2, 3),
        )
        out, middle, hidden, scale = call(token, entry, *weights)
        saved[turn] = (entry, middle, hidden, scale)
        crossing[turn] = out
        token = after(place, scale)

    def cross(turn):
        nonlocal token
        out = lax.optimization_barrier((crossing[turn], token))[0]
        crossing[turn] = send(out, "section", upward)

    def last_stage(turn):
        nonlocal token
        call = stage_call(
            last_stage_kernel, turn, "last_stage", 7,
            (state_type, jax.ShapeDtypeStruct((8, lanes), f32)) + square_types,
            [
                levels, pltpu.VMEM(label_rows.shape, bf16),
                pltpu.VMEM((part, 1), jnp.int32), pltpu.VMEM((8, lanes), f32),
                pre, scales, levels,
            ] + square_scratch + [pltpu.SemaphoreType.DMA((5,))],
            4 * layer_flops + 4 * part * width * label_count,
            hbm_in=(3, 4, 5, 6, 7), hbm_out=(2, 3),
        )
        grad, picked[turn], *squares[turn] = call(
            token, crossing[turn], label_columns, label_rows, *weights
        )
        returned[turn] = send(grad, "section", downward)
        token = after(place, picked[turn])

    def first_backward(turn):
        nonlocal token
        call = stage_call(
            first_backward_kernel, turn, "first_backward", 11, square_types,
            [levels, levels, pre, scales] + square_scratch + [pltpu.SemaphoreType.DMA((5,))],
            2 * layer_flops,
            hbm_in=range(2, 12), hbm_out=(0, 1),
            input_output_aliases={6: 0, 7: 1},
        )
        squares[turn] = call(token, returned[turn], *saved[turn], *squares[turn], *weights)
        token = after(place, squares[turn][1])

    block = block_size(width)

    def fisher(task, away, sums=()):
        first = not sums

        def layer_of(s):
            return 1 - s[1] if away else s[1]

        pairs = [squares[task * halves + half] for half in range(halves)]
        sum_spec = pl.BlockSpec((2, block, rank), lambda i, s: (0, i, 0))
        call = pl.pallas_call(
            functools.partial(fisher_kernel, halves, first),
            out_shape=(jax.ShapeDtypeStruct((2, width, rank), bf16 if task == tasks - 1 else f32),) * 2,
            grid_spec=pltpu.PrefetchScalarGridSpec(
                num_scalar_prefetch=1,
                grid=(width // block,),
                in_specs=[pl.BlockSpec((1, 2, part, block), lambda i, s: (layer_of(s), 0, 0, i))] * halves
                + [pl.BlockSpec((1, 2, part, rank), lambda i, s: (layer_of(s), 0, 0, 0))] * halves
                + [pl.BlockSpec((1, block, rank), lambda i, s: (task if away else s[1] * tasks + task, i, 0))] * 2
                + [sum_spec] * len(sums),
                out_specs=(sum_spec,) * 2,
            ),
            compiler_params=params,
            cost_estimate=pl.CostEstimate(
                flops=4 * halves * part * width * rank,
                bytes_accessed=8 * halves * part * width,
                transcendentals=0,
            ),
            name="fisher_away" if away else "fisher_own",
        )
        return call(
            token, *[wide for wide, _ in pairs], *[narrow for _, narrow in pairs],
            *(weights[2:] if away else weights[:2]), *sums,
        )

    sums = {True: (), False: ()}

    def add_task(task):
        nonlocal token
        for away in (True, False):
            sums[away] = fisher(task, away, sums[away])
            token = after(place, sums[away][0])

    for turn in range(chunks):
        first_forward(turn)
        cross(turn)
    for turn in range(chunks):
        if turn >= 2:
            first_backward(turn - 2)
        last_stage(turn)
    first_backward(chunks - 2)
    for task in range(tasks - 1):
        add_task(task)
    values = jnp.stack([picked[turn][0, :part] for turn in range(chunks)]).reshape(tasks, micro, rows)
    values = after(values, token)
    label_logprob = jnp.zeros((micro, rows), f32)
    for index in range(tasks):
        route = [(section_count - 2 + m, m * tasks + index) for m in range(2)]
        landed = send(values[index], "section", route)
        label_logprob = jnp.where(section % tasks == index, landed, label_logprob)
    token = after(token, label_logprob)
    first_backward(chunks - 1)
    away_sums = fisher(tasks - 1, True, sums[True])
    other_sums = [send(value, "section", swap) for value in away_sums]
    token = after(place, away_sums[0])
    sums = fisher(tasks - 1, False, sums[False])
    shares = ring_scatter(sums, other_sums, spot, "dp")
    numerator, denominator = shares
    merged_part = (numerator / (denominator + merge_eps)).astype(bf16)
    pieces, offsets = ring_gather(merged_part, "dp")
    fisher_log = jnp.log(denominator + merge_eps)

    current, result = eval_states, eval_states
    for step in range(section_count):
        result = pl.pallas_call(
            functools.partial(eval_kernel, step, offsets),
            out_shape=jax.ShapeDtypeStruct(eval_states.shape, bf16),
            in_specs=[smem] + [anywhere] * (2 + len(pieces)),
            out_specs=anywhere,
            scratch_shapes=[
                pltpu.VMEM(eval_states.shape, bf16), pltpu.VMEM(eval_states.shape, bf16),
                pltpu.VMEM((2, width, rank), bf16), pltpu.SemaphoreType.DMA((4 + 2 * len(pieces),)),
            ],
            compiler_params=pltpu.CompilerParams(vmem_limit_bytes=vmem_bytes // 4),
            cost_estimate=pl.CostEstimate(
                flops=4 * eval_states.size * rank, bytes_accessed=4 * width * rank, transcendentals=0
            ),
            name="eval_block",
        )(place, current, result, *pieces)
        if step + 1 < section_count:
            current = send(result, "section", [(step, step + 1)])
    return (result[None], label_logprob[None], fisher_log[None])


def solution(mesh):
    placed = (
        P(None, "dp", None),
        P("section", None, None, None),
        P("section", None, None, None),
        P(),
        P(None, None, "dp"),
        P("dp", None),
    )
    return jax.shard_map(
        local,
        mesh=mesh,
        in_specs=placed,
        out_specs=(
            P("section", "dp", None),
            P("section", None, "dp"),
            P("section", None, "dp", None),
        ),
        check_vma=False,
    )
```

time: 340 us -> 312 us (0.918)
  Pallas kernels: 135 us -> 112 us
  waiting for transfers between devices: 125 us -> 120 us
    pallas_call x5 -> x4, Pallas kernels: 94.4 us -> 48.7 us  [last_stage(): call(token, crossing[turn], label_columns, label_rows, *weights)]
    pallas_call x7 -> x8, Pallas kernels: 26.6 us -> 51 us  [the longest x4 48 us: fisher(): call(token, *[wide for wide, _ in pairs], *[narrow for _, narrow in pairs...]
    ppermute x40 -> x38, waiting for transfers between devices: 125 us -> 120 us  [send(): return lax.ppermute(block, axis, route)]
    unnamed x47 -> x35, local copies, waits for them, and re-layouts: 7.18 us -> 7.59 us
    ppermute x40 -> x38, starting transfers between devices: 40 us -> 39.7 us  [send(): return lax.ppermute(block, axis, route)]
  transfers between devices with their start and end apart: 40 -> 38, of which waited for: 21 -> 25; matrix products, arithmetic and copies ran while one was open for 7% -> 8% of each run, Pallas kernels for 33% -> 29%
where the time goes in v1:
time: 312 us; the launch traced here: 310 us
  waiting for transfers between devices  120 us (38%)
  Pallas kernels  112 us (36%)
  starting transfers between devices  39.7 us (13%)
  other arithmetic  20.9 us (7%)
  local copies, waits for them, and re-layouts  16.2 us (5%)
    ppermute x38, waiting for transfers between devices, send(): return lax.ppermute(block, axis, route)  120 us
    pallas_call x4, Pallas kernels, last_stage(): call(token, crossing[turn], label_columns, label_rows, *weights)  48.7 us
    pallas_call x4, Pallas kernels, fisher(): call(token, *[wide for wide, _ in pairs], *[narrow for _, narrow in pairs...  48 us
    ppermute x38, starting transfers between devices, send(): return lax.ppermute(block, axis, route)  39.7 us
    convert_element_type x12, other arithmetic, ring_scatter(): moving = sums if last else [value.astype(bf16) for value in sums]  15.2 us
    pallas_call x4, Pallas kernels, local(): pl.pallas_call(functools.partial(eval_kernel, step, offsets), out_shape=j...  8.94 us
    unnamed x35, local copies, waits for them, and re-layouts  7.59 us
  transfers between devices with their start and end apart: 38, of which 25 were waited for; matrix products, arithmetic and copies ran while one was open for 8% of the time, Pallas kernels for 29%

profile of v1, /device:TPU:23, one launch (start us, length us, event | category | flops | bytes accessed | tf_op | source)
XLA Modules:
  0.0 310.4 jit_solution(18144064065423021384)
XLA Ops:
  0.7 3.4 %dynamic-slice_bitcast_fusion.1 = bf16[2,4608,128]{2,1,0:T(8,128)(2,1)} fusion(bf16[1,4,4608,128]{3,2,1,0:T(8,128)(2,1)} %param.7, s32[]{:T(128)S(6)} %select_n.154), kind=kLoop, calls=%fused_computation.1 | loop fusion | bytes 4718596 | tf_op jit(solution)/shard_map/dynamic_slice | solution.py:482
  4.8 1.6 dynamic-slice_bitcast_fusion
  7.0 2.1 collective-permute-done.down_other.refs_4_
  9.1 3.5 %collective-permute-done.1.up_other.refs_5_ = bf16[2,4608,128]{2,1,0:T(8,128)(2,1)} collective-permute-done((bf16[2,4608,128]{2,1,0:T(8,128)(2,1)}, bf16[2,4608,128]{2,1,0:T(8,128)(2,1)}, u32[]{:S(2)}, u32[]{:S(2)}) %collective-permute-start.1) | collective-permute-done | bytes 2359328 | tf_op jit(solution)/shard_map/ppermute | solution.py:399
  13.4 1.3 collective-permute-start.2
  15.4 1.3 collective-permute-start.3
  19.1 19.3 %collective-permute-done.2.states = bf16[80,4608]{1,0:T(8,128)(2,1)S(1)} collective-permute-done((bf16[80,4608]{1,0:T(8,128)(2,1)}, bf16[80,4608]{1,0:T(8,128)(2,1)S(1)}, u32[]{:S(2)}, u32[]{:S(2)}) %collective-permute-start.2) | collective-permute-done | bytes 737312 | tf_op jit(solution)/shard_map/ppermute | solution.py:399
  39.3 11.8 %last_stage.4 = (bf16[80,4608]{1,0:T(8,128)(2,1)}, f32[8,128]{1,0:T(8,128)}, bf16[2,2,80,4608]{3,2,1,0:T(8,128)(2,1)}, bf16[2,2,80,128]{3,2,1,0:T(8,128)(2,1)}) custom-call(s32[4]{0:T(128)} %pad_add_fusion.place, bf16[80,4608]{1,0:T(8,128)(2,1)} %copy-done.13, s32[2,2,80,1]{3,2,1,0:T(8,128)} %reshape.20.labels, bf16[256,4608]{1,0:T(8,128)(2,1)} %label_rows.7, ...), custom_call_target="tpu_custom_call" | custom-call | flops 1132462080 | bytes 4718592 | tf_op jit(solution)/shard_map/last_stage/pallas_call | solution.py:560
  51.1 1.3 collective-permute-start.4
  52.5 1.3 collective-permute-start.5
  55.1 11.8 %last_stage.5 = (bf16[80,4608]{1,0:T(8,128)(2,1)}, f32[8,128]{1,0:T(8,128)}, bf16[2,2,80,4608]{3,2,1,0:T(8,128)(2,1)}, bf16[2,2,80,128]{3,2,1,0:T(8,128)(2,1)}) custom-call(s32[4]{0:T(128)} %pad_add_fusion.place, bf16[80,4608]{1,0:T(8,128)(2,1)} %copy-done.11, s32[2,2,80,1]{3,2,1,0:T(8,128)} %reshape.20.labels, bf16[256,4608]{1,0:T(8,128)(2,1)} %label_rows.7, ...), custom_call_target="tpu_custom_call" | custom-call | flops 1132462080 | bytes 4718592 | tf_op jit(solution)/shard_map/last_stage/pallas_call | solution.py:560
  66.9 1.3 collective-permute-start.6
  68.3 1.3 collective-permute-start.7
  72.5 12.5 %last_stage.6 = (bf16[80,4608]{1,0:T(8,128)(2,1)}, f32[8,128]{1,0:T(8,128)}, bf16[2,2,80,4608]{3,2,1,0:T(8,128)(2,1)}, bf16[2,2,80,128]{3,2,1,0:T(8,128)(2,1)}) custom-call(s32[4]{0:T(128)} %pad_add_fusion.place, bf16[80,4608]{1,0:T(8,128)(2,1)} %copy-done.12, s32[2,2,80,1]{3,2,1,0:T(8,128)} %reshape.20.labels, bf16[256,4608]{1,0:T(8,128)(2,1)} %label_rows.7, ...), custom_call_target="tpu_custom_call" | custom-call | flops 1132462080 | bytes 4718592 | tf_op jit(solution)/shard_map/last_stage/pallas_call | solution.py:560
  85.0 1.3 collective-permute-start.8
  88.9 12.5 %last_stage.7 = (bf16[80,4608]{1,0:T(8,128)(2,1)}, f32[8,128]{1,0:T(8,128)}, bf16[2,2,80,4608]{3,2,1,0:T(8,128)(2,1)}, bf16[2,2,80,128]{3,2,1,0:T(8,128)(2,1)}) custom-call(s32[4]{0:T(128)} %pad_add_fusion.place, bf16[80,4608]{1,0:T(8,128)(2,1)} %copy-done.10, s32[2,2,80,1]{3,2,1,0:T(8,128)} %reshape.20.labels, bf16[256,4608]{1,0:T(8,128)(2,1)} %label_rows.7, ...), custom_call_target="tpu_custom_call" | custom-call | flops 1132462080 | bytes 4718592 | tf_op jit(solution)/shard_map/last_stage/pallas_call | solution.py:560
  101.5 1.3 collective-permute-start.11
  107.3 12.0 %fisher_away.2 = (f32[2,4608,128]{2,1,0:T(8,128)}, f32[2,4608,128]{2,1,0:T(8,128)}) custom-call(s32[4]{0:T(128)} %pad_add_fusion.place, bf16[2,2,80,4608]{3,2,1,0:T(8,128)(2,1)} %get-tuple-element.117.refs_0_, bf16[2,2,80,4608]{3,2,1,0:T(8,128)(2,1)} %get-tuple-element.118.refs_1_, bf16[2,2,80,128]{3,2,1,0:T(8,128)(2,1)} %get-tuple-element.93.refs_2_, ...), custom_call_target="tpu_custom_call" | custom-call | flops 377487360 | bytes 5898240 | tf_op jit(solution)/shard_map/fisher_away/pallas_call | solution.py:608
  119.3 12.0 %fisher_own.2 = (f32[2,4608,128]{2,1,0:T(8,128)}, f32[2,4608,128]{2,1,0:T(8,128)}) custom-call(s32[4]{0:T(128)} %pad_add_fusion.place, bf16[2,2,80,4608]{3,2,1,0:T(8,128)(2,1)} %get-tuple-element.117.refs_0_, bf16[2,2,80,4608]{3,2,1,0:T(8,128)(2,1)} %get-tuple-element.118.refs_1_, bf16[2,2,80,128]{3,2,1,0:T(8,128)(2,1)} %get-tuple-element.93.refs_2_, ...), custom_call_target="tpu_custom_call" | custom-call | flops 377487360 | bytes 5898240 | tf_op jit(solution)/shard_map/fisher_own/pallas_call | solution.py:608
  131.3 2.9 collective-permute-start.10
  137.5 12.0 %fisher_away.3 = (bf16[2,4608,128]{2,1,0:T(8,128)(2,1)}, bf16[2,4608,128]{2,1,0:T(8,128)(2,1)}) custom-call(s32[4]{0:T(128)} %pad_add_fusion.place, bf16[2,2,80,4608]{3,2,1,0:T(8,128)(2,1)} %get-tuple-element.132.refs_0_, bf16[2,2,80,4608]{3,2,1,0:T(8,128)(2,1)} %get-tuple-element.133.refs_1_, bf16[2,2,80,128]{3,2,1,0:T(8,128)(2,1)} %get-tuple-element.115.refs_2_, ...), custom_call_target="tpu_custom_call" | custom-call | flops 377487360 | bytes 5898240 | tf_op jit(solution)/shard_map/fisher_away/pallas_call | solution.py:608
  149.6 7.0 %collective-permute-start.12 = (bf16[2,4608,128]{2,1,0:T(8,128)(2,1)}, bf16[2,4608,128]{2,1,0:T(8,128)(2,1)S(1)}, u32[]{:S(2)}, u32[]{:S(2)}) collective-permute-start(bf16[2,4608,128]{2,1,0:T(8,128)(2,1)} %get-tuple-element.135), channel_id=1, source_target_pairs={{0,8},{8,0},{16,24},{24,16},{1,9},{9,1},{17,25},{25,17},{2,10},{10... | collective-permute-start | bytes 7077896 | tf_op jit(solution)/shard_map/ppermute | solution.py:399
  156.7 12.0 %fisher_own.3 = (bf16[2,4608,128]{2,1,0:T(8,128)(2,1)}, bf16[2,4608,128]{2,1,0:T(8,128)(2,1)}) custom-call(s32[4]{0:T(128)} %pad_add_fusion.place, bf16[2,2,80,4608]{3,2,1,0:T(8,128)(2,1)} %get-tuple-element.132.refs_0_, bf16[2,2,80,4608]{3,2,1,0:T(8,128)(2,1)} %get-tuple-element.133.refs_1_, bf16[2,2,80,128]{3,2,1,0:T(8,128)(2,1)} %get-tuple-element.115.refs_2_, ...), custom_call_target="tpu_custom_call" | custom-call | flops 377487360 | bytes 5898240 | tf_op jit(solution)/shard_map/fisher_own/pallas_call | solution.py:608
  170.0 1.1 add_convert_fusion.6
  171.1 1.3 collective-permute-start.21
  172.4 5.5 %collective-permute-done.13 = bf16[2,576,128]{2,1,0:T(8,128)(2,1)S(1)} collective-permute-done((bf16[2,576,128]{2,1,0:T(8,128)(2,1)S(1)}, bf16[2,576,128]{2,1,0:T(8,128)(2,1)S(1)}, u32[]{:S(2)}, u32[]{:S(2)}) %collective-permute-start.13) | collective-permute-done | bytes 294944 | tf_op jit(solution)/shard_map/ppermute | solution.py:399
  177.9 1.1 add_convert_fusion.12
  179.3 1.2 add_convert_fusion.5
  180.5 1.3 collective-permute-start.22
  181.8 4.5 %collective-permute-done.14 = bf16[2,576,128]{2,1,0:T(8,128)(2,1)S(1)} collective-permute-done((bf16[2,576,128]{2,1,0:T(8,128)(2,1)S(1)}, bf16[2,576,128]{2,1,0:T(8,128)(2,1)S(1)}, u32[]{:S(2)}, u32[]{:S(2)}) %collective-permute-start.14) | collective-permute-done | bytes 294944 | tf_op jit(solution)/shard_map/ppermute | solution.py:399
  186.3 1.1 add_convert_fusion.11
  187.6 1.2 add_convert_fusion.4
  188.8 1.3 collective-permute-start.23
  190.1 3.6 %collective-permute-done.15 = bf16[2,576,128]{2,1,0:T(8,128)(2,1)S(1)} collective-permute-done((bf16[2,576,128]{2,1,0:T(8,128)(2,1)S(1)}, bf16[2,576,128]{2,1,0:T(8,128)(2,1)S(1)}, u32[]{:S(2)}, u32[]{:S(2)}) %collective-permute-start.15) | collective-permute-done | bytes 294944 | tf_op jit(solution)/shard_map/ppermute | solution.py:399
  193.7 1.1 add_convert_fusion.10
  195.1 1.2 add_convert_fusion.3
  196.3 1.3 collective-permute-start.24
  197.5 2.9 collective-permute-done.16
  200.4 1.1 add_convert_fusion.9
  202.2 1.2 add_convert_fusion.2
  203.3 1.3 collective-permute-start.25
  204.6 2.6 collective-permute-done.17
  207.3 1.2 add_convert_fusion.8
  209.4 1.9 add_convert_fusion.1
  211.3 1.2 collective-permute-start.26
  212.5 2.6 collective-permute-done.18
  215.1 1.2 add_convert_fusion.7
  217.1 2.0 add_convert_fusion
  219.1 1.2 collective-permute-start.27
  220.4 4.0 %collective-permute-done.19 = bf16[2,576,128]{2,1,0:T(8,128)(2,1)S(1)} collective-permute-done((bf16[2,576,128]{2,1,0:T(8,128)(2,1)S(1)}, bf16[2,576,128]{2,1,0:T(8,128)(2,1)S(1)}, u32[]{:S(2)}, u32[]{:S(2)}) %collective-permute-start.19) | collective-permute-done | bytes 294944 | tf_op jit(solution)/shard_map/ppermute | solution.py:399
  224.4 2.2 collective-permute-done.27
  226.6 2.3 log_bitcast_fusion
  229.0 1.3 collective-permute-start.29
  230.3 4.4 %collective-permute-done.28.refs_1_ = bf16[2,576,128]{2,1,0:T(8,128)(2,1)S(1)} collective-permute-done((bf16[2,576,128]{2,1,0:T(8,128)(2,1)S(1)}, bf16[2,576,128]{2,1,0:T(8,128)(2,1)S(1)}, u32[]{:S(2)}, u32[]{:S(2)}) %collective-permute-start.28) | collective-permute-done | bytes 294944 | tf_op jit(solution)/shard_map/ppermute | solution.py:399
  234.9 2.3 collective-permute-done.29.refs_2_
  237.2 1.2 collective-permute-start.31
  238.4 1.9 collective-permute-done.30.refs_3_
  240.4 2.6 collective-permute-done.31.refs_4_
  243.0 1.2 collective-permute-start.33
  244.3 4.6 %collective-permute-done.32.refs_5_ = bf16[2,576,128]{2,1,0:T(8,128)(2,1)S(1)} collective-permute-done((bf16[2,576,128]{2,1,0:T(8,128)(2,1)S(1)}, bf16[2,576,128]{2,1,0:T(8,128)(2,1)S(1)}, u32[]{:S(2)}, u32[]{:S(2)}) %collective-permute-start.32) | collective-permute-done | bytes 294944 | tf_op jit(solution)/shard_map/ppermute | solution.py:399
  249.1 8.1 %collective-permute-done.34.refs_7_ = bf16[2,576,128]{2,1,0:T(8,128)(2,1)S(1)} collective-permute-done((bf16[2,576,128]{2,1,0:T(8,128)(2,1)S(1)}, bf16[2,576,128]{2,1,0:T(8,128)(2,1)S(1)}, u32[]{:S(2)}, u32[]{:S(2)}) %collective-permute-start.34) | collective-permute-done | bytes 294944 | tf_op jit(solution)/shard_map/ppermute | solution.py:399
  261.2 1.3 collective-permute-start.37
  263.0 40.8 %collective-permute-done.37.states = bf16[32,4608]{1,0:T(8,128)(2,1)S(1)} collective-permute-done((bf16[32,4608]{1,0:T(8,128)(2,1)S(1)}, bf16[32,4608]{1,0:T(8,128)(2,1)S(1)}, u32[]{:S(2)}, u32[]{:S(2)}) %collective-permute-start.37) | collective-permute-done | bytes 294944 | tf_op jit(solution)/shard_map/ppermute | solution.py:399
  303.9 6.4 %eval_block.7 = bf16[32,4608]{1,0:T(8,128)(2,1)} custom-call(s32[4]{0:T(128)S(1)} %copy-done.3, bf16[32,4608]{1,0:T(8,128)(2,1)S(1)} %collective-permute-done.37.states, bf16[32,4608]{1,0:T(8,128)(2,1)S(1)} %eval_block.6.before, bf16[2,576,128]{2,1,0:T(8,128)(2,1)S(1)} %get-tuple-element.145.refs_0_, ...), custom_call_target="tpu_custom_call" | custom-call | flops 75497472 | bytes 2359296 | tf_op jit(solution)/shard_map/eval_block/pallas_call | solution.py:652
  (96 shorter events, 30.4 us)
Async XLA Ops:
  0.6 16.1 %copy-start = (s32[4,5,32]{2,0,1:T(4,128)S(1)}, s32[4,5,32]{2,0,1:T(4,128)}, u32[]{:S(2)}) copy-start(s32[4,5,32]{2,0,1:T(4,128)} %param.10) | copy-start | bytes 7684
  0.7 4.1 %copy-start.4 = (bf16[1,4,4608,128]{3,2,1,0:T(8,128)(2,1)S(1)}, bf16[1,4,4608,128]{3,2,1,0:T(8,128)(2,1)}, u32[]{:S(2)}) copy-start(bf16[1,4,4608,128]{3,2,1,0:T(8,128)(2,1)} %param.8) | copy-start | bytes 14155780
  4.1 5.0 %collective-permute-start = (bf16[2,4608,128]{2,1,0:T(8,128)(2,1)}, bf16[2,4608,128]{2,1,0:T(8,128)(2,1)S(1)}, u32[]{:S(2)}, u32[]{:S(2)}) collective-permute-start(bf16[2,4608,128]{2,1,0:T(8,128)(2,1)} %dynamic-slice_bitcast_fusion.1), channel_id=1, source_target_pairs={{0,8},{8,0},{16,24},{24,16},{1,9},{9,1},{17,25},{25,17},{2,10},{10... | collective-permute-start | bytes 7077896 | tf_op jit(solution)/shard_map/ppermute | solution.py:399
  6.3 6.3 %collective-permute-start.1 = (bf16[2,4608,128]{2,1,0:T(8,128)(2,1)}, bf16[2,4608,128]{2,1,0:T(8,128)(2,1)}, u32[]{:S(2)}, u32[]{:S(2)}) collective-permute-start(bf16[2,4608,128]{2,1,0:T(8,128)(2,1)} %dynamic-slice_bitcast_fusion), channel_id=1, source_target_pairs={{0,8},{8,0},{16,24},{24,16},{1,9},{9,1},{17,25},{25,17},{2,10},{10... | collective-permute-start | bytes 7077896 | tf_op jit(solution)/shard_map/ppermute | solution.py:399
  9.1 3.5 %copy-start.5 = (bf16[2,4608,128]{2,1,0:T(8,128)(2,1)}, bf16[2,4608,128]{2,1,0:T(8,128)(2,1)S(1)}, u32[]{:S(2)}) copy-start(bf16[2,4608,128]{2,1,0:T(8,128)(2,1)S(1)} %collective-permute-done.down_other.refs_4_) | copy-start | bytes 7077892
  13.4 25.0 %collective-permute-start.2 = (bf16[80,4608]{1,0:T(8,128)(2,1)}, bf16[80,4608]{1,0:T(8,128)(2,1)S(1)}, u32[]{:S(2)}, u32[]{:S(2)}) collective-permute-start(bf16[80,4608]{1,0:T(8,128)(2,1)} %get-tuple-element.81), channel_id=1, source_target_pairs={{0,16},{8,24},{1,17},{9,25},{2,18},{10,26},{3,19},{11,27},{4,20},{... | collective-permute-start | bytes 2211848 | tf_op jit(solution)/shard_map/ppermute | solution.py:399
  15.4 38.8 %collective-permute-start.3 = (bf16[80,4608]{1,0:T(8,128)(2,1)}, bf16[80,4608]{1,0:T(8,128)(2,1)S(1)}, u32[]{:S(2)}, u32[]{:S(2)}) collective-permute-start(bf16[80,4608]{1,0:T(8,128)(2,1)} %get-tuple-element.85), channel_id=1, source_target_pairs={{0,16},{8,24},{1,17},{9,25},{2,18},{10,26},{3,19},{11,27},{4,20},{... | collective-permute-start | bytes 2211848 | tf_op jit(solution)/shard_map/ppermute | solution.py:399
  19.1 33.3 %copy-start.16 = (bf16[80,4608]{1,0:T(8,128)(2,1)S(1)}, bf16[80,4608]{1,0:T(8,128)(2,1)}, u32[]{:S(2)}) copy-start(bf16[80,4608]{1,0:T(8,128)(2,1)} %get-tuple-element.96) | copy-start | bytes 2211844
  38.4 0.9 copy-start.13
  51.1 18.4 %collective-permute-start.4 = (bf16[80,4608]{1,0:T(8,128)(2,1)}, bf16[80,4608]{1,0:T(8,128)(2,1)S(1)}, u32[]{:S(2)}, u32[]{:S(2)}) collective-permute-start(bf16[80,4608]{1,0:T(8,128)(2,1)} %get-tuple-element.88), channel_id=1, source_target_pairs={{16,0},{24,8},{17,1},{25,9},{18,2},{26,10},{19,3},{27,11},{20,4},{... | collective-permute-start | bytes 2211848 | tf_op jit(solution)/shard_map/ppermute | solution.py:399
  52.5 19.1 %collective-permute-start.5 = (bf16[80,4608]{1,0:T(8,128)(2,1)S(1)}, bf16[80,4608]{1,0:T(8,128)(2,1)S(1)}, u32[]{:S(2)}, u32[]{:S(2)}) collective-permute-start(bf16[80,4608]{1,0:T(8,128)(2,1)S(1)} %copy-done.16), channel_id=1, source_target_pairs={{0,16},{8,24},{1,17},{9,25},{2,18},{10,26},{3,19},{11,27},{4,20},{... | collective-permute-start | bytes 2211848 | tf_op jit(solution)/shard_map/ppermute | solution.py:399
  53.8 14.5 %copy-start.15 = (bf16[80,4608]{1,0:T(8,128)(2,1)S(1)}, bf16[80,4608]{1,0:T(8,128)(2,1)}, u32[]{:S(2)}) copy-start(bf16[80,4608]{1,0:T(8,128)(2,1)} %get-tuple-element.107) | copy-start | bytes 2211844
  54.2 0.9 copy-start.11
  66.9 19.4 %collective-permute-start.6 = (bf16[80,4608]{1,0:T(8,128)(2,1)}, bf16[80,4608]{1,0:T(8,128)(2,1)S(1)}, u32[]{:S(2)}, u32[]{:S(2)}) collective-permute-start(bf16[80,4608]{1,0:T(8,128)(2,1)} %get-tuple-element.99), channel_id=1, source_target_pairs={{16,0},{24,8},{17,1},{25,9},{18,2},{26,10},{19,3},{27,11},{20,4},{... | collective-permute-start | bytes 2211848 | tf_op jit(solution)/shard_map/ppermute | solution.py:399
  68.3 19.8 %collective-permute-start.7 = (bf16[80,4608]{1,0:T(8,128)(2,1)S(1)}, bf16[80,4608]{1,0:T(8,128)(2,1)S(1)}, u32[]{:S(2)}, u32[]{:S(2)}) collective-permute-start(bf16[80,4608]{1,0:T(8,128)(2,1)S(1)} %copy-done.15), channel_id=1, source_target_pairs={{0,16},{8,24},{1,17},{9,25},{2,18},{10,26},{3,19},{11,27},{4,20},{... | collective-permute-start | bytes 2211848 | tf_op jit(solution)/shard_map/ppermute | solution.py:399
  69.6 0.9 copy-start.9
  71.6 0.9 copy-start.12
  85.0 20.6 %collective-permute-start.8 = (bf16[80,4608]{1,0:T(8,128)(2,1)}, bf16[80,4608]{1,0:T(8,128)(2,1)S(1)}, u32[]{:S(2)}, u32[]{:S(2)}) collective-permute-start(bf16[80,4608]{1,0:T(8,128)(2,1)} %get-tuple-element.110), channel_id=1, source_target_pairs={{16,0},{24,8},{17,1},{25,9},{18,2},{26,10},{19,3},{27,11},{20,4},{... | collective-permute-start | bytes 2211848 | tf_op jit(solution)/shard_map/ppermute | solution.py:399
  86.3 0.9 copy-start.8
  88.1 0.9 copy-start.10
  101.5 34.2 %collective-permute-start.11 = (bf16[80,4608]{1,0:T(8,128)(2,1)}, bf16[80,4608]{1,0:T(8,128)(2,1)S(1)}, u32[]{:S(2)}, u32[]{:S(2)}) collective-permute-start(bf16[80,4608]{1,0:T(8,128)(2,1)} %get-tuple-element.125), channel_id=1, source_target_pairs={{16,0},{24,8},{17,1},{25,9},{18,2},{26,10},{19,3},{27,11},{20,4},{... | collective-permute-start | bytes 2211848 | tf_op jit(solution)/shard_map/ppermute | solution.py:399
  105.6 0.9 copy-start.7
  131.3 3.7 %collective-permute-start.10 = (f32[5,32]{1,0:T(8,128)S(1)}, f32[5,32]{1,0:T(8,128)S(1)}, u32[]{:S(2)}, u32[]{:S(2)}) collective-permute-start(f32[5,32]{1,0:T(8,128)S(1)} %get-tuple-element.146), channel_id=1, source_target_pairs={{16,0},{24,16},{17,1},{25,17},{18,2},{26,18},{19,3},{27,19},{20,4}... | collective-permute-start | bytes 1928 | tf_op jit(solution)/shard_map/ppermute | solution.py:399
  134.2 0.8 collective-permute-start.9
  135.6 0.9 copy-start.6
  149.6 19.1 %collective-permute-start.12 = (bf16[2,4608,128]{2,1,0:T(8,128)(2,1)}, bf16[2,4608,128]{2,1,0:T(8,128)(2,1)S(1)}, u32[]{:S(2)}, u32[]{:S(2)}) collective-permute-start(bf16[2,4608,128]{2,1,0:T(8,128)(2,1)} %get-tuple-element.135), channel_id=1, source_target_pairs={{0,8},{8,0},{16,24},{24,16},{1,9},{9,1},{17,25},{25,17},{2,10},{10... | collective-permute-start | bytes 7077896 | tf_op jit(solution)/shard_map/ppermute | solution.py:399
  156.6 13.4 %collective-permute-start.20 = (bf16[2,4608,128]{2,1,0:T(8,128)(2,1)}, bf16[2,4608,128]{2,1,0:T(8,128)(2,1)}, u32[]{:S(2)}, u32[]{:S(2)}) collective-permute-start(bf16[2,4608,128]{2,1,0:T(8,128)(2,1)} %get-tuple-element.140), channel_id=1, source_target_pairs={{0,8},{8,0},{16,24},{24,16},{1,9},{9,1},{17,25},{25,17},{2,10},{10... | collective-permute-start | bytes 7077896 | tf_op jit(solution)/shard_map/ppermute | solution.py:399
  169.7 8.2 %collective-permute-start.13 = (bf16[2,576,128]{2,1,0:T(8,128)(2,1)S(1)}, bf16[2,576,128]{2,1,0:T(8,128)(2,1)S(1)}, u32[]{:S(2)}, u32[]{:S(2)}) collective-permute-start(bf16[2,576,128]{2,1,0:T(8,128)(2,1)S(1)} %add_convert_fusion.13), channel_id=1, source_target_pairs={{0,2},{2,4},{4,6},{6,7},{7,5},{5,3},{3,1},{1,0},{8,10},{10,12},{12... | collective-permute-start | bytes 884744 | tf_op jit(solution)/shard_map/ppermute | solution.py:399
  171.1 8.1 %collective-permute-start.21 = (bf16[2,576,128]{2,1,0:T(8,128)(2,1)S(1)}, bf16[2,576,128]{2,1,0:T(8,128)(2,1)S(1)}, u32[]{:S(2)}, u32[]{:S(2)}) collective-permute-start(bf16[2,576,128]{2,1,0:T(8,128)(2,1)S(1)} %add_convert_fusion.6), channel_id=1, source_target_pairs={{2,0},{4,2},{6,4},{7,6},{5,7},{3,5},{1,3},{0,1},{10,8},{12,10},{14... | collective-permute-start | bytes 884744 | tf_op jit(solution)/shard_map/ppermute | solution.py:399
  179.0 7.3 %collective-permute-start.14 = (bf16[2,576,128]{2,1,0:T(8,128)(2,1)S(1)}, bf16[2,576,128]{2,1,0:T(8,128)(2,1)S(1)}, u32[]{:S(2)}, u32[]{:S(2)}) collective-permute-start(bf16[2,576,128]{2,1,0:T(8,128)(2,1)S(1)} %add_convert_fusion.12), channel_id=1, source_target_pairs={{0,2},{2,4},{4,6},{6,7},{7,5},{5,3},{3,1},{1,0},{8,10},{10,12},{12... | collective-permute-start | bytes 884744 | tf_op jit(solution)/shard_map/ppermute | solution.py:399
  180.5 7.2 %collective-permute-start.22 = (bf16[2,576,128]{2,1,0:T(8,128)(2,1)S(1)}, bf16[2,576,128]{2,1,0:T(8,128)(2,1)S(1)}, u32[]{:S(2)}, u32[]{:S(2)}) collective-permute-start(bf16[2,576,128]{2,1,0:T(8,128)(2,1)S(1)} %add_convert_fusion.5), channel_id=1, source_target_pairs={{2,0},{4,2},{6,4},{7,6},{5,7},{3,5},{1,3},{0,1},{10,8},{12,10},{14... | collective-permute-start | bytes 884744 | tf_op jit(solution)/shard_map/ppermute | solution.py:399
  187.4 6.4 %collective-permute-start.15 = (bf16[2,576,128]{2,1,0:T(8,128)(2,1)S(1)}, bf16[2,576,128]{2,1,0:T(8,128)(2,1)S(1)}, u32[]{:S(2)}, u32[]{:S(2)}) collective-permute-start(bf16[2,576,128]{2,1,0:T(8,128)(2,1)S(1)} %add_convert_fusion.11), channel_id=1, source_target_pairs={{0,2},{2,4},{4,6},{6,7},{7,5},{5,3},{3,1},{1,0},{8,10},{10,12},{12... | collective-permute-start | bytes 884744 | tf_op jit(solution)/shard_map/ppermute | solution.py:399
  188.8 6.3 %collective-permute-start.23 = (bf16[2,576,128]{2,1,0:T(8,128)(2,1)S(1)}, bf16[2,576,128]{2,1,0:T(8,128)(2,1)S(1)}, u32[]{:S(2)}, u32[]{:S(2)}) collective-permute-start(bf16[2,576,128]{2,1,0:T(8,128)(2,1)S(1)} %add_convert_fusion.4), channel_id=1, source_target_pairs={{2,0},{4,2},{6,4},{7,6},{5,7},{3,5},{1,3},{0,1},{10,8},{12,10},{14... | collective-permute-start | bytes 884744 | tf_op jit(solution)/shard_map/ppermute | solution.py:399
  194.8 5.6 %collective-permute-start.16 = (bf16[2,576,128]{2,1,0:T(8,128)(2,1)S(1)}, bf16[2,576,128]{2,1,0:T(8,128)(2,1)S(1)}, u32[]{:S(2)}, u32[]{:S(2)}) collective-permute-start(bf16[2,576,128]{2,1,0:T(8,128)(2,1)S(1)} %add_convert_fusion.10), channel_id=1, source_target_pairs={{0,2},{2,4},{4,6},{6,7},{7,5},{5,3},{3,1},{1,0},{8,10},{10,12},{12... | collective-permute-start | bytes 884744 | tf_op jit(solution)/shard_map/ppermute | solution.py:399
  196.3 5.9 %collective-permute-start.24 = (bf16[2,576,128]{2,1,0:T(8,128)(2,1)S(1)}, bf16[2,576,128]{2,1,0:T(8,128)(2,1)S(1)}, u32[]{:S(2)}, u32[]{:S(2)}) collective-permute-start(bf16[2,576,128]{2,1,0:T(8,128)(2,1)S(1)} %add_convert_fusion.3), channel_id=1, source_target_pairs={{2,0},{4,2},{6,4},{7,6},{5,7},{3,5},{1,3},{0,1},{10,8},{12,10},{14... | collective-permute-start | bytes 884744 | tf_op jit(solution)/shard_map/ppermute | solution.py:399
  201.5 5.8 %collective-permute-start.17 = (bf16[2,576,128]{2,1,0:T(8,128)(2,1)S(1)}, bf16[2,576,128]{2,1,0:T(8,128)(2,1)}, u32[]{:S(2)}, u32[]{:S(2)}) collective-permute-start(bf16[2,576,128]{2,1,0:T(8,128)(2,1)S(1)} %add_convert_fusion.9), channel_id=1, source_target_pairs={{0,2},{2,4},{4,6},{6,7},{7,5},{5,3},{3,1},{1,0},{8,10},{10,12},{12... | collective-permute-start | bytes 884744 | tf_op jit(solution)/shard_map/ppermute | solution.py:399
  203.3 6.0 %collective-permute-start.25 = (bf16[2,576,128]{2,1,0:T(8,128)(2,1)S(1)}, bf16[2,576,128]{2,1,0:T(8,128)(2,1)S(1)}, u32[]{:S(2)}, u32[]{:S(2)}) collective-permute-start(bf16[2,576,128]{2,1,0:T(8,128)(2,1)S(1)} %add_convert_fusion.2), channel_id=1, source_target_pairs={{2,0},{4,2},{6,4},{7,6},{5,7},{3,5},{1,3},{0,1},{10,8},{12,10},{14... | collective-permute-start | bytes 884744 | tf_op jit(solution)/shard_map/ppermute | solution.py:399
  208.4 6.7 %collective-permute-start.18 = (bf16[2,576,128]{2,1,0:T(8,128)(2,1)S(1)}, bf16[2,576,128]{2,1,0:T(8,128)(2,1)}, u32[]{:S(2)}, u32[]{:S(2)}) collective-permute-start(bf16[2,576,128]{2,1,0:T(8,128)(2,1)S(1)} %add_convert_fusion.8), channel_id=1, source_target_pairs={{0,2},{2,4},{4,6},{6,7},{7,5},{5,3},{3,1},{1,0},{8,10},{10,12},{12... | collective-permute-start | bytes 884744 | tf_op jit(solution)/shard_map/ppermute | solution.py:399
  211.3 5.9 %collective-permute-start.26 = (bf16[2,576,128]{2,1,0:T(8,128)(2,1)}, bf16[2,576,128]{2,1,0:T(8,128)(2,1)}, u32[]{:S(2)}, u32[]{:S(2)}) collective-permute-start(bf16[2,576,128]{2,1,0:T(8,128)(2,1)} %add_convert_fusion.1), channel_id=1, source_target_pairs={{2,0},{4,2},{6,4},{7,6},{5,7},{3,5},{1,3},{0,1},{10,8},{12,10},{14... | collective-permute-start | bytes 884744 | tf_op jit(solution)/shard_map/ppermute | solution.py:399
  212.5 44.6 %copy-start.2 = (bf16[32,4608]{1,0:T(8,128)(2,1)S(1)}, bf16[32,4608]{1,0:T(8,128)(2,1)}, u32[]{:S(2)}) copy-start(bf16[32,4608]{1,0:T(8,128)(2,1)} %before.1) | copy-start | bytes 884740
  212.5 44.6 %copy-start.3 = (s32[4]{0:T(128)S(1)}, s32[4]{0:T(128)}, u32[]{:S(2)}) copy-start(s32[4]{0:T(128)} %pad_add_fusion.place) | copy-start | bytes 52
  216.3 8.1 %collective-permute-start.19 = (bf16[2,576,128]{2,1,0:T(8,128)(2,1)S(1)}, bf16[2,576,128]{2,1,0:T(8,128)(2,1)S(1)}, u32[]{:S(2)}, u32[]{:S(2)}) collective-permute-start(bf16[2,576,128]{2,1,0:T(8,128)(2,1)S(1)} %add_convert_fusion.7), channel_id=1, source_target_pairs={{0,2},{2,4},{4,6},{6,7},{7,5},{5,3},{3,1},{1,0},{8,10},{10,12},{12... | collective-permute-start | bytes 884744 | tf_op jit(solution)/shard_map/ppermute | solution.py:399
  219.1 7.5 %collective-permute-start.27 = (bf16[2,576,128]{2,1,0:T(8,128)(2,1)}, bf16[2,576,128]{2,1,0:T(8,128)(2,1)S(1)}, u32[]{:S(2)}, u32[]{:S(2)}) collective-permute-start(bf16[2,576,128]{2,1,0:T(8,128)(2,1)} %add_convert_fusion), channel_id=1, source_target_pairs={{2,0},{4,2},{6,4},{7,6},{5,7},{3,5},{1,3},{0,1},{10,8},{12,10},{14... | collective-permute-start | bytes 884744 | tf_op jit(solution)/shard_map/ppermute | solution.py:399
  228.8 5.9 %collective-permute-start.28 = (bf16[2,576,128]{2,1,0:T(8,128)(2,1)S(1)}, bf16[2,576,128]{2,1,0:T(8,128)(2,1)S(1)}, u32[]{:S(2)}, u32[]{:S(2)}) collective-permute-start(bf16[2,576,128]{2,1,0:T(8,128)(2,1)S(1)} %get-tuple-element.145.refs_0_), channel_id=1, source_target_pairs={{0,2},{2,4},{4,6},{6,7},{7,5},{5,3},{3,1},{1,0},{8,10},{10,12},{12... | collective-permute-start | bytes 884744 | tf_op jit(solution)/shard_map/ppermute | solution.py:399
  229.0 8.2 %collective-permute-start.29 = (bf16[2,576,128]{2,1,0:T(8,128)(2,1)S(1)}, bf16[2,576,128]{2,1,0:T(8,128)(2,1)S(1)}, u32[]{:S(2)}, u32[]{:S(2)}) collective-permute-start(bf16[2,576,128]{2,1,0:T(8,128)(2,1)S(1)} %get-tuple-element.145.refs_0_), channel_id=1, source_target_pairs={{2,0},{4,2},{6,4},{7,6},{5,7},{3,5},{1,3},{0,1},{10,8},{12,10},{14... | collective-permute-start | bytes 884744 | tf_op jit(solution)/shard_map/ppermute | solution.py:399
  234.7 5.6 %collective-permute-start.30 = (bf16[2,576,128]{2,1,0:T(8,128)(2,1)S(1)}, bf16[2,576,128]{2,1,0:T(8,128)(2,1)S(1)}, u32[]{:S(2)}, u32[]{:S(2)}) collective-permute-start(bf16[2,576,128]{2,1,0:T(8,128)(2,1)S(1)} %collective-permute-done.28.refs_1_), channel_id=1, source_target_pairs={{0,2},{2,4},{4,6},{6,7},{7,5},{5,3},{3,1},{1,0},{8,10},{10,12},{12... | collective-permute-start | bytes 884744 | tf_op jit(solution)/shard_map/ppermute | solution.py:399
  237.2 5.9 %collective-permute-start.31 = (bf16[2,576,128]{2,1,0:T(8,128)(2,1)S(1)}, bf16[2,576,128]{2,1,0:T(8,128)(2,1)S(1)}, u32[]{:S(2)}, u32[]{:S(2)}) collective-permute-start(bf16[2,576,128]{2,1,0:T(8,128)(2,1)S(1)} %collective-permute-done.29.refs_2_), channel_id=1, source_target_pairs={{2,0},{4,2},{6,4},{7,6},{5,7},{3,5},{1,3},{0,1},{10,8},{12,10},{14... | collective-permute-start | bytes 884744 | tf_op jit(solution)/shard_map/ppermute | solution.py:399
  240.3 8.7 %collective-permute-start.32 = (bf16[2,576,128]{2,1,0:T(8,128)(2,1)S(1)}, bf16[2,576,128]{2,1,0:T(8,128)(2,1)S(1)}, u32[]{:S(2)}, u32[]{:S(2)}) collective-permute-start(bf16[2,576,128]{2,1,0:T(8,128)(2,1)S(1)} %collective-permute-done.30.refs_3_), channel_id=1, source_target_pairs={{0,2},{2,4},{4,6},{6,7},{7,5},{5,3},{3,1},{1,0},{8,10},{10,12},{12... | collective-permute-start | bytes 884744 | tf_op jit(solution)/shard_map/ppermute | solution.py:399
  243.0 6.0 %collective-permute-start.33 = (bf16[2,576,128]{2,1,0:T(8,128)(2,1)S(1)}, bf16[2,576,128]{2,1,0:T(8,128)(2,1)S(1)}, u32[]{:S(2)}, u32[]{:S(2)}) collective-permute-start(bf16[2,576,128]{2,1,0:T(8,128)(2,1)S(1)} %collective-permute-done.31.refs_4_), channel_id=1, source_target_pairs={{2,0},{4,2},{6,4},{7,6},{5,7},{3,5},{1,3},{0,1},{10,8},{12,10},{14... | collective-permute-start | bytes 884744 | tf_op jit(solution)/shard_map/ppermute | solution.py:399
  248.9 8.2 %collective-permute-start.34 = (bf16[2,576,128]{2,1,0:T(8,128)(2,1)S(1)}, bf16[2,576,128]{2,1,0:T(8,128)(2,1)S(1)}, u32[]{:S(2)}, u32[]{:S(2)}) collective-permute-start(bf16[2,576,128]{2,1,0:T(8,128)(2,1)S(1)} %collective-permute-done.32.refs_5_), channel_id=1, source_target_pairs={{0,2},{2,4},{4,6},{6,7},{7,5},{5,3},{3,1},{1,0},{8,10},{10,12},{12... | collective-permute-start | bytes 884744 | tf_op jit(solution)/shard_map/ppermute | solution.py:399
  258.0 0.7 collective-permute-start.35
  259.6 2.9 copy-start.14
  259.6 0.7 collective-permute-start.36
  260.3 50.0 %copy-start.1 = (s32[4,5,32]{2,0,1:T(4,128)S(1)}, s32[4,5,32]{2,0,1:T(4,128)}, u32[]{:S(2)}) copy-start(s32[4,5,32]{2,0,1:T(4,128)} %param.10) | copy-start | bytes 7684
  261.2 42.7 %collective-permute-start.37 = (bf16[32,4608]{1,0:T(8,128)(2,1)S(1)}, bf16[32,4608]{1,0:T(8,128)(2,1)S(1)}, u32[]{:S(2)}, u32[]{:S(2)}) collective-permute-start(bf16[32,4608]{1,0:T(8,128)(2,1)S(1)} %eval_block.6.before), channel_id=1, source_target_pairs={{16,24},{17,25},{18,26},{19,27},{20,28},{21,29},{22,30},{23,31}} | collective-permute-start | bytes 884744 | tf_op jit(solution)/shard_map/ppermute | solution.py:399

commit v2 on v1

--- a/solution.py
+++ b/solution.py
@@ -117,12 +117,10 @@
         self.held, self.sems = held, sems
 
     def copy(self, kind, layer):
-        return pltpu.make_async_copy(
-            self.other[kind].at[self.task], self.held[kind].at[layer], self.sems.at[kind, layer]
-        )
+        return pltpu.make_async_copy(self.other[kind], self.held[kind].at[layer], self.sems.at[kind, layer])
 
     def start(self, order):
-        tasks = self.other[0].shape[0]
+        tasks = self.own[0].shape[0] // 2
         for kind, layer in order:
             @pl.when(self.member == layer)
             def _():
@@ -344,26 +342,15 @@
                 loads[1 + kind].append(copies.start(piece.at[kind], held.at[kind, spot]))
         for load in loads[0]:
             load.wait()
-        total_rows, width = base.shape
-        loop = tiled(width)
-
-        def squared(cols, total):
-            wide = base[:, cols].astype(f32)
-            return total + row_sum(wide * wide)
-
-        scale = row_scale(loop(squared, zeros(total_rows, 1)), width)
+        width = base.shape[1]
+        wide = base[...].astype(f32)
+        scale = row_scale(row_sum(wide * wide), width)
         for load in loads[1]:
             load.wait()
-        pre = loop(lambda cols, sums: sums + nn_dot(base[:, cols], held[0, cols]), zeros(total_rows, held.shape[-1]))
-        active = gelu_value(pre * scale).astype(bf16)
+        active = gelu_value(nn_dot(base[...], held[0]) * scale).astype(bf16)
         for load in loads[2]:
             load.wait()
-
-        def up(cols, carry):
-            top[:, cols] = (base[:, cols].astype(f32) + nt_dot(active, held[1, cols])).astype(bf16)
-            return carry
-
-        loop(up, 0)
+        top[...] = (base[...].astype(f32) + nt_dot(active, held[1])).astype(bf16)
         copies.start(top, out).wait()
 
     @pl.when(place[2] != step)
@@ -372,22 +359,27 @@
         copies.start(base, out).wait()
 
 
-def fisher_kernel(halves, first, place, *refs):
+def fisher_kernel(tasks, halves, place, *refs):
     del place
-    wides, narrows, weights = refs[:halves], refs[halves:2 * halves], refs[2 * halves:2 * halves + 2]
-    before, outs = ((), refs[2 * halves + 2:]) if first else (refs[2 * halves + 2:-2], refs[-2:])
+    count = tasks * halves
+    wides, narrows = refs[:count], refs[count:2 * count]
+    weights, outs = refs[2 * count:-2], refs[-2:]
     for kind in range(2):
-        left = jnp.concatenate([ref[0, kind] for ref in wides], axis=0)
-        right = jnp.concatenate([ref[0, kind] for ref in narrows], axis=0)
-        term = tn_dot(left, right)
-        values = (term * weights[kind][0].astype(f32), term)
-        for index, out in enumerate(outs):
-            value = values[index] if first else values[index] + before[index][kind]
-            out[kind] = value.astype(out.dtype)
+        top, total = None, None
+        for task in range(tasks):
+            span = slice(task * halves, (task + 1) * halves)
+            left = jnp.concatenate([ref[0, kind] for ref in wides[span]], axis=0)
+            right = jnp.concatenate([ref[0, kind] for ref in narrows[span]], axis=0)
+            term = tn_dot(left, right)
+            scaled = term * weights[task * 2 + kind][...].astype(f32)
+            top = scaled if top is None else top + scaled
+            total = term if total is None else total + term
+        outs[0][kind] = top.astype(bf16)
+        outs[1][kind] = total.astype(bf16)
 
 
 def block_size(width):
-    return max(size for size in range(128, 513, 128) if width % size == 0)
+    return max(size for size in range(128, 1153, 128) if width % size == 0)
 
 
 smem = pl.BlockSpec(memory_space=pltpu.SMEM)
@@ -425,20 +417,22 @@
 def ring_scatter(own, other, spot, axis):
     count, ahead, back = ring_routes(axis)
     rows = own[0].shape[1] // count
-
-    def part(index, offset):
+    streams = [(index, kind) for kind in range(own[0].shape[0]) for index in range(2)]
+
+    def part(index, kind, step):
+        offset = -1 - step if index == 0 else 1 + step
         start = block_at(spot, offset, count) * rows
         return sum(
-            lax.dynamic_slice_in_dim(array[index], start, rows, 1).astype(f32) for array in (own, other)
-        )
-
-    moving = [part(0, -1).astype(bf16), part(1, 1).astype(bf16)]
-    for step in range(count - 1):
-        last = step == count - 2
-        landed = [send(moving[0], axis, ahead), send(moving[1], axis, back)]
-        sums = [landed[0].astype(f32) + part(0, -2 - step), landed[1].astype(f32) + part(1, 2 + step)]
-        moving = sums if last else [value.astype(bf16) for value in sums]
-    return moving
+            lax.dynamic_slice_in_dim(array[index][kind], start, rows, 0).astype(f32) for array in (own, other)
+        )
+
+    moving = {stream: part(*stream, 0).astype(bf16) for stream in streams}
+    for step in range(1, count):
+        for stream in streams:
+            landed = send(moving[stream], axis, back if stream[0] else ahead)
+            total = landed.astype(f32) + part(*stream, step)
+            moving[stream] = total if step == count - 1 else total.astype(bf16)
+    return [jnp.stack([moving[index, kind] for kind in range(own[0].shape[0])]) for index in range(2)]
 
 
 def ring_gather(own, axis):
@@ -479,9 +473,13 @@
     downward = [(i, i - 2) for i in sections if i - 2 >= 0]
 
     away = (1 - member) * tasks
-    down_other = send(lax.dynamic_slice_in_dim(w_down, away, tasks, 0), "section", swap)
-    up_other = send(lax.dynamic_slice_in_dim(w_up, away, tasks, 0), "section", swap)
-    weights = (w_down, w_up, down_other, up_other)
+    others = [
+        [send(lax.dynamic_index_in_dim(array, away + task, 0, keepdims=False), "section", swap) for array in (w_down, w_up)]
+        for task in range(tasks)
+    ]
+
+    def weights(turn):
+        return (w_down, w_up, *others[turn // halves])
 
     held = [
         pltpu.VMEM((2, width, rank), bf16),
@@ -534,7 +532,7 @@
             [levels, pre, scales, pltpu.SemaphoreType.DMA((4,))],
             2 * layer_flops, hbm_in=(1, 2, 3, 4, 5), hbm_out=(1, 2, 3),
         )
-        out, middle, hidden, scale = call(token, entry, *weights)
+        out, middle, hidden, scale = call(token, entry, *weights(turn))
         saved[turn] = (entry, middle, hidden, scale)
         crossing[turn] = out
         token = after(place, scale)
@@ -558,7 +556,7 @@
             hbm_in=(3, 4, 5, 6, 7), hbm_out=(2, 3),
         )
         grad, picked[turn], *squares[turn] = call(
-            token, crossing[turn], label_columns, label_rows, *weights
+            token, crossing[turn], label_columns, label_rows, *weights(turn)
         )
         returned[turn] = send(grad, "section", downward)
         token = after(place, picked[turn])
@@ -572,51 +570,42 @@
             hbm_in=range(2, 12), hbm_out=(0, 1),
             input_output_aliases={6: 0, 7: 1},
         )
-        squares[turn] = call(token, returned[turn], *saved[turn], *squares[turn], *weights)
+        squares[turn] = call(token, returned[turn], *saved[turn], *squares[turn], *weights(turn))
         token = after(place, squares[turn][1])
 
     block = block_size(width)
 
-    def fisher(task, away, sums=()):
-        first = not sums
-
+    def fisher(away):
         def layer_of(s):
             return 1 - s[1] if away else s[1]
 
-        pairs = [squares[task * halves + half] for half in range(halves)]
+        def own_spec(task):
+            return pl.BlockSpec((pl.squeezed, block, rank), lambda i, s: (s[1] * tasks + task, i, 0))
+
+        pairs = [squares[turn] for turn in range(chunks)]
         sum_spec = pl.BlockSpec((2, block, rank), lambda i, s: (0, i, 0))
+        other_spec = pl.BlockSpec((block, rank), lambda i, s: (i, 0))
         call = pl.pallas_call(
-            functools.partial(fisher_kernel, halves, first),
-            out_shape=(jax.ShapeDtypeStruct((2, width, rank), bf16 if task == tasks - 1 else f32),) * 2,
+            functools.partial(fisher_kernel, tasks, halves),
+            out_shape=(jax.ShapeDtypeStruct((2, width, rank), bf16),) * 2,
             grid_spec=pltpu.PrefetchScalarGridSpec(
                 num_scalar_prefetch=1,
                 grid=(width // block,),
-                in_specs=[pl.BlockSpec((1, 2, part, block), lambda i, s: (layer_of(s), 0, 0, i))] * halves
-                + [pl.BlockSpec((1, 2, part, rank), lambda i, s: (layer_of(s), 0, 0, 0))] * halves
-                + [pl.BlockSpec((1, block, rank), lambda i, s: (task if away else s[1] * tasks + task, i, 0))] * 2
-                + [sum_spec] * len(sums),
+                in_specs=[pl.BlockSpec((1, 2, part, block), lambda i, s: (layer_of(s), 0, 0, i))] * chunks
+                + [pl.BlockSpec((1, 2, part, rank), lambda i, s: (layer_of(s), 0, 0, 0))] * chunks
+                + [other_spec if away else own_spec(task) for task in range(tasks) for _ in range(2)],
                 out_specs=(sum_spec,) * 2,
             ),
             compiler_params=params,
             cost_estimate=pl.CostEstimate(
-                flops=4 * halves * part * width * rank,
-                bytes_accessed=8 * halves * part * width,
+                flops=4 * chunks * part * width * rank,
+                bytes_accessed=8 * chunks * part * width,
                 transcendentals=0,
             ),
             name="fisher_away" if away else "fisher_own",
         )
-        return call(
-            token, *[wide for wide, _ in pairs], *[narrow for _, narrow in pairs],
-            *(weights[2:] if away else weights[:2]), *sums,
-        )
-
-    sums = {True: (), False: ()}
-
-    def add_task(task):
-        nonlocal token
-        for away in (True, False):
-            sums[away] = fisher(task, away, sums[away])
-            token = after(place, sums[away][0])
+        matrices = sum(others, []) if away else [w_down, w_up] * tasks
+        return call(token, *[wide for wide, _ in pairs], *[narrow for _, narrow in pairs], *matrices)
 
     for turn in range(chunks):
         first_forward(turn)
@@ -626,8 +615,6 @@
             first_backward(turn - 2)
         last_stage(turn)
     first_backward(chunks - 2)
-    for task in range(tasks - 1):
-        add_task(task)
     values = jnp.stack([picked[turn][0, :part] for turn in range(chunks)]).reshape(tasks, micro, rows)
     values = after(values, token)
     label_logprob = jnp.zeros((micro, rows), f32)
@@ -637,10 +624,10 @@
         label_logprob = jnp.where(section % tasks == index, landed, label_logprob)
     token = after(token, label_logprob)
     first_backward(chunks - 1)
-    away_sums = fisher(tasks - 1, True, sums[True])
-    other_sums = [send(value, "section", swap) for value in away_sums]
+    away_sums = fisher(True)
+    other_sums = lax.optimization_barrier([send(value, "section", swap) for value in away_sums])
     token = after(place, away_sums[0])
-    sums = fisher(tasks - 1, False, sums[False])
+    sums = fisher(False)
     shares = ring_scatter(sums, other_sums, spot, "dp")
     numerator, denominator = shares
     merged_part = (numerator / (denominator + merge_eps)).astype(bf16)

time: 312 us -> 272 us (0.87)
  Pallas kernels: 112 us -> 81.4 us
  other arithmetic: 20.9 us -> 3.57 us
  starting transfers between devices: 39.7 us -> 50.5 us
  waiting for transfers between devices: 120 us -> 111 us
  local copies, waits for them, and re-layouts: 16.2 us -> 23.2 us
    pallas_call x4 -> x2, Pallas kernels: 48 us -> 18 us  [fisher(): call(token, *[wide for wide, _ in pairs], *[narrow for _, narrow in pairs...]
    convert_element_type x14 -> x29, other arithmetic: 17.4 us -> 1.78 us  [the longest x24 1.52 us: ring_scatter(): moving[stream] = total if step == count - 1 else total.astype(bf16)]
    ppermute x38 -> x54, starting transfers between devices: 39.7 us -> 50.5 us  [send(): return lax.ppermute(block, axis, route)]
    ppermute x38 -> x54, waiting for transfers between devices: 120 us -> 111 us  [send(): return lax.ppermute(block, axis, route)]
    squeeze x0 -> x2, local copies, waits for them, and re-layouts: none -> 4.97 us  [local(): lax.dynamic_index_in_dim(array, away + task, 0, keepdims=False)]
    dynamic_slice x2 -> x0, local copies, waits for them, and re-layouts: 4.95 us -> none  [the longest x1 3.4 us: local(): lax.dynamic_slice_in_dim(w_down, away, tasks, 0)]
    slice x0 -> x2, local copies, waits for them, and re-layouts: none -> 4.88 us  [part(): array[index][kind]]
    unnamed x35 -> x37, local copies, waits for them, and re-layouts: 7.59 us -> 9.75 us
  transfers between devices with their start and end apart: 38 -> 54, of which waited for: 25 -> 29; matrix products, arithmetic and copies ran while one was open for 8% -> 4% of each run, Pallas kernels for 29% -> 23%
where the time goes in v2:
time: 272 us; the launch traced here: 271 us
  waiting for transfers between devices  111 us (41%)
  Pallas kernels  81.4 us (30%)
  starting transfers between devices  50.5 us (19%)
  local copies, waits for them, and re-layouts  23.2 us (9%)
  other arithmetic  3.57 us (1%)
    ppermute x54, waiting for transfers between devices, send(): return lax.ppermute(block, axis, route)  111 us
    ppermute x54, starting transfers between devices, send(): return lax.ppermute(block, axis, route)  50.5 us
    pallas_call x4, Pallas kernels, last_stage(): call(token, crossing[turn], label_columns, label_rows, *weights(turn))  48.7 us
    pallas_call x2, Pallas kernels, fisher(): call(token, *[wide for wide, _ in pairs], *[narrow for _, narrow in pairs...  18 us
    unnamed x37, local copies, waits for them, and re-layouts  9.75 us
    pallas_call x4, Pallas kernels, local(): pl.pallas_call(functools.partial(eval_kernel, step, offsets), out_shape=j...  8.29 us
  transfers between devices with their start and end apart: 54, of which 29 were waited for; matrix products, arithmetic and copies ran while one was open for 4% of the time, Pallas kernels for 23%

profile of v2, /device:TPU:23, one launch (start us, length us, event | category | flops | bytes accessed | tf_op | source)
XLA Modules:
  0.0 271.3 jit_solution(16849601350480577476)
XLA Ops:
  0.7 3.4 %dynamic-slice_bitcast_fusion = (bf16[4608,128]{1,0:T(8,128)(2,1)}, bf16[4608,128]{1,0:T(8,128)(2,1)}) fusion(bf16[1,4,4608,128]{3,2,1,0:T(8,128)(2,1)} %param.8, s32[]{:T(128)S(6)} %select_n.208, s32[]{:T(128)S(6)} %select_n.207), kind=kLoop, calls=%fused_computation | loop fusion | bytes 4718600 | tf_op jit(solution)/shard_map/jit(dynamic_index_in_dim)/squeeze | solution.py:477
  4.7 1.6 dynamic-slice_bitcast_fusion.1
  7.6 1.8 collective-permute-done.down_other.refs_8_
  9.4 1.0 copy-done.6
  11.2 1.3 collective-permute-start.4
  13.2 1.3 collective-permute-start.5
  15.4 1.0 copy-done.7
  18.0 18.4 %collective-permute-done.4.states = bf16[80,4608]{1,0:T(8,128)(2,1)S(1)} collective-permute-done((bf16[80,4608]{1,0:T(8,128)(2,1)}, bf16[80,4608]{1,0:T(8,128)(2,1)S(1)}, u32[]{:S(2)}, u32[]{:S(2)}) %collective-permute-start.4) | collective-permute-done | bytes 737312 | tf_op jit(solution)/shard_map/ppermute | solution.py:391
  37.2 11.8 %last_stage.4 = (bf16[80,4608]{1,0:T(8,128)(2,1)}, f32[8,128]{1,0:T(8,128)}, bf16[2,2,80,4608]{3,2,1,0:T(8,128)(2,1)}, bf16[2,2,80,128]{3,2,1,0:T(8,128)(2,1)}) custom-call(s32[4]{0:T(128)} %pad_add_fusion.place, bf16[80,4608]{1,0:T(8,128)(2,1)} %copy-done.12, s32[2,2,80,1]{3,2,1,0:T(8,128)} %reshape.224.labels, bf16[256,4608]{1,0:T(8,128)(2,1)} %label_rows.7, ...), custom_call_target="tpu_custom_call" | custom-call | flops 1132462080 | bytes 4718592 | tf_op jit(solution)/shard_map/last_stage/pallas_call | solution.py:558
  49.0 1.3 collective-permute-start.6
  50.4 1.3 collective-permute-start.7
  52.9 11.9 %last_stage.5 = (bf16[80,4608]{1,0:T(8,128)(2,1)}, f32[8,128]{1,0:T(8,128)}, bf16[2,2,80,4608]{3,2,1,0:T(8,128)(2,1)}, bf16[2,2,80,128]{3,2,1,0:T(8,128)(2,1)}) custom-call(s32[4]{0:T(128)} %pad_add_fusion.place, bf16[80,4608]{1,0:T(8,128)(2,1)} %copy-done.10, s32[2,2,80,1]{3,2,1,0:T(8,128)} %reshape.224.labels, bf16[256,4608]{1,0:T(8,128)(2,1)} %label_rows.7, ...), custom_call_target="tpu_custom_call" | custom-call | flops 1132462080 | bytes 4718592 | tf_op jit(solution)/shard_map/last_stage/pallas_call | solution.py:558
  64.8 1.3 collective-permute-start.8
  66.2 1.3 collective-permute-start.9
  70.0 0.9 copy-done.14
  71.0 12.5 %last_stage.6 = (bf16[80,4608]{1,0:T(8,128)(2,1)}, f32[8,128]{1,0:T(8,128)}, bf16[2,2,80,4608]{3,2,1,0:T(8,128)(2,1)}, bf16[2,2,80,128]{3,2,1,0:T(8,128)(2,1)}) custom-call(s32[4]{0:T(128)} %pad_add_fusion.place, bf16[80,4608]{1,0:T(8,128)(2,1)} %copy-done.14, s32[2,2,80,1]{3,2,1,0:T(8,128)} %reshape.224.labels, bf16[256,4608]{1,0:T(8,128)(2,1)} %label_rows.7, ...), custom_call_target="tpu_custom_call" | custom-call | flops 1132462080 | bytes 4718592 | tf_op jit(solution)/shard_map/last_stage/pallas_call | solution.py:558
  83.5 1.3 collective-permute-start.10
  84.9 0.9 copy-done.13
  87.5 12.5 %last_stage.7 = (bf16[80,4608]{1,0:T(8,128)(2,1)}, f32[8,128]{1,0:T(8,128)}, bf16[2,2,80,4608]{3,2,1,0:T(8,128)(2,1)}, bf16[2,2,80,128]{3,2,1,0:T(8,128)(2,1)}) custom-call(s32[4]{0:T(128)} %pad_add_fusion.place, bf16[80,4608]{1,0:T(8,128)(2,1)} %copy-done.11, s32[2,2,80,1]{3,2,1,0:T(8,128)} %reshape.224.labels, bf16[256,4608]{1,0:T(8,128)(2,1)} %label_rows.7, ...), custom_call_target="tpu_custom_call" | custom-call | flops 1132462080 | bytes 4718592 | tf_op jit(solution)/shard_map/last_stage/pallas_call | solution.py:558
  100.0 1.3 collective-permute-start.13
  106.6 7.7 %collective-permute-start.12 = (f32[5,32]{1,0:T(8,128)S(1)}, f32[5,32]{1,0:T(8,128)S(1)}, u32[]{:S(2)}, u32[]{:S(2)}) collective-permute-start(f32[5,32]{1,0:T(8,128)S(1)} %get-tuple-element.152), channel_id=1, source_target_pairs={{16,0},{24,16},{17,1},{25,17},{18,2},{26,18},{19,3},{27,19},{20,4}... | collective-permute-start | bytes 1928 | tf_op jit(solution)/shard_map/ppermute | solution.py:391
  115.0 2.3 collective-permute-done.13.grad
  118.2 1.0 first_backward.7
  119.2 9.0 %fisher_away.1 = (bf16[2,4608,128]{2,1,0:T(8,128)(2,1)}, bf16[2,4608,128]{2,1,0:T(8,128)(2,1)}) custom-call(s32[4]{0:T(128)} %pad_add_fusion.place, bf16[2,2,80,4608]{3,2,1,0:T(8,128)(2,1)} %get-tuple-element.122.refs_0_, bf16[2,2,80,4608]{3,2,1,0:T(8,128)(2,1)} %get-tuple-element.123.refs_1_, bf16[2,2,80,4608]{3,2,1,0:T(8,128)(2,1)} %get-tuple-element.124.refs_2_, ...), custom_call_target="tpu_custom_call" | custom-call | flops 754974720 | bytes 11796480 | tf_op jit(solution)/shard_map/fisher_away/pallas_call | solution.py:608
  128.2 0.9 collective-permute-start.14
  129.3 9.0 %fisher_own.1 = (bf16[2,4608,128]{2,1,0:T(8,128)(2,1)}, bf16[2,4608,128]{2,1,0:T(8,128)(2,1)}) custom-call(s32[4]{0:T(128)} %pad_add_fusion.place, bf16[2,2,80,4608]{3,2,1,0:T(8,128)(2,1)} %get-tuple-element.122.refs_0_, bf16[2,2,80,4608]{3,2,1,0:T(8,128)(2,1)} %get-tuple-element.123.refs_1_, bf16[2,2,80,4608]{3,2,1,0:T(8,128)(2,1)} %get-tuple-element.124.refs_2_, ...), custom_call_target="tpu_custom_call" | custom-call | flops 754974720 | bytes 11796480 | tf_op jit(solution)/shard_map/fisher_own/pallas_call | solution.py:608
  138.2 2.6 fusion.36
  140.9 2.2 fusion.37
  143.2 1.4 collective-permute-start.30
  145.0 1.3 collective-permute-start.16
  146.5 1.7 collective-permute-done.30
  148.3 1.3 collective-permute-start.31
  149.6 1.8 collective-permute-done.37
  151.4 1.3 collective-permute-start.38
  154.0 1.3 collective-permute-start.32
  155.3 1.8 collective-permute-done.38
  157.2 1.3 collective-permute-start.39
  159.2 1.0 collective-permute-done.32
  160.3 1.4 collective-permute-start.33
  161.6 1.5 collective-permute-done.39
  163.1 1.3 collective-permute-start.40
  166.1 1.3 collective-permute-start.34
  167.4 1.4 collective-permute-done.40
  168.9 1.3 collective-permute-start.41
  170.5 1.3 collective-permute-done.26
  172.2 1.4 collective-permute-start.35
  173.6 1.0 collective-permute-done.41
  174.6 1.2 collective-permute-start.42
  176.5 2.3 collective-permute-done.27
  179.1 1.4 collective-permute-start.36
  180.7 1.3 collective-permute-start.43
  182.3 2.7 %collective-permute-done.28 = bf16[576,128]{1,0:T(8,128)(2,1)S(1)} collective-permute-done((bf16[576,128]{1,0:T(8,128)(2,1)S(1)}, bf16[576,128]{1,0:T(8,128)(2,1)S(1)}, u32[]{:S(2)}, u32[]{:S(2)}) %collective-permute-start.28) | collective-permute-done | bytes 147488 | tf_op jit(solution)/shard_map/ppermute | solution.py:391
  185.4 2.3 collective-permute-done.43
  187.9 2.9 %collective-permute-done.29 = bf16[576,128]{1,0:T(8,128)(2,1)S(1)} collective-permute-done((bf16[576,128]{1,0:T(8,128)(2,1)S(1)}, bf16[576,128]{1,0:T(8,128)(2,1)S(1)}, u32[]{:S(2)}, u32[]{:S(2)}) %collective-permute-start.29) | collective-permute-done | bytes 147488 | tf_op jit(solution)/shard_map/ppermute | solution.py:391
  191.1 1.3 collective-permute-start.45
  192.4 7.3 %collective-permute-done.44.refs_1_ = bf16[2,576,128]{2,1,0:T(8,128)(2,1)S(1)} collective-permute-done((bf16[2,576,128]{2,1,0:T(8,128)(2,1)S(1)}, bf16[2,576,128]{2,1,0:T(8,128)(2,1)S(1)}, u32[]{:S(2)}, u32[]{:S(2)}) %collective-permute-start.44) | collective-permute-done | bytes 294944 | tf_op jit(solution)/shard_map/ppermute | solution.py:391
  199.9 1.4 collective-permute-start.47
  201.3 6.5 %collective-permute-done.46.refs_3_ = bf16[2,576,128]{2,1,0:T(8,128)(2,1)S(1)} collective-permute-done((bf16[2,576,128]{2,1,0:T(8,128)(2,1)S(1)}, bf16[2,576,128]{2,1,0:T(8,128)(2,1)S(1)}, u32[]{:S(2)}, u32[]{:S(2)}) %collective-permute-start.46) | collective-permute-done | bytes 294944 | tf_op jit(solution)/shard_map/ppermute | solution.py:391
  207.9 1.4 collective-permute-start.49
  209.2 5.6 %collective-permute-done.48.refs_5_ = bf16[2,576,128]{2,1,0:T(8,128)(2,1)S(1)} collective-permute-done((bf16[2,576,128]{2,1,0:T(8,128)(2,1)S(1)}, bf16[2,576,128]{2,1,0:T(8,128)(2,1)S(1)}, u32[]{:S(2)}, u32[]{:S(2)}) %collective-permute-start.48) | collective-permute-done | bytes 294944 | tf_op jit(solution)/shard_map/ppermute | solution.py:391
  214.9 6.0 %collective-permute-done.50.refs_7_ = bf16[2,576,128]{2,1,0:T(8,128)(2,1)S(1)} collective-permute-done((bf16[2,576,128]{2,1,0:T(8,128)(2,1)S(1)}, bf16[2,576,128]{2,1,0:T(8,128)(2,1)S(1)}, u32[]{:S(2)}, u32[]{:S(2)}) %collective-permute-start.50) | collective-permute-done | bytes 294944 | tf_op jit(solution)/shard_map/ppermute | solution.py:391
  224.9 1.3 collective-permute-start.53
  227.7 37.7 %collective-permute-done.53.states = bf16[32,4608]{1,0:T(8,128)(2,1)S(1)} collective-permute-done((bf16[32,4608]{1,0:T(8,128)(2,1)S(1)}, bf16[32,4608]{1,0:T(8,128)(2,1)S(1)}, u32[]{:S(2)}, u32[]{:S(2)}) %collective-permute-start.53) | collective-permute-done | bytes 294944 | tf_op jit(solution)/shard_map/ppermute | solution.py:391
  265.4 5.7 %eval_block.7 = bf16[32,4608]{1,0:T(8,128)(2,1)} custom-call(s32[4]{0:T(128)S(1)} %copy-done.3, bf16[32,4608]{1,0:T(8,128)(2,1)S(1)} %collective-permute-done.53.states, bf16[32,4608]{1,0:T(8,128)(2,1)S(1)} %eval_block.6.before, bf16[2,576,128]{2,1,0:T(8,128)(2,1)S(1)} %fusion.refs_0_, bf16[2,576,128]{2,1,0:T(8,128)(2,1)S(1)} %collective-permute-done.44.refs_1_, ...), custom_call_target="tpu_custom_call" | custom-call | flops 75497472 | bytes 2359296 | tf_op jit(solution)/shard_map/eval_block/pallas_call | solution.py:639
  (149 shorter events, 32.3 us)
Async XLA Ops:
  0.6 13.9 %copy-start = (s32[4,5,32]{2,0,1:T(4,128)S(1)}, s32[4,5,32]{2,0,1:T(4,128)}, u32[]{:S(2)}) copy-start(s32[4,5,32]{2,0,1:T(4,128)} %param.10) | copy-start | bytes 7684
  0.7 4.1 %copy-start.4 = (bf16[1,4,4608,128]{3,2,1,0:T(8,128)(2,1)S(1)}, bf16[1,4,4608,128]{3,2,1,0:T(8,128)(2,1)}, u32[]{:S(2)}) copy-start(bf16[1,4,4608,128]{3,2,1,0:T(8,128)(2,1)} %param.7) | copy-start | bytes 14155780
  4.1 3.5 %collective-permute-start.1 = (bf16[4608,128]{1,0:T(8,128)(2,1)}, bf16[4608,128]{1,0:T(8,128)(2,1)S(1)}, u32[]{:S(2)}, u32[]{:S(2)}) collective-permute-start(bf16[4608,128]{1,0:T(8,128)(2,1)} %get-tuple-element.137), channel_id=1, source_target_pairs={{0,8},{8,0},{16,24},{24,16},{1,9},{9,1},{17,25},{25,17},{2,10},{10... | collective-permute-start | bytes 3538952 | tf_op jit(solution)/shard_map/ppermute | solution.py:391
  6.3 3.1 %collective-permute-start = (bf16[4608,128]{1,0:T(8,128)(2,1)}, bf16[4608,128]{1,0:T(8,128)(2,1)S(1)}, u32[]{:S(2)}, u32[]{:S(2)}) collective-permute-start(bf16[4608,128]{1,0:T(8,128)(2,1)} %get-tuple-element.139), channel_id=1, source_target_pairs={{0,8},{8,0},{16,24},{24,16},{1,9},{9,1},{17,25},{25,17},{2,10},{10... | collective-permute-start | bytes 3538952 | tf_op jit(solution)/shard_map/ppermute | solution.py:391
  6.4 9.0 %collective-permute-start.3 = (bf16[4608,128]{1,0:T(8,128)(2,1)}, bf16[4608,128]{1,0:T(8,128)(2,1)S(1)}, u32[]{:S(2)}, u32[]{:S(2)}) collective-permute-start(bf16[4608,128]{1,0:T(8,128)(2,1)} %get-tuple-element.136), channel_id=1, source_target_pairs={{0,8},{8,0},{16,24},{24,16},{1,9},{9,1},{17,25},{25,17},{2,10},{10... | collective-permute-start | bytes 3538952 | tf_op jit(solution)/shard_map/ppermute | solution.py:391
  6.8 8.5 %collective-permute-start.2 = (bf16[4608,128]{1,0:T(8,128)(2,1)}, bf16[4608,128]{1,0:T(8,128)(2,1)}, u32[]{:S(2)}, u32[]{:S(2)}) collective-permute-start(bf16[4608,128]{1,0:T(8,128)(2,1)} %get-tuple-element.138), channel_id=1, source_target_pairs={{0,8},{8,0},{16,24},{24,16},{1,9},{9,1},{17,25},{25,17},{2,10},{10... | collective-permute-start | bytes 3538952 | tf_op jit(solution)/shard_map/ppermute | solution.py:391
  7.6 1.8 copy-start.5
  9.4 1.0 copy-start.6
  11.2 25.2 %collective-permute-start.4 = (bf16[80,4608]{1,0:T(8,128)(2,1)}, bf16[80,4608]{1,0:T(8,128)(2,1)S(1)}, u32[]{:S(2)}, u32[]{:S(2)}) collective-permute-start(bf16[80,4608]{1,0:T(8,128)(2,1)} %get-tuple-element.77), channel_id=1, source_target_pairs={{0,16},{8,24},{1,17},{9,25},{2,18},{10,26},{3,19},{11,27},{4,20},{... | collective-permute-start | bytes 2211848 | tf_op jit(solution)/shard_map/ppermute | solution.py:391
  13.2 38.8 %collective-permute-start.5 = (bf16[80,4608]{1,0:T(8,128)(2,1)}, bf16[80,4608]{1,0:T(8,128)(2,1)S(1)}, u32[]{:S(2)}, u32[]{:S(2)}) collective-permute-start(bf16[80,4608]{1,0:T(8,128)(2,1)} %get-tuple-element.81), channel_id=1, source_target_pairs={{0,16},{8,24},{1,17},{9,25},{2,18},{10,26},{3,19},{11,27},{4,20},{... | collective-permute-start | bytes 2211848 | tf_op jit(solution)/shard_map/ppermute | solution.py:391
  15.4 1.1 copy-start.7
  17.9 32.4 %copy-start.17 = (bf16[80,4608]{1,0:T(8,128)(2,1)S(1)}, bf16[80,4608]{1,0:T(8,128)(2,1)}, u32[]{:S(2)}) copy-start(bf16[80,4608]{1,0:T(8,128)(2,1)} %get-tuple-element.92) | copy-start | bytes 2211844
  49.0 18.4 %collective-permute-start.6 = (bf16[80,4608]{1,0:T(8,128)(2,1)}, bf16[80,4608]{1,0:T(8,128)(2,1)S(1)}, u32[]{:S(2)}, u32[]{:S(2)}) collective-permute-start(bf16[80,4608]{1,0:T(8,128)(2,1)} %get-tuple-element.84), channel_id=1, source_target_pairs={{16,0},{24,8},{17,1},{25,9},{18,2},{26,10},{19,3},{27,11},{20,4},{... | collective-permute-start | bytes 2211848 | tf_op jit(solution)/shard_map/ppermute | solution.py:391
  50.4 19.7 %collective-permute-start.7 = (bf16[80,4608]{1,0:T(8,128)(2,1)S(1)}, bf16[80,4608]{1,0:T(8,128)(2,1)S(1)}, u32[]{:S(2)}, u32[]{:S(2)}) collective-permute-start(bf16[80,4608]{1,0:T(8,128)(2,1)S(1)} %copy-done.17), channel_id=1, source_target_pairs={{0,16},{8,24},{1,17},{9,25},{2,18},{10,26},{3,19},{11,27},{4,20},{... | collective-permute-start | bytes 2211848 | tf_op jit(solution)/shard_map/ppermute | solution.py:391
  51.7 14.5 %copy-start.16 = (bf16[80,4608]{1,0:T(8,128)(2,1)S(1)}, bf16[80,4608]{1,0:T(8,128)(2,1)}, u32[]{:S(2)}) copy-start(bf16[80,4608]{1,0:T(8,128)(2,1)} %get-tuple-element.103) | copy-start | bytes 2211844
  64.8 20.0 %collective-permute-start.8 = (bf16[80,4608]{1,0:T(8,128)(2,1)}, bf16[80,4608]{1,0:T(8,128)(2,1)S(1)}, u32[]{:S(2)}, u32[]{:S(2)}) collective-permute-start(bf16[80,4608]{1,0:T(8,128)(2,1)} %get-tuple-element.95), channel_id=1, source_target_pairs={{16,0},{24,8},{17,1},{25,9},{18,2},{26,10},{19,3},{27,11},{20,4},{... | collective-permute-start | bytes 2211848 | tf_op jit(solution)/shard_map/ppermute | solution.py:391
  66.2 20.4 %collective-permute-start.9 = (bf16[80,4608]{1,0:T(8,128)(2,1)S(1)}, bf16[80,4608]{1,0:T(8,128)(2,1)S(1)}, u32[]{:S(2)}, u32[]{:S(2)}) collective-permute-start(bf16[80,4608]{1,0:T(8,128)(2,1)S(1)} %copy-done.16), channel_id=1, source_target_pairs={{0,16},{8,24},{1,17},{9,25},{2,18},{10,26},{3,19},{11,27},{4,20},{... | collective-permute-start | bytes 2211848 | tf_op jit(solution)/shard_map/ppermute | solution.py:391
  83.5 20.7 %collective-permute-start.10 = (bf16[80,4608]{1,0:T(8,128)(2,1)}, bf16[80,4608]{1,0:T(8,128)(2,1)S(1)}, u32[]{:S(2)}, u32[]{:S(2)}) collective-permute-start(bf16[80,4608]{1,0:T(8,128)(2,1)} %get-tuple-element.106), channel_id=1, source_target_pairs={{16,0},{24,8},{17,1},{25,9},{18,2},{26,10},{19,3},{27,11},{20,4},{... | collective-permute-start | bytes 2211848 | tf_op jit(solution)/shard_map/ppermute | solution.py:391
  100.0 17.3 %collective-permute-start.13 = (bf16[80,4608]{1,0:T(8,128)(2,1)}, bf16[80,4608]{1,0:T(8,128)(2,1)S(1)}, u32[]{:S(2)}, u32[]{:S(2)}) collective-permute-start(bf16[80,4608]{1,0:T(8,128)(2,1)} %get-tuple-element.115), channel_id=1, source_target_pairs={{16,0},{24,8},{17,1},{25,9},{18,2},{26,10},{19,3},{27,11},{20,4},{... | collective-permute-start | bytes 2211848 | tf_op jit(solution)/shard_map/ppermute | solution.py:391
  105.9 8.4 %collective-permute-start.11 = (f32[5,32]{1,0:T(8,128)S(1)}, f32[5,32]{1,0:T(8,128)S(1)}, u32[]{:S(2)}, u32[]{:S(2)}) collective-permute-start(f32[5,32]{1,0:T(8,128)S(1)} %get-tuple-element.153), channel_id=1, source_target_pairs={{16,8},{24,24},{17,9},{25,25},{18,10},{26,26},{19,11},{27,27},{20,... | collective-permute-start | bytes 1928 | tf_op jit(solution)/shard_map/ppermute | solution.py:391
  106.6 8.5 %collective-permute-start.12 = (f32[5,32]{1,0:T(8,128)S(1)}, f32[5,32]{1,0:T(8,128)S(1)}, u32[]{:S(2)}, u32[]{:S(2)}) collective-permute-start(f32[5,32]{1,0:T(8,128)S(1)} %get-tuple-element.152), channel_id=1, source_target_pairs={{16,0},{24,16},{17,1},{25,17},{18,2},{26,18},{19,3},{27,19},{20,4}... | collective-permute-start | bytes 1928 | tf_op jit(solution)/shard_map/ppermute | solution.py:391
  128.2 12.7 %collective-permute-start.14 = (bf16[2,4608,128]{2,1,0:T(8,128)(2,1)}, bf16[2,4608,128]{2,1,0:T(8,128)(2,1)S(1)}, u32[]{:S(2)}, u32[]{:S(2)}) collective-permute-start(bf16[2,4608,128]{2,1,0:T(8,128)(2,1)} %get-tuple-element.126), channel_id=1, source_target_pairs={{0,8},{8,0},{16,24},{24,16},{1,9},{9,1},{17,25},{25,17},{2,10},{10... | collective-permute-start | bytes 7077896 | tf_op jit(solution)/shard_map/ppermute | solution.py:391
  129.2 11.7 %collective-permute-start.15 = (bf16[2,4608,128]{2,1,0:T(8,128)(2,1)}, bf16[2,4608,128]{2,1,0:T(8,128)(2,1)}, u32[]{:S(2)}, u32[]{:S(2)}) collective-permute-start(bf16[2,4608,128]{2,1,0:T(8,128)(2,1)} %get-tuple-element.129), channel_id=1, source_target_pairs={{0,8},{8,0},{16,24},{24,16},{1,9},{9,1},{17,25},{25,17},{2,10},{10... | collective-permute-start | bytes 7077896 | tf_op jit(solution)/shard_map/ppermute | solution.py:391
  143.2 5.0 %collective-permute-start.30 = (bf16[576,128]{1,0:T(8,128)(2,1)S(1)}, bf16[576,128]{1,0:T(8,128)(2,1)S(1)}, u32[]{:S(2)}, u32[]{:S(2)}) collective-permute-start(bf16[576,128]{1,0:T(8,128)(2,1)S(1)} %fusion.34), channel_id=1, source_target_pairs={{2,0},{4,2},{6,4},{7,6},{5,7},{3,5},{1,3},{0,1},{10,8},{12,10},{14... | collective-permute-start | bytes 442376 | tf_op jit(solution)/shard_map/ppermute | solution.py:391
  144.6 6.8 %collective-permute-start.37 = (bf16[576,128]{1,0:T(8,128)(2,1)S(1)}, bf16[576,128]{1,0:T(8,128)(2,1)S(1)}, u32[]{:S(2)}, u32[]{:S(2)}) collective-permute-start(bf16[576,128]{1,0:T(8,128)(2,1)S(1)} %fusion.35), channel_id=1, source_target_pairs={{2,0},{4,2},{6,4},{7,6},{5,7},{3,5},{1,3},{0,1},{10,8},{12,10},{14... | collective-permute-start | bytes 442376 | tf_op jit(solution)/shard_map/ppermute | solution.py:391
  145.0 7.8 %collective-permute-start.16 = (bf16[576,128]{1,0:T(8,128)(2,1)S(1)}, bf16[576,128]{1,0:T(8,128)(2,1)S(1)}, u32[]{:S(2)}, u32[]{:S(2)}) collective-permute-start(bf16[576,128]{1,0:T(8,128)(2,1)S(1)} %fusion.32), channel_id=1, source_target_pairs={{0,2},{2,4},{4,6},{6,7},{7,5},{5,3},{3,1},{1,0},{8,10},{10,12},{12... | collective-permute-start | bytes 442376 | tf_op jit(solution)/shard_map/ppermute | solution.py:391
  146.3 6.8 %collective-permute-start.23 = (bf16[576,128]{1,0:T(8,128)(2,1)S(1)}, bf16[576,128]{1,0:T(8,128)(2,1)S(1)}, u32[]{:S(2)}, u32[]{:S(2)}) collective-permute-start(bf16[576,128]{1,0:T(8,128)(2,1)S(1)} %fusion.33), channel_id=1, source_target_pairs={{0,2},{2,4},{4,6},{6,7},{7,5},{5,3},{3,1},{1,0},{8,10},{10,12},{12... | collective-permute-start | bytes 442376 | tf_op jit(solution)/shard_map/ppermute | solution.py:391
  148.3 5.7 %collective-permute-start.31 = (bf16[576,128]{1,0:T(8,128)(2,1)S(1)}, bf16[576,128]{1,0:T(8,128)(2,1)S(1)}, u32[]{:S(2)}, u32[]{:S(2)}) collective-permute-start(bf16[576,128]{1,0:T(8,128)(2,1)S(1)} %fusion.13), channel_id=1, source_target_pairs={{2,0},{4,2},{6,4},{7,6},{5,7},{3,5},{1,3},{0,1},{10,8},{12,10},{14... | collective-permute-start | bytes 442376 | tf_op jit(solution)/shard_map/ppermute | solution.py:391
  151.4 5.7 %collective-permute-start.38 = (bf16[576,128]{1,0:T(8,128)(2,1)S(1)}, bf16[576,128]{1,0:T(8,128)(2,1)S(1)}, u32[]{:S(2)}, u32[]{:S(2)}) collective-permute-start(bf16[576,128]{1,0:T(8,128)(2,1)S(1)} %fusion.7), channel_id=1, source_target_pairs={{2,0},{4,2},{6,4},{7,6},{5,7},{3,5},{1,3},{0,1},{10,8},{12,10},{14... | collective-permute-start | bytes 442376 | tf_op jit(solution)/shard_map/ppermute | solution.py:391
  152.8 5.7 %collective-permute-start.17 = (bf16[576,128]{1,0:T(8,128)(2,1)S(1)}, bf16[576,128]{1,0:T(8,128)(2,1)S(1)}, u32[]{:S(2)}, u32[]{:S(2)}) collective-permute-start(bf16[576,128]{1,0:T(8,128)(2,1)S(1)} %fusion.27), channel_id=1, source_target_pairs={{0,2},{2,4},{4,6},{6,7},{7,5},{5,3},{3,1},{1,0},{8,10},{10,12},{12... | collective-permute-start | bytes 442376 | tf_op jit(solution)/shard_map/ppermute | solution.py:391
  153.1 5.7 %collective-permute-start.24 = (bf16[576,128]{1,0:T(8,128)(2,1)S(1)}, bf16[576,128]{1,0:T(8,128)(2,1)S(1)}, u32[]{:S(2)}, u32[]{:S(2)}) collective-permute-start(bf16[576,128]{1,0:T(8,128)(2,1)S(1)} %fusion.20), channel_id=1, source_target_pairs={{0,2},{2,4},{4,6},{6,7},{7,5},{5,3},{3,1},{1,0},{8,10},{10,12},{12... | collective-permute-start | bytes 442376 | tf_op jit(solution)/shard_map/ppermute | solution.py:391
  154.0 6.2 %collective-permute-start.32 = (bf16[576,128]{1,0:T(8,128)(2,1)S(1)}, bf16[576,128]{1,0:T(8,128)(2,1)S(1)}, u32[]{:S(2)}, u32[]{:S(2)}) collective-permute-start(bf16[576,128]{1,0:T(8,128)(2,1)S(1)} %fusion.12), channel_id=1, source_target_pairs={{2,0},{4,2},{6,4},{7,6},{5,7},{3,5},{1,3},{0,1},{10,8},{12,10},{14... | collective-permute-start | bytes 442376 | tf_op jit(solution)/shard_map/ppermute | solution.py:391
  157.2 5.9 %collective-permute-start.39 = (bf16[576,128]{1,0:T(8,128)(2,1)S(1)}, bf16[576,128]{1,0:T(8,128)(2,1)S(1)}, u32[]{:S(2)}, u32[]{:S(2)}) collective-permute-start(bf16[576,128]{1,0:T(8,128)(2,1)S(1)} %fusion.6), channel_id=1, source_target_pairs={{2,0},{4,2},{6,4},{7,6},{5,7},{3,5},{1,3},{0,1},{10,8},{12,10},{14... | collective-permute-start | bytes 442376 | tf_op jit(solution)/shard_map/ppermute | solution.py:391
  158.5 5.9 %collective-permute-start.18 = (bf16[576,128]{1,0:T(8,128)(2,1)S(1)}, bf16[576,128]{1,0:T(8,128)(2,1)S(1)}, u32[]{:S(2)}, u32[]{:S(2)}) collective-permute-start(bf16[576,128]{1,0:T(8,128)(2,1)S(1)} %fusion.26), channel_id=1, source_target_pairs={{0,2},{2,4},{4,6},{6,7},{7,5},{5,3},{3,1},{1,0},{8,10},{10,12},{12... | collective-permute-start | bytes 442376 | tf_op jit(solution)/shard_map/ppermute | solution.py:391
  158.9 6.2 %collective-permute-start.25 = (bf16[576,128]{1,0:T(8,128)(2,1)S(1)}, bf16[576,128]{1,0:T(8,128)(2,1)S(1)}, u32[]{:S(2)}, u32[]{:S(2)}) collective-permute-start(bf16[576,128]{1,0:T(8,128)(2,1)S(1)} %fusion.19), channel_id=1, source_target_pairs={{0,2},{2,4},{4,6},{6,7},{7,5},{5,3},{3,1},{1,0},{8,10},{10,12},{12... | collective-permute-start | bytes 442376 | tf_op jit(solution)/shard_map/ppermute | solution.py:391
  160.3 5.7 %collective-permute-start.33 = (bf16[576,128]{1,0:T(8,128)(2,1)S(1)}, bf16[576,128]{1,0:T(8,128)(2,1)S(1)}, u32[]{:S(2)}, u32[]{:S(2)}) collective-permute-start(bf16[576,128]{1,0:T(8,128)(2,1)S(1)} %fusion.11), channel_id=1, source_target_pairs={{2,0},{4,2},{6,4},{7,6},{5,7},{3,5},{1,3},{0,1},{10,8},{12,10},{14... | collective-permute-start | bytes 442376 | tf_op jit(solution)/shard_map/ppermute | solution.py:391
  163.1 5.7 %collective-permute-start.40 = (bf16[576,128]{1,0:T(8,128)(2,1)S(1)}, bf16[576,128]{1,0:T(8,128)(2,1)S(1)}, u32[]{:S(2)}, u32[]{:S(2)}) collective-permute-start(bf16[576,128]{1,0:T(8,128)(2,1)S(1)} %fusion.5), channel_id=1, source_target_pairs={{2,0},{4,2},{6,4},{7,6},{5,7},{3,5},{1,3},{0,1},{10,8},{12,10},{14... | collective-permute-start | bytes 442376 | tf_op jit(solution)/shard_map/ppermute | solution.py:391
  164.5 5.7 %collective-permute-start.19 = (bf16[576,128]{1,0:T(8,128)(2,1)S(1)}, bf16[576,128]{1,0:T(8,128)(2,1)S(1)}, u32[]{:S(2)}, u32[]{:S(2)}) collective-permute-start(bf16[576,128]{1,0:T(8,128)(2,1)S(1)} %fusion.25), channel_id=1, source_target_pairs={{0,2},{2,4},{4,6},{6,7},{7,5},{5,3},{3,1},{1,0},{8,10},{10,12},{12... | collective-permute-start | bytes 442376 | tf_op jit(solution)/shard_map/ppermute | solution.py:391
  165.1 6.7 %collective-permute-start.26 = (bf16[576,128]{1,0:T(8,128)(2,1)S(1)}, bf16[576,128]{1,0:T(8,128)(2,1)S(1)}, u32[]{:S(2)}, u32[]{:S(2)}) collective-permute-start(bf16[576,128]{1,0:T(8,128)(2,1)S(1)} %fusion.18), channel_id=1, source_target_pairs={{0,2},{2,4},{4,6},{6,7},{7,5},{5,3},{3,1},{1,0},{8,10},{10,12},{12... | collective-permute-start | bytes 442376 | tf_op jit(solution)/shard_map/ppermute | solution.py:391
  166.1 6.1 %collective-permute-start.34 = (bf16[576,128]{1,0:T(8,128)(2,1)S(1)}, bf16[576,128]{1,0:T(8,128)(2,1)S(1)}, u32[]{:S(2)}, u32[]{:S(2)}) collective-permute-start(bf16[576,128]{1,0:T(8,128)(2,1)S(1)} %fusion.10), channel_id=1, source_target_pairs={{2,0},{4,2},{6,4},{7,6},{5,7},{3,5},{1,3},{0,1},{10,8},{12,10},{14... | collective-permute-start | bytes 442376 | tf_op jit(solution)/shard_map/ppermute | solution.py:391
  168.9 5.7 %collective-permute-start.41 = (bf16[576,128]{1,0:T(8,128)(2,1)S(1)}, bf16[576,128]{1,0:T(8,128)(2,1)S(1)}, u32[]{:S(2)}, u32[]{:S(2)}) collective-permute-start(bf16[576,128]{1,0:T(8,128)(2,1)S(1)} %fusion.4), channel_id=1, source_target_pairs={{2,0},{4,2},{6,4},{7,6},{5,7},{3,5},{1,3},{0,1},{10,8},{12,10},{14... | collective-permute-start | bytes 442376 | tf_op jit(solution)/shard_map/ppermute | solution.py:391
  170.3 5.9 %collective-permute-start.20 = (bf16[576,128]{1,0:T(8,128)(2,1)S(1)}, bf16[576,128]{1,0:T(8,128)(2,1)S(1)}, u32[]{:S(2)}, u32[]{:S(2)}) collective-permute-start(bf16[576,128]{1,0:T(8,128)(2,1)S(1)} %fusion.24), channel_id=1, source_target_pairs={{0,2},{2,4},{4,6},{6,7},{7,5},{5,3},{3,1},{1,0},{8,10},{10,12},{12... | collective-permute-start | bytes 442376 | tf_op jit(solution)/shard_map/ppermute | solution.py:391
  171.9 6.8 %collective-permute-start.27 = (bf16[576,128]{1,0:T(8,128)(2,1)S(1)}, bf16[576,128]{1,0:T(8,128)(2,1)S(1)}, u32[]{:S(2)}, u32[]{:S(2)}) collective-permute-start(bf16[576,128]{1,0:T(8,128)(2,1)S(1)} %fusion.17), channel_id=1, source_target_pairs={{0,2},{2,4},{4,6},{6,7},{7,5},{5,3},{3,1},{1,0},{8,10},{10,12},{12... | collective-permute-start | bytes 442376 | tf_op jit(solution)/shard_map/ppermute | solution.py:391
  172.2 6.8 %collective-permute-start.35 = (bf16[576,128]{1,0:T(8,128)(2,1)S(1)}, bf16[576,128]{1,0:T(8,128)(2,1)S(1)}, u32[]{:S(2)}, u32[]{:S(2)}) collective-permute-start(bf16[576,128]{1,0:T(8,128)(2,1)S(1)} %fusion.9), channel_id=1, source_target_pairs={{2,0},{4,2},{6,4},{7,6},{5,7},{3,5},{1,3},{0,1},{10,8},{12,10},{14... | collective-permute-start | bytes 442376 | tf_op jit(solution)/shard_map/ppermute | solution.py:391
  174.6 6.0 %collective-permute-start.42 = (bf16[576,128]{1,0:T(8,128)(2,1)S(1)}, bf16[576,128]{1,0:T(8,128)(2,1)S(1)}, u32[]{:S(2)}, u32[]{:S(2)}) collective-permute-start(bf16[576,128]{1,0:T(8,128)(2,1)S(1)} %fusion.3), channel_id=1, source_target_pairs={{2,0},{4,2},{6,4},{7,6},{5,7},{3,5},{1,3},{0,1},{10,8},{12,10},{14... | collective-permute-start | bytes 442376 | tf_op jit(solution)/shard_map/ppermute | solution.py:391
  176.3 5.7 %collective-permute-start.21 = (bf16[576,128]{1,0:T(8,128)(2,1)S(1)}, bf16[576,128]{1,0:T(8,128)(2,1)S(1)}, u32[]{:S(2)}, u32[]{:S(2)}) collective-permute-start(bf16[576,128]{1,0:T(8,128)(2,1)S(1)} %fusion.23), channel_id=1, source_target_pairs={{0,2},{2,4},{4,6},{6,7},{7,5},{5,3},{3,1},{1,0},{8,10},{10,12},{12... | collective-permute-start | bytes 442376 | tf_op jit(solution)/shard_map/ppermute | solution.py:391
  178.8 6.2 %collective-permute-start.28 = (bf16[576,128]{1,0:T(8,128)(2,1)S(1)}, bf16[576,128]{1,0:T(8,128)(2,1)S(1)}, u32[]{:S(2)}, u32[]{:S(2)}) collective-permute-start(bf16[576,128]{1,0:T(8,128)(2,1)S(1)} %fusion.16), channel_id=1, source_target_pairs={{0,2},{2,4},{4,6},{6,7},{7,5},{5,3},{3,1},{1,0},{8,10},{10,12},{12... | collective-permute-start | bytes 442376 | tf_op jit(solution)/shard_map/ppermute | solution.py:391
  179.1 6.2 %collective-permute-start.36 = (bf16[576,128]{1,0:T(8,128)(2,1)S(1)}, bf16[576,128]{1,0:T(8,128)(2,1)S(1)}, u32[]{:S(2)}, u32[]{:S(2)}) collective-permute-start(bf16[576,128]{1,0:T(8,128)(2,1)S(1)} %fusion.8), channel_id=1, source_target_pairs={{2,0},{4,2},{6,4},{7,6},{5,7},{3,5},{1,3},{0,1},{10,8},{12,10},{14... | collective-permute-start | bytes 442376 | tf_op jit(solution)/shard_map/ppermute | solution.py:391
  180.7 7.0 %collective-permute-start.43 = (bf16[576,128]{1,0:T(8,128)(2,1)S(1)}, bf16[576,128]{1,0:T(8,128)(2,1)S(1)}, u32[]{:S(2)}, u32[]{:S(2)}) collective-permute-start(bf16[576,128]{1,0:T(8,128)(2,1)S(1)} %fusion.2), channel_id=1, source_target_pairs={{2,0},{4,2},{6,4},{7,6},{5,7},{3,5},{1,3},{0,1},{10,8},{12,10},{14... | collective-permute-start | bytes 442376 | tf_op jit(solution)/shard_map/ppermute | solution.py:391
  182.1 5.7 %collective-permute-start.22 = (bf16[576,128]{1,0:T(8,128)(2,1)S(1)}, bf16[576,128]{1,0:T(8,128)(2,1)S(1)}, u32[]{:S(2)}, u32[]{:S(2)}) collective-permute-start(bf16[576,128]{1,0:T(8,128)(2,1)S(1)} %fusion.22), channel_id=1, source_target_pairs={{0,2},{2,4},{4,6},{6,7},{7,5},{5,3},{3,1},{1,0},{8,10},{10,12},{12... | collective-permute-start | bytes 442376 | tf_op jit(solution)/shard_map/ppermute | solution.py:391
  185.1 5.7 %collective-permute-start.29 = (bf16[576,128]{1,0:T(8,128)(2,1)S(1)}, bf16[576,128]{1,0:T(8,128)(2,1)S(1)}, u32[]{:S(2)}, u32[]{:S(2)}) collective-permute-start(bf16[576,128]{1,0:T(8,128)(2,1)S(1)} %fusion.15), channel_id=1, source_target_pairs={{0,2},{2,4},{4,6},{6,7},{7,5},{5,3},{3,1},{1,0},{8,10},{10,12},{12... | collective-permute-start | bytes 442376 | tf_op jit(solution)/shard_map/ppermute | solution.py:391
  187.9 33.0 %copy-start.2 = (bf16[32,4608]{1,0:T(8,128)(2,1)S(1)}, bf16[32,4608]{1,0:T(8,128)(2,1)}, u32[]{:S(2)}) copy-start(bf16[32,4608]{1,0:T(8,128)(2,1)} %before.1) | copy-start | bytes 884740
  187.9 33.0 %copy-start.3 = (s32[4]{0:T(128)S(1)}, s32[4]{0:T(128)}, u32[]{:S(2)}) copy-start(s32[4]{0:T(128)} %pad_add_fusion.place) | copy-start | bytes 52
  190.9 8.9 %collective-permute-start.44 = (bf16[2,576,128]{2,1,0:T(8,128)(2,1)S(1)}, bf16[2,576,128]{2,1,0:T(8,128)(2,1)S(1)}, u32[]{:S(2)}, u32[]{:S(2)}) collective-permute-start(bf16[2,576,128]{2,1,0:T(8,128)(2,1)S(1)} %fusion.refs_0_), channel_id=1, source_target_pairs={{0,2},{2,4},{4,6},{6,7},{7,5},{5,3},{3,1},{1,0},{8,10},{10,12},{12... | collective-permute-start | bytes 884744 | tf_op jit(solution)/shard_map/ppermute | solution.py:391
  191.1 8.8 %collective-permute-start.45 = (bf16[2,576,128]{2,1,0:T(8,128)(2,1)S(1)}, bf16[2,576,128]{2,1,0:T(8,128)(2,1)S(1)}, u32[]{:S(2)}, u32[]{:S(2)}) collective-permute-start(bf16[2,576,128]{2,1,0:T(8,128)(2,1)S(1)} %fusion.refs_0_), channel_id=1, source_target_pairs={{2,0},{4,2},{6,4},{7,6},{5,7},{3,5},{1,3},{0,1},{10,8},{12,10},{14... | collective-permute-start | bytes 884744 | tf_op jit(solution)/shard_map/ppermute | solution.py:391
  199.8 8.0 %collective-permute-start.46 = (bf16[2,576,128]{2,1,0:T(8,128)(2,1)S(1)}, bf16[2,576,128]{2,1,0:T(8,128)(2,1)S(1)}, u32[]{:S(2)}, u32[]{:S(2)}) collective-permute-start(bf16[2,576,128]{2,1,0:T(8,128)(2,1)S(1)} %collective-permute-done.44.refs_1_), channel_id=1, source_target_pairs={{0,2},{2,4},{4,6},{6,7},{7,5},{5,3},{3,1},{1,0},{8,10},{10,12},{12... | collective-permute-start | bytes 884744 | tf_op jit(solution)/shard_map/ppermute | solution.py:391
  199.9 8.0 %collective-permute-start.47 = (bf16[2,576,128]{2,1,0:T(8,128)(2,1)S(1)}, bf16[2,576,128]{2,1,0:T(8,128)(2,1)S(1)}, u32[]{:S(2)}, u32[]{:S(2)}) collective-permute-start(bf16[2,576,128]{2,1,0:T(8,128)(2,1)S(1)} %collective-permute-done.45.refs_2_), channel_id=1, source_target_pairs={{2,0},{4,2},{6,4},{7,6},{5,7},{3,5},{1,3},{0,1},{10,8},{12,10},{14... | collective-permute-start | bytes 884744 | tf_op jit(solution)/shard_map/ppermute | solution.py:391
  207.8 7.0 %collective-permute-start.48 = (bf16[2,576,128]{2,1,0:T(8,128)(2,1)S(1)}, bf16[2,576,128]{2,1,0:T(8,128)(2,1)S(1)}, u32[]{:S(2)}, u32[]{:S(2)}) collective-permute-start(bf16[2,576,128]{2,1,0:T(8,128)(2,1)S(1)} %collective-permute-done.46.refs_3_), channel_id=1, source_target_pairs={{0,2},{2,4},{4,6},{6,7},{7,5},{5,3},{3,1},{1,0},{8,10},{10,12},{12... | collective-permute-start | bytes 884744 | tf_op jit(solution)/shard_map/ppermute | solution.py:391
  207.9 7.0 %collective-permute-start.49 = (bf16[2,576,128]{2,1,0:T(8,128)(2,1)S(1)}, bf16[2,576,128]{2,1,0:T(8,128)(2,1)S(1)}, u32[]{:S(2)}, u32[]{:S(2)}) collective-permute-start(bf16[2,576,128]{2,1,0:T(8,128)(2,1)S(1)} %collective-permute-done.47.refs_4_), channel_id=1, source_target_pairs={{2,0},{4,2},{6,4},{7,6},{5,7},{3,5},{1,3},{0,1},{10,8},{12,10},{14... | collective-permute-start | bytes 884744 | tf_op jit(solution)/shard_map/ppermute | solution.py:391
  214.8 6.1 %collective-permute-start.50 = (bf16[2,576,128]{2,1,0:T(8,128)(2,1)S(1)}, bf16[2,576,128]{2,1,0:T(8,128)(2,1)S(1)}, u32[]{:S(2)}, u32[]{:S(2)}) collective-permute-start(bf16[2,576,128]{2,1,0:T(8,128)(2,1)S(1)} %collective-permute-done.48.refs_5_), channel_id=1, source_target_pairs={{0,2},{2,4},{4,6},{6,7},{7,5},{5,3},{3,1},{1,0},{8,10},{10,12},{12... | collective-permute-start | bytes 884744 | tf_op jit(solution)/shard_map/ppermute | solution.py:391
  221.8 0.7 collective-permute-start.51
  223.3 0.7 collective-permute-start.52
  224.9 40.5 %collective-permute-start.53 = (bf16[32,4608]{1,0:T(8,128)(2,1)S(1)}, bf16[32,4608]{1,0:T(8,128)(2,1)S(1)}, u32[]{:S(2)}, u32[]{:S(2)}) collective-permute-start(bf16[32,4608]{1,0:T(8,128)(2,1)S(1)} %eval_block.6.before), channel_id=1, source_target_pairs={{16,24},{17,25},{18,26},{19,27},{20,28},{21,29},{22,30},{23,31}} | collective-permute-start | bytes 884744 | tf_op jit(solution)/shard_map/ppermute | solution.py:391
  226.8 44.3 %copy-start.1 = (s32[4,5,32]{2,0,1:T(4,128)S(1)}, s32[4,5,32]{2,0,1:T(4,128)}, u32[]{:S(2)}) copy-start(s32[4,5,32]{2,0,1:T(4,128)} %param.10) | copy-start | bytes 7684
  (8 other events, 7.1 us)

commit v3 on v2

--- a/solution.py
+++ b/solution.py
@@ -228,13 +228,13 @@
     loop(finish, 0)
 
 
-def first_forward_kernel(task, half, place, entry, down, up, down_other, up_other, out, middle, hidden, scales_out,
+def first_forward_kernel(task, start, place, entry, down, up, down_other, up_other, out, middle, hidden, scales_out,
                          levels, pre, scales, sems, held_down, held_up, weight_sems):
     @pl.when(place[0] == 0)
     def _():
         rows = levels.shape[1]
         copies = Copies(sems)
-        load = copies.start(entry.at[pl.ds(half * rows, rows)], levels.at[0])
+        load = copies.start(entry.at[pl.ds(start, rows)], levels.at[0])
         weights = StageWeights(
             place[1], task, (down, up), (down_other, up_other), (held_down, held_up), weight_sems
         )
@@ -261,7 +261,7 @@
             copy.wait()
 
 
-def first_backward_kernel(task, half, place, grad, entry, middle, hidden, scales_in, wide_in, narrow_in,
+def first_backward_kernel(task, start, place, grad, entry, middle, hidden, scales_in, wide_in, narrow_in,
                           down, up, down_other, up_other, wide_out, narrow_out,
                           grads, levels, pre, scales, wide, narrow, square_sems, sems,
                           held_down, held_up, weight_sems):
@@ -275,7 +275,7 @@
             copies.start(source, target)
             for source, target in (
                 (grad, grads.at[2]), (hidden, pre), (scales_in, scales), (middle, levels.at[1]),
-                (entry.at[pl.ds(half * rows, rows)], levels.at[0]),
+                (entry.at[pl.ds(start, rows)], levels.at[0]),
             )
         ]
         weights = StageWeights(
@@ -290,7 +290,7 @@
         squares.wait()
 
 
-def last_stage_kernel(task, half, place, states, labels, label_rows, down, up, down_other, up_other,
+def last_stage_kernel(task, start, place, states, labels, label_rows, down, up, down_other, up_other,
                       grad_out, picked, wide_out, narrow_out,
                       levels, words, marks, chosen, pre, scales, grads, wide, narrow, square_sems, sems,
                       held_down, held_up, weight_sems):
@@ -303,7 +303,7 @@
             place[1], task, (down, up), (down_other, up_other), (held_down, held_up), weight_sems
         )
         weights.start([(0, 0), (1, 0), (0, 1), (1, 1)])
-        later = [copies.start(label_rows, words), copies.start(labels.at[task, half], marks)]
+        later = [copies.start(label_rows, words), copies.start(labels.at[task, pl.ds(start, rows)], marks)]
         loaded.wait()
         forward_loop(levels, pre, scales, weights, held_down, held_up, lambda layer: None)
         for copy in later:
@@ -327,43 +327,19 @@
         last.wait()
 
 
-def eval_kernel(step, offsets, place, states, before, *refs):
-    *pieces, out, base, top, held, sems = refs
-    copies = Copies(sems)
-    rows = pieces[0].shape[1]
-
-    @pl.when(place[2] == step)
-    def _():
-        loads = [[copies.start(states, base)], [], []]
-        for kind in range(2):
-            for index, piece in enumerate(pieces):
-                block = block_at(place[3], offsets[index], len(pieces))
-                spot = pl.ds(pl.multiple_of(block * rows, 16), rows)
-                loads[1 + kind].append(copies.start(piece.at[kind], held.at[kind, spot]))
-        for load in loads[0]:
-            load.wait()
-        width = base.shape[1]
-        wide = base[...].astype(f32)
-        scale = row_scale(row_sum(wide * wide), width)
-        for load in loads[1]:
-            load.wait()
-        active = gelu_value(nn_dot(base[...], held[0]) * scale).astype(bf16)
-        for load in loads[2]:
-            load.wait()
-        top[...] = (base[...].astype(f32) + nt_dot(active, held[1])).astype(bf16)
-        copies.start(top, out).wait()
-
-    @pl.when(place[2] != step)
-    def _():
-        copies.start(before, base).wait()
-        copies.start(base, out).wait()
+def block_forward(states, w_down, w_up):
+    wide = states.astype(f32)
+    scale = row_scale(row_sum(wide * wide), states.shape[-1])
+    hidden = jnp.einsum("nd,dr->nr", states, w_down, preferred_element_type=f32) * scale
+    update = jnp.einsum("nr,dr->nd", gelu_value(hidden).astype(bf16), w_up, preferred_element_type=f32)
+    return (wide + update).astype(bf16)
 
 
 def fisher_kernel(tasks, halves, place, *refs):
     del place
     count = tasks * halves
     wides, narrows = refs[:count], refs[count:2 * count]
-    weights, outs = refs[2 * count:-2], refs[-2:]
+    weights, outs = refs[2 * count:-4], refs[-4:]
     for kind in range(2):
         top, total = None, None
         for task in range(tasks):
@@ -374,8 +350,8 @@
             scaled = term * weights[task * 2 + kind][...].astype(f32)
             top = scaled if top is None else top + scaled
             total = term if total is None else total + term
-        outs[0][kind] = top.astype(bf16)
-        outs[1][kind] = total.astype(bf16)
+        outs[kind][...] = top.astype(bf16)
+        outs[2 + kind][...] = total.astype(bf16)
 
 
 def block_size(width):
@@ -416,8 +392,8 @@
 
 def ring_scatter(own, other, spot, axis):
     count, ahead, back = ring_routes(axis)
-    rows = own[0].shape[1] // count
-    streams = [(index, kind) for kind in range(own[0].shape[0]) for index in range(2)]
+    rows = own[0][0].shape[0] // count
+    streams = [(index, kind) for kind in range(2) for index in range(2)]
 
     def part(index, kind, step):
         offset = -1 - step if index == 0 else 1 + step
@@ -432,22 +408,28 @@
             landed = send(moving[stream], axis, back if stream[0] else ahead)
             total = landed.astype(f32) + part(*stream, step)
             moving[stream] = total if step == count - 1 else total.astype(bf16)
-    return [jnp.stack([moving[index, kind] for kind in range(own[0].shape[0])]) for index in range(2)]
-
-
-def ring_gather(own, axis):
+    return [jnp.stack([moving[index, kind] for kind in range(2)]) for index in range(2)]
+
+
+def ring_gather(own, spot, axis):
     count, ahead, back = ring_routes(axis)
-    pieces, offsets = [own], [0]
+    kinds, rows, rank = own.shape
+
+    def put(whole, piece, offset):
+        return lax.dynamic_update_slice(whole, piece, (0, block_at(spot, offset, count) * rows, 0))
+
+    whole = put(jnp.zeros((kinds, count * rows, rank), own.dtype), own, 0)
     down = up = own
+    placed = 1
     for step in range(1, count // 2 + 1):
         down = send(down, axis, ahead)
-        pieces.append(down)
-        offsets.append(-step)
-        if len(pieces) < count:
+        whole = put(whole, down, -step)
+        placed += 1
+        if placed < count:
             up = send(up, axis, back)
-            pieces.append(up)
-            offsets.append(step)
-    return pieces, offsets
+            whole = put(whole, up, step)
+            placed += 1
+    return whole
 
 
 def after(value, done):
@@ -463,8 +445,13 @@
     tasks = all_tasks // 2
     micro, rows, _ = entry_states.shape
     label_count = label_rows.shape[0]
-    halves = 2
-    chunks, part = tasks * halves, micro * rows // halves
+    total_rows, halves = micro * rows, 2
+    chunks = tasks * halves
+    small = max(total_rows * 2 // 5 // 16 * 16, 16)
+    parts = []
+    for task in range(tasks):
+        sizes = (small, total_rows - small) if task == 0 else (total_rows - small, small)
+        parts += [(0, sizes[0]), (sizes[0], sizes[1])]
     spot = spot_of(lax.axis_index("dp"), lax.axis_size("dp"))
     place = jnp.stack([stage, member, section, spot]).astype(jnp.int32)
     sections = range(section_count)
@@ -487,21 +474,28 @@
         pltpu.SemaphoreType.DMA((2, 2)),
     ]
     params = pltpu.CompilerParams(vmem_limit_bytes=vmem_bytes)
-    state_shape, hidden_shape = (part, width), (2, part, rank)
-    wide_shape, narrow_shape = (2, 2, part, width), (2, 2, part, rank)
-    state_type = jax.ShapeDtypeStruct(state_shape, bf16)
-    square_types = (jax.ShapeDtypeStruct(wide_shape, bf16), jax.ShapeDtypeStruct(narrow_shape, bf16))
-    square_scratch = [
-        pltpu.VMEM(wide_shape, bf16),
-        pltpu.VMEM(narrow_shape, bf16),
-        pltpu.SemaphoreType.DMA((2, 2, 2)),
-    ]
-    layer_flops = 4 * part * width * rank
+
+    class Chunk:
+        def __init__(self, turn):
+            self.start, part = parts[turn]
+            self.part, self.lanes = part, 128 * ((part + 127) // 128)
+            state, hidden, scale = (part, width), (2, part, rank), (2, part, 128)
+            wide, narrow = (2, 2, part, width), (2, 2, part, rank)
+            self.state, self.wide, self.narrow = (jax.ShapeDtypeStruct(shape, bf16) for shape in (state, wide, narrow))
+            self.hidden, self.scale = (jax.ShapeDtypeStruct(shape, f32) for shape in (hidden, scale))
+            self.levels = pltpu.VMEM((3,) + state, bf16)
+            self.pre, self.scales = pltpu.VMEM(hidden, f32), pltpu.VMEM(scale, f32)
+            self.squares = (self.wide, self.narrow)
+            self.square_scratch = [
+                pltpu.VMEM(wide, bf16), pltpu.VMEM(narrow, bf16), pltpu.SemaphoreType.DMA((2, 2, 2))
+            ]
+            self.flops = 4 * part * width * rank
+
     weight_bytes = 8 * width * rank
 
     def stage_call(kernel, turn, name, operands, outputs, scratch, flops, hbm_in=(), hbm_out=(), **more):
         return pl.pallas_call(
-            functools.partial(kernel, turn // halves, turn % halves),
+            functools.partial(kernel, turn // halves, parts[turn][0]),
             out_shape=outputs,
             in_specs=[smem] + [hbm if index in hbm_in else anywhere for index in range(1, operands + 1)],
             out_specs=tuple(hbm if index in hbm_out else anywhere for index in range(len(outputs))),
@@ -513,24 +507,20 @@
         )
 
     own_labels = lax.dynamic_slice_in_dim(sampled_labels, member * tasks, tasks, 0)
-    label_columns = own_labels.reshape(tasks, halves, part, 1)
-    entry = entry_states.reshape(micro * rows, width)
+    label_columns = own_labels.reshape(tasks, total_rows, 1)
+    entry = entry_states.reshape(total_rows, width)
     saved, crossing, returned, picked = {}, {}, {}, {}
     squares = {}
     token = place
 
-    levels, pre = pltpu.VMEM((3,) + state_shape, bf16), pltpu.VMEM(hidden_shape, f32)
-    scale_shape = (2, part, 128)
-    lanes = 128 * ((part + 127) // 128)
-    scales, scale_type = pltpu.VMEM(scale_shape, f32), jax.ShapeDtypeStruct(scale_shape, f32)
-
     def first_forward(turn):
         nonlocal token
+        chunk = Chunk(turn)
         call = stage_call(
             first_forward_kernel, turn, "first_forward", 5,
-            (state_type, state_type, jax.ShapeDtypeStruct(hidden_shape, f32), scale_type),
-            [levels, pre, scales, pltpu.SemaphoreType.DMA((4,))],
-            2 * layer_flops, hbm_in=(1, 2, 3, 4, 5), hbm_out=(1, 2, 3),
+            (chunk.state, chunk.state, chunk.hidden, chunk.scale),
+            [chunk.levels, chunk.pre, chunk.scales, pltpu.SemaphoreType.DMA((4,))],
+            2 * chunk.flops, hbm_in=(1, 2, 3, 4, 5), hbm_out=(1, 2, 3),
         )
         out, middle, hidden, scale = call(token, entry, *weights(turn))
         saved[turn] = (entry, middle, hidden, scale)
@@ -544,15 +534,16 @@
 
     def last_stage(turn):
         nonlocal token
+        chunk = Chunk(turn)
         call = stage_call(
             last_stage_kernel, turn, "last_stage", 7,
-            (state_type, jax.ShapeDtypeStruct((8, lanes), f32)) + square_types,
+            (chunk.state, jax.ShapeDtypeStruct((8, chunk.lanes), f32)) + chunk.squares,
             [
-                levels, pltpu.VMEM(label_rows.shape, bf16),
-                pltpu.VMEM((part, 1), jnp.int32), pltpu.VMEM((8, lanes), f32),
-                pre, scales, levels,
-            ] + square_scratch + [pltpu.SemaphoreType.DMA((5,))],
-            4 * layer_flops + 4 * part * width * label_count,
+                chunk.levels, pltpu.VMEM(label_rows.shape, bf16),
+                pltpu.VMEM((chunk.part, 1), jnp.int32), pltpu.VMEM((8, chunk.lanes), f32),
+                chunk.pre, chunk.scales, chunk.levels,
+            ] + chunk.square_scratch + [pltpu.SemaphoreType.DMA((5,))],
+            4 * chunk.flops + 4 * chunk.part * width * label_count,
             hbm_in=(3, 4, 5, 6, 7), hbm_out=(2, 3),
         )
         grad, picked[turn], *squares[turn] = call(
@@ -563,10 +554,11 @@
 
     def first_backward(turn):
         nonlocal token
+        chunk = Chunk(turn)
         call = stage_call(
-            first_backward_kernel, turn, "first_backward", 11, square_types,
-            [levels, levels, pre, scales] + square_scratch + [pltpu.SemaphoreType.DMA((5,))],
-            2 * layer_flops,
+            first_backward_kernel, turn, "first_backward", 11, chunk.squares,
+            [chunk.levels, chunk.levels, chunk.pre, chunk.scales] + chunk.square_scratch + [pltpu.SemaphoreType.DMA((5,))],
+            2 * chunk.flops,
             hbm_in=range(2, 12), hbm_out=(0, 1),
             input_output_aliases={6: 0, 7: 1},
         )
@@ -583,39 +575,43 @@
             return pl.BlockSpec((pl.squeezed, block, rank), lambda i, s: (s[1] * tasks + task, i, 0))
 
         pairs = [squares[turn] for turn in range(chunks)]
-        sum_spec = pl.BlockSpec((2, block, rank), lambda i, s: (0, i, 0))
         other_spec = pl.BlockSpec((block, rank), lambda i, s: (i, 0))
         call = pl.pallas_call(
             functools.partial(fisher_kernel, tasks, halves),
-            out_shape=(jax.ShapeDtypeStruct((2, width, rank), bf16),) * 2,
+            out_shape=(jax.ShapeDtypeStruct((width, rank), bf16),) * 4,
             grid_spec=pltpu.PrefetchScalarGridSpec(
                 num_scalar_prefetch=1,
                 grid=(width // block,),
-                in_specs=[pl.BlockSpec((1, 2, part, block), lambda i, s: (layer_of(s), 0, 0, i))] * chunks
-                + [pl.BlockSpec((1, 2, part, rank), lambda i, s: (layer_of(s), 0, 0, 0))] * chunks
+                in_specs=[pl.BlockSpec((1, 2, part, block), lambda i, s: (layer_of(s), 0, 0, i)) for _, part in parts]
+                + [pl.BlockSpec((1, 2, part, rank), lambda i, s: (layer_of(s), 0, 0, 0)) for _, part in parts]
                 + [other_spec if away else own_spec(task) for task in range(tasks) for _ in range(2)],
-                out_specs=(sum_spec,) * 2,
+                out_specs=(other_spec,) * 4,
             ),
             compiler_params=params,
             cost_estimate=pl.CostEstimate(
-                flops=4 * chunks * part * width * rank,
-                bytes_accessed=8 * chunks * part * width,
+                flops=4 * tasks * total_rows * width * rank,
+                bytes_accessed=8 * tasks * total_rows * width,
                 transcendentals=0,
             ),
             name="fisher_away" if away else "fisher_own",
         )
         matrices = sum(others, []) if away else [w_down, w_up] * tasks
-        return call(token, *[wide for wide, _ in pairs], *[narrow for _, narrow in pairs], *matrices)
+        made = call(token, *[wide for wide, _ in pairs], *[narrow for _, narrow in pairs], *matrices)
+        return [made[:2], made[2:]]
 
     for turn in range(chunks):
+        if turn == 2:
+            token = after(token, crossing[0])
         first_forward(turn)
+        if turn == 0:
+            token = after(token, others)
         cross(turn)
     for turn in range(chunks):
         if turn >= 2:
             first_backward(turn - 2)
         last_stage(turn)
     first_backward(chunks - 2)
-    values = jnp.stack([picked[turn][0, :part] for turn in range(chunks)]).reshape(tasks, micro, rows)
+    values = jnp.concatenate([picked[turn][0, :parts[turn][1]] for turn in range(chunks)]).reshape(tasks, micro, rows)
     values = after(values, token)
     label_logprob = jnp.zeros((micro, rows), f32)
     for index in range(tasks):
@@ -625,34 +621,21 @@
     token = after(token, label_logprob)
     first_backward(chunks - 1)
     away_sums = fisher(True)
-    other_sums = lax.optimization_barrier([send(value, "section", swap) for value in away_sums])
-    token = after(place, away_sums[0])
+    other_sums = lax.optimization_barrier([[send(value, "section", swap) for value in pair] for pair in away_sums])
+    token = after(place, away_sums[0][0])
     sums = fisher(False)
     shares = ring_scatter(sums, other_sums, spot, "dp")
     numerator, denominator = shares
     merged_part = (numerator / (denominator + merge_eps)).astype(bf16)
-    pieces, offsets = ring_gather(merged_part, "dp")
+    merged = ring_gather(merged_part, spot, "dp")
     fisher_log = jnp.log(denominator + merge_eps)
 
     current, result = eval_states, eval_states
     for step in range(section_count):
-        result = pl.pallas_call(
-            functools.partial(eval_kernel, step, offsets),
-            out_shape=jax.ShapeDtypeStruct(eval_states.shape, bf16),
-            in_specs=[smem] + [anywhere] * (2 + len(pieces)),
-            out_specs=anywhere,
-            scratch_shapes=[
-                pltpu.VMEM(eval_states.shape, bf16), pltpu.VMEM(eval_states.shape, bf16),
-                pltpu.VMEM((2, width, rank), bf16), pltpu.SemaphoreType.DMA((4 + 2 * len(pieces),)),
-            ],
-            compiler_params=pltpu.CompilerParams(vmem_limit_bytes=vmem_bytes // 4),
-            cost_estimate=pl.CostEstimate(
-                flops=4 * eval_states.size * rank, bytes_accessed=4 * width * rank, transcendentals=0
-            ),
-            name="eval_block",
-        )(place, current, result, *pieces)
+        output = block_forward(current, merged[0], merged[1])
+        result = jnp.where(section == step, output, result)
         if step + 1 < section_count:
-            current = send(result, "section", [(step, step + 1)])
+            current = send(output, "section", [(step, step + 1)])
     return (result[None], label_logprob[None], fisher_log[None])
 
 

time: 272 us -> 263 us (0.967)
  waiting for transfers between devices: 111 us -> 85.5 us
  other arithmetic: 3.57 us -> 16.8 us
  starting transfers between devices: 50.5 us -> 60.4 us
  Pallas kernels: 81.4 us -> 72.9 us
  matrix products: 0 us -> 7.18 us
  local copies, waits for them, and re-layouts: 23.2 us -> 17.2 us
    ppermute x54 -> x56, waiting for transfers between devices: 111 us -> 85.5 us  [send(): return lax.ppermute(block, axis, route)]
    ppermute x54 -> x56, starting transfers between devices: 50.5 us -> 60.4 us  [send(): return lax.ppermute(block, axis, route)]
    pallas_call x4 -> x0, Pallas kernels: 8.29 us -> none  [local(): pl.pallas_call(functools.partial(eval_kernel, step, offsets), out_shape=j...]
    slice x6 -> x0, local copies, waits for them, and re-layouts: 7.59 us -> none  [the longest x2 4.88 us: part(): array[index][kind]]
    dot_general x0 -> x4, matrix products: none -> 7.18 us  [block_forward(): jnp.einsum('nr,dr->nd', gelu_value(hidden).astype(bf16), w_up, preferred_...]
    convert_element_type x24, other arithmetic: 1.52 us -> 7.04 us  [ring_scatter(): moving[stream] = total if step == count - 1 else total.astype(bf16)]
    convert_element_type x4, other arithmetic: 0.17 us -> 4.28 us  [ring_scatter(): moving = {stream: part(*stream, 0).astype(bf16) for stream in streams}]
    unnamed x37 -> x45, local copies, waits for them, and re-layouts: 9.75 us -> 7.97 us
  transfers between devices with their start and end apart: 54 -> 56, of which waited for: 29 -> 28; matrix products, arithmetic and copies ran while one was open for 4% -> 7% of each run, Pallas kernels for 23% -> 24%
where the time goes in v3:
time: 263 us; the launch traced here: 261 us
  waiting for transfers between devices  85.5 us (33%)
  Pallas kernels  72.9 us (28%)
  starting transfers between devices  60.4 us (23%)
  local copies, waits for them, and re-layouts  17.2 us (7%)
  other arithmetic  16.8 us (6%)
  matrix products  7.18 us (3%)
    ppermute x56, waiting for transfers between devices, send(): return lax.ppermute(block, axis, route)  85.5 us
    ppermute x56, starting transfers between devices, send(): return lax.ppermute(block, axis, route)  60.4 us
    pallas_call x4, Pallas kernels, last_stage(): call(token, crossing[turn], label_columns, label_rows, *weights(turn))  48.9 us
    pallas_call x2, Pallas kernels, fisher(): call(token, *[wide for wide, _ in pairs], *[narrow for _, narrow in pairs...  17.6 us
    unnamed x45, local copies, waits for them, and re-layouts  7.97 us
    dot_general x4, matrix products, block_forward(): jnp.einsum('nr,dr->nd', gelu_value(hidden).astype(bf16), w_up, preferred_...  7.18 us
    convert_element_type x24, other arithmetic, ring_scatter(): moving[stream] = total if step == count - 1 else total.astype(bf16)  7.04 us
  transfers between devices with their start and end apart: 56, of which 28 were waited for; matrix products, arithmetic and copies ran while one was open for 7% of the time, Pallas kernels for 24%

profile of v3, /device:TPU:23, one launch (start us, length us, event | category | flops | bytes accessed | tf_op | source)
XLA Modules:
  0.0 261.3 jit_solution(4768542441590247695)
XLA Ops:
  0.7 3.4 %dynamic-slice_bitcast_fusion.1 = (bf16[4608,128]{1,0:T(8,128)(2,1)}, bf16[4608,128]{1,0:T(8,128)(2,1)}) fusion(bf16[1,4,4608,128]{3,2,1,0:T(8,128)(2,1)} %param.7, s32[]{:T(128)S(6)} %select_n.255, s32[]{:T(128)S(6)} %select_n.254), kind=kLoop, calls=%fused_computation.13 | loop fusion | bytes 4718600 | tf_op jit(solution)/shard_map/jit(dynamic_index_in_dim)/squeeze | solution.py:464
  4.7 1.6 dynamic-slice_bitcast_fusion
  7.5 1.8 collective-permute-done.1.up_other.refs_9_
  9.4 1.1 copy-done.4
  11.2 1.6 collective-permute-done.2.down_other.refs_10_
  12.9 1.3 collective-permute-start.4
  14.9 1.3 collective-permute-start.5
  16.2 16.7 %collective-permute-done.4.states = bf16[64,4608]{1,0:T(8,128)(2,1)S(1)} collective-permute-done((bf16[64,4608]{1,0:T(8,128)(2,1)}, bf16[64,4608]{1,0:T(8,128)(2,1)S(1)}, u32[]{:S(2)}, u32[]{:S(2)}) %collective-permute-start.4) | collective-permute-done | bytes 589856 | tf_op jit(solution)/shard_map/ppermute | solution.py:367
  33.8 1.3 collective-permute-start.7
  36.7 11.4 %last_stage.4 = (bf16[64,4608]{1,0:T(8,128)(2,1)}, f32[8,128]{1,0:T(8,128)}, bf16[2,2,64,4608]{3,2,1,0:T(8,128)(2,1)}, bf16[2,2,64,128]{3,2,1,0:T(8,128)(2,1)}) custom-call(s32[4]{0:T(128)} %pad_add_fusion.place, bf16[64,4608]{1,0:T(8,128)(2,1)} %copy-done.18, s32[2,160,1]{2,1,0:T(8,128)} %reshape.92.labels, bf16[256,4608]{1,0:T(8,128)(2,1)} %label_rows.7, ...), custom_call_target="tpu_custom_call" | custom-call | flops 905969664 | bytes 4718592 | tf_op jit(solution)/shard_map/last_stage/pallas_call | solution.py:549
  48.1 3.7 %collective-permute-start.6 = (bf16[64,4608]{1,0:T(8,128)(2,1)}, bf16[64,4608]{1,0:T(8,128)(2,1)S(1)}, u32[]{:S(2)}, u32[]{:S(2)}) collective-permute-start(bf16[64,4608]{1,0:T(8,128)(2,1)} %get-tuple-element.94), channel_id=1, source_target_pairs={{16,0},{24,8},{17,1},{25,9},{18,2},{26,10},{19,3},{27,11},{20,4},{... | collective-permute-start | bytes 1769480 | tf_op jit(solution)/shard_map/ppermute | solution.py:367
  51.9 1.0 copy-done.15
  52.9 12.4 %last_stage.5 = (bf16[96,4608]{1,0:T(8,128)(2,1)}, f32[8,128]{1,0:T(8,128)}, bf16[2,2,96,4608]{3,2,1,0:T(8,128)(2,1)}, bf16[2,2,96,128]{3,2,1,0:T(8,128)(2,1)}) custom-call(s32[4]{0:T(128)} %pad_add_fusion.place, bf16[96,4608]{1,0:T(8,128)(2,1)} %copy-done.15, s32[2,160,1]{2,1,0:T(8,128)} %reshape.92.labels, bf16[256,4608]{1,0:T(8,128)(2,1)} %label_rows.7, ...), custom_call_target="tpu_custom_call" | custom-call | flops 1358954496 | bytes 4718592 | tf_op jit(solution)/shard_map/last_stage/pallas_call | solution.py:549
  65.3 1.3 collective-permute-start.8
  66.7 1.3 collective-permute-start.9
  71.7 13.1 %last_stage.6 = (bf16[96,4608]{1,0:T(8,128)(2,1)}, f32[8,128]{1,0:T(8,128)}, bf16[2,2,96,4608]{3,2,1,0:T(8,128)(2,1)}, bf16[2,2,96,128]{3,2,1,0:T(8,128)(2,1)}) custom-call(s32[4]{0:T(128)} %pad_add_fusion.place, bf16[96,4608]{1,0:T(8,128)(2,1)} %copy-done.12, s32[2,160,1]{2,1,0:T(8,128)} %reshape.92.labels, bf16[256,4608]{1,0:T(8,128)(2,1)} %label_rows.7, ...), custom_call_target="tpu_custom_call" | custom-call | flops 1358954496 | bytes 4718592 | tf_op jit(solution)/shard_map/last_stage/pallas_call | solution.py:549
  84.8 1.3 collective-permute-start.10
  90.1 12.0 %last_stage.7 = (bf16[64,4608]{1,0:T(8,128)(2,1)}, f32[8,128]{1,0:T(8,128)}, bf16[2,2,64,4608]{3,2,1,0:T(8,128)(2,1)}, bf16[2,2,64,128]{3,2,1,0:T(8,128)(2,1)}) custom-call(s32[4]{0:T(128)} %pad_add_fusion.place, bf16[64,4608]{1,0:T(8,128)(2,1)} %copy-done.17, s32[2,160,1]{2,1,0:T(8,128)} %reshape.92.labels, bf16[256,4608]{1,0:T(8,128)(2,1)} %label_rows.7, ...), custom_call_target="tpu_custom_call" | custom-call | flops 905969664 | bytes 4718592 | tf_op jit(solution)/shard_map/last_stage/pallas_call | solution.py:549
  102.2 1.3 collective-permute-start.13
  104.4 1.3 collective-permute-done.10.grad
  108.1 12.0 %collective-permute-start.12 = (f32[5,32]{1,0:T(8,128)S(1)}, f32[5,32]{1,0:T(8,128)S(1)}, u32[]{:S(2)}, u32[]{:S(2)}) collective-permute-start(f32[5,32]{1,0:T(8,128)S(1)} %get-tuple-element.162), channel_id=1, source_target_pairs={{16,0},{24,16},{17,1},{25,17},{18,2},{26,18},{19,3},{27,19},{20,4}... | collective-permute-start | bytes 1928 | tf_op jit(solution)/shard_map/ppermute | solution.py:367
  121.7 1.0 first_backward.7
  122.7 8.8 %fisher_away.1 = (bf16[4608,128]{1,0:T(8,128)(2,1)}, bf16[4608,128]{1,0:T(8,128)(2,1)}, bf16[4608,128]{1,0:T(8,128)(2,1)}, bf16[4608,128]{1,0:T(8,128)(2,1)}) custom-call(s32[4]{0:T(128)} %pad_add_fusion.place, bf16[2,2,64,4608]{3,2,1,0:T(8,128)(2,1)} %get-tuple-element.132.refs_0_, bf16[2,2,96,4608]{3,2,1,0:T(8,128)(2,1)} %get-tuple-element.133.refs_1_, ...), custom_call_target="tpu_custom_call" | custom-call | flops 754974720 | bytes 11796480 | tf_op jit(solution)/shard_map/fisher_away/pallas_call | solution.py:599
  132.7 8.8 %fisher_own.1 = (bf16[4608,128]{1,0:T(8,128)(2,1)}, bf16[4608,128]{1,0:T(8,128)(2,1)}, bf16[4608,128]{1,0:T(8,128)(2,1)}, bf16[4608,128]{1,0:T(8,128)(2,1)}) custom-call(s32[4]{0:T(128)} %pad_add_fusion.place, bf16[2,2,64,4608]{3,2,1,0:T(8,128)(2,1)} %get-tuple-element.132.refs_0_, bf16[2,2,96,4608]{3,2,1,0:T(8,128)(2,1)} %get-tuple-element.133.refs_1_, ...), custom_call_target="tpu_custom_call" | custom-call | flops 754974720 | bytes 11796480 | tf_op jit(solution)/shard_map/fisher_own/pallas_call | solution.py:599
  141.5 1.4 add_convert_fusion.13
  142.9 1.4 collective-permute-start.32
  145.5 1.0 add_convert_fusion.27
  146.5 1.3 collective-permute-start.18
  149.1 1.2 collective-permute-start.33
  151.2 1.2 collective-permute-start.40
  152.4 1.0 add_convert_fusion.26
  157.2 1.0 collective-permute-start.41
  158.3 1.0 add_convert_fusion.25
  160.4 1.5 collective-permute-start.35
  162.5 1.4 collective-permute-start.42
  164.1 1.0 add_convert_fusion.24
  166.6 1.3 collective-permute-start.36
  168.4 1.7 collective-permute-start.43
  170.4 1.0 add_convert_fusion.23
  172.8 1.0 collective-permute-start.37
  174.5 1.4 collective-permute-start.44
  175.9 1.4 collective-permute-done.22
  177.3 1.0 add_convert_fusion.22
  179.6 1.0 collective-permute-start.38
  180.9 1.2 collective-permute-start.45
  182.1 2.1 collective-permute-done.23
  184.1 1.0 add_convert_fusion.21
  186.5 1.7 collective-permute-done.45
  188.2 2.8 %collective-permute-done.24 = bf16[576,128]{1,0:T(8,128)(2,1)S(1)} collective-permute-done((bf16[576,128]{1,0:T(8,128)(2,1)S(1)}, bf16[576,128]{1,0:T(8,128)(2,1)S(1)}, u32[]{:S(2)}, u32[]{:S(2)}) %collective-permute-start.24) | collective-permute-done | bytes 147488 | tf_op jit(solution)/shard_map/ppermute | solution.py:367
  191.0 1.0 add_bitcast_fusion.1
  192.6 1.0 add_bitcast_fusion
  195.6 4.1 %collective-permute-done.46 = bf16[2,576,128]{2,1,0:T(8,128)(2,1)S(1)} collective-permute-done((bf16[2,576,128]{2,1,0:T(8,128)(2,1)S(1)}, bf16[2,576,128]{2,1,0:T(8,128)(2,1)S(1)}, u32[]{:S(2)}, u32[]{:S(2)}) %collective-permute-start.46) | collective-permute-done | bytes 294944 | tf_op jit(solution)/shard_map/ppermute | solution.py:367
  200.5 1.0 collective-permute-start.49
  201.5 6.8 %collective-permute-done.48 = bf16[2,576,128]{2,1,0:T(8,128)(2,1)S(1)} collective-permute-done((bf16[2,576,128]{2,1,0:T(8,128)(2,1)S(1)}, bf16[2,576,128]{2,1,0:T(8,128)(2,1)S(1)}, u32[]{:S(2)}, u32[]{:S(2)}) %collective-permute-start.48) | collective-permute-done | bytes 294944 | tf_op jit(solution)/shard_map/ppermute | solution.py:367
  208.8 1.1 collective-permute-start.51
  209.9 7.0 %collective-permute-done.50 = bf16[2,576,128]{2,1,0:T(8,128)(2,1)S(1)} collective-permute-done((bf16[2,576,128]{2,1,0:T(8,128)(2,1)S(1)}, bf16[2,576,128]{2,1,0:T(8,128)(2,1)S(1)}, u32[]{:S(2)}, u32[]{:S(2)}) %collective-permute-start.50) | collective-permute-done | bytes 294944 | tf_op jit(solution)/shard_map/ppermute | solution.py:367
  217.6 7.2 %collective-permute-done.52 = bf16[2,576,128]{2,1,0:T(8,128)(2,1)S(1)} collective-permute-done((bf16[2,576,128]{2,1,0:T(8,128)(2,1)S(1)}, bf16[2,576,128]{2,1,0:T(8,128)(2,1)S(1)}, u32[]{:S(2)}, u32[]{:S(2)}) %collective-permute-start.52) | collective-permute-done | bytes 294944 | tf_op jit(solution)/shard_map/ppermute | solution.py:367
  224.8 1.5 fusion
  227.2 1.5 fusion.1
  229.6 1.5 fusion.2
  231.1 1.4 collective-permute-start.55
  234.1 23.5 %collective-permute-done.55 = bf16[32,4608]{1,0:T(8,128)(2,1)} collective-permute-done((bf16[32,4608]{1,0:T(8,128)(2,1)}, bf16[32,4608]{1,0:T(8,128)(2,1)}, u32[]{:S(2)}, u32[]{:S(2)}) %collective-permute-start.55) | collective-permute-done | bytes 294944 | tf_op jit(solution)/shard_map/ppermute | solution.py:367
  257.5 1.1 fusion.10
  258.7 2.6 fusion.5
  (175 shorter events, 44.1 us)
Async XLA Ops:
  0.6 34.5 %copy-start = (s32[4,5,32]{2,0,1:T(4,128)S(1)}, s32[4,5,32]{2,0,1:T(4,128)}, u32[]{:S(2)}) copy-start(s32[4,5,32]{2,0,1:T(4,128)} %param.10) | copy-start | bytes 7684
  4.1 3.5 %collective-permute-start = (bf16[4608,128]{1,0:T(8,128)(2,1)}, bf16[4608,128]{1,0:T(8,128)(2,1)S(1)}, u32[]{:S(2)}, u32[]{:S(2)}) collective-permute-start(bf16[4608,128]{1,0:T(8,128)(2,1)} %get-tuple-element.157), channel_id=1, source_target_pairs={{0,8},{8,0},{16,24},{24,16},{1,9},{9,1},{17,25},{25,17},{2,10},{10... | collective-permute-start | bytes 3538952 | tf_op jit(solution)/shard_map/ppermute | solution.py:367
  6.3 3.1 %collective-permute-start.1 = (bf16[4608,128]{1,0:T(8,128)(2,1)}, bf16[4608,128]{1,0:T(8,128)(2,1)S(1)}, u32[]{:S(2)}, u32[]{:S(2)}) collective-permute-start(bf16[4608,128]{1,0:T(8,128)(2,1)} %get-tuple-element.155), channel_id=1, source_target_pairs={{0,8},{8,0},{16,24},{24,16},{1,9},{9,1},{17,25},{25,17},{2,10},{10... | collective-permute-start | bytes 3538952 | tf_op jit(solution)/shard_map/ppermute | solution.py:367
  6.4 6.3 %collective-permute-start.2 = (bf16[4608,128]{1,0:T(8,128)(2,1)}, bf16[4608,128]{1,0:T(8,128)(2,1)S(1)}, u32[]{:S(2)}, u32[]{:S(2)}) collective-permute-start(bf16[4608,128]{1,0:T(8,128)(2,1)} %get-tuple-element.156), channel_id=1, source_target_pairs={{0,8},{8,0},{16,24},{24,16},{1,9},{9,1},{17,25},{25,17},{2,10},{10... | collective-permute-start | bytes 3538952 | tf_op jit(solution)/shard_map/ppermute | solution.py:367
  6.8 6.1 %collective-permute-start.3 = (bf16[4608,128]{1,0:T(8,128)(2,1)}, bf16[4608,128]{1,0:T(8,128)(2,1)}, u32[]{:S(2)}, u32[]{:S(2)}) collective-permute-start(bf16[4608,128]{1,0:T(8,128)(2,1)} %get-tuple-element.154), channel_id=1, source_target_pairs={{0,8},{8,0},{16,24},{24,16},{1,9},{9,1},{17,25},{25,17},{2,10},{10... | collective-permute-start | bytes 3538952 | tf_op jit(solution)/shard_map/ppermute | solution.py:367
  12.9 20.1 %collective-permute-start.4 = (bf16[64,4608]{1,0:T(8,128)(2,1)}, bf16[64,4608]{1,0:T(8,128)(2,1)S(1)}, u32[]{:S(2)}, u32[]{:S(2)}) collective-permute-start(bf16[64,4608]{1,0:T(8,128)(2,1)} %get-tuple-element.82), channel_id=1, source_target_pairs={{0,16},{8,24},{1,17},{9,25},{2,18},{10,26},{3,19},{11,27},{4,20},{... | collective-permute-start | bytes 1769480 | tf_op jit(solution)/shard_map/ppermute | solution.py:367
  14.9 37.0 %collective-permute-start.5 = (bf16[96,4608]{1,0:T(8,128)(2,1)}, bf16[96,4608]{1,0:T(8,128)(2,1)S(1)}, u32[]{:S(2)}, u32[]{:S(2)}) collective-permute-start(bf16[96,4608]{1,0:T(8,128)(2,1)} %get-tuple-element.91), channel_id=1, source_target_pairs={{0,16},{8,24},{1,17},{9,25},{2,18},{10,26},{3,19},{11,27},{4,20},{... | collective-permute-start | bytes 2654216 | tf_op jit(solution)/shard_map/ppermute | solution.py:367
  33.8 37.0 %collective-permute-start.7 = (bf16[96,4608]{1,0:T(8,128)(2,1)}, bf16[96,4608]{1,0:T(8,128)(2,1)S(1)}, u32[]{:S(2)}, u32[]{:S(2)}) collective-permute-start(bf16[96,4608]{1,0:T(8,128)(2,1)} %get-tuple-element.102), channel_id=1, source_target_pairs={{0,16},{8,24},{1,17},{9,25},{2,18},{10,26},{3,19},{11,27},{4,20},{... | collective-permute-start | bytes 2654216 | tf_op jit(solution)/shard_map/ppermute | solution.py:367
  48.1 20.6 %collective-permute-start.6 = (bf16[64,4608]{1,0:T(8,128)(2,1)}, bf16[64,4608]{1,0:T(8,128)(2,1)S(1)}, u32[]{:S(2)}, u32[]{:S(2)}) collective-permute-start(bf16[64,4608]{1,0:T(8,128)(2,1)} %get-tuple-element.94), channel_id=1, source_target_pairs={{16,0},{24,8},{17,1},{25,9},{18,2},{26,10},{19,3},{27,11},{20,4},{... | collective-permute-start | bytes 1769480 | tf_op jit(solution)/shard_map/ppermute | solution.py:367
  51.8 14.9 %copy-start.21 = (bf16[64,4608]{1,0:T(8,128)(2,1)S(1)}, bf16[64,4608]{1,0:T(8,128)(2,1)}, u32[]{:S(2)}) copy-start(bf16[64,4608]{1,0:T(8,128)(2,1)} %get-tuple-element.113) | copy-start | bytes 1769476
  65.3 22.2 %collective-permute-start.8 = (bf16[96,4608]{1,0:T(8,128)(2,1)}, bf16[96,4608]{1,0:T(8,128)(2,1)S(1)}, u32[]{:S(2)}, u32[]{:S(2)}) collective-permute-start(bf16[96,4608]{1,0:T(8,128)(2,1)} %get-tuple-element.105), channel_id=1, source_target_pairs={{16,0},{24,8},{17,1},{25,9},{18,2},{26,10},{19,3},{27,11},{20,4},{... | collective-permute-start | bytes 2654216 | tf_op jit(solution)/shard_map/ppermute | solution.py:367
  66.7 22.7 %collective-permute-start.9 = (bf16[64,4608]{1,0:T(8,128)(2,1)S(1)}, bf16[64,4608]{1,0:T(8,128)(2,1)S(1)}, u32[]{:S(2)}, u32[]{:S(2)}) collective-permute-start(bf16[64,4608]{1,0:T(8,128)(2,1)S(1)} %copy-done.21), channel_id=1, source_target_pairs={{0,16},{8,24},{1,17},{9,25},{2,18},{10,26},{3,19},{11,27},{4,20},{... | collective-permute-start | bytes 1769480 | tf_op jit(solution)/shard_map/ppermute | solution.py:367
  84.8 20.8 %collective-permute-start.10 = (bf16[96,4608]{1,0:T(8,128)(2,1)}, bf16[96,4608]{1,0:T(8,128)(2,1)S(1)}, u32[]{:S(2)}, u32[]{:S(2)}) collective-permute-start(bf16[96,4608]{1,0:T(8,128)(2,1)} %get-tuple-element.116), channel_id=1, source_target_pairs={{16,0},{24,8},{17,1},{25,9},{18,2},{26,10},{19,3},{27,11},{20,4},{... | collective-permute-start | bytes 2654216 | tf_op jit(solution)/shard_map/ppermute | solution.py:367
  102.2 18.7 %collective-permute-start.13 = (bf16[64,4608]{1,0:T(8,128)(2,1)}, bf16[64,4608]{1,0:T(8,128)(2,1)S(1)}, u32[]{:S(2)}, u32[]{:S(2)}) collective-permute-start(bf16[64,4608]{1,0:T(8,128)(2,1)} %get-tuple-element.125), channel_id=1, source_target_pairs={{16,0},{24,8},{17,1},{25,9},{18,2},{26,10},{19,3},{27,11},{20,4},{... | collective-permute-start | bytes 1769480 | tf_op jit(solution)/shard_map/ppermute | solution.py:367
  107.4 12.7 %collective-permute-start.11 = (f32[5,32]{1,0:T(8,128)S(1)}, f32[5,32]{1,0:T(8,128)S(1)}, u32[]{:S(2)}, u32[]{:S(2)}) collective-permute-start(f32[5,32]{1,0:T(8,128)S(1)} %get-tuple-element.163), channel_id=1, source_target_pairs={{16,8},{24,24},{17,9},{25,25},{18,10},{26,26},{19,11},{27,27},{20,... | collective-permute-start | bytes 1928 | tf_op jit(solution)/shard_map/ppermute | solution.py:367
  108.1 12.8 %collective-permute-start.12 = (f32[5,32]{1,0:T(8,128)S(1)}, f32[5,32]{1,0:T(8,128)S(1)}, u32[]{:S(2)}, u32[]{:S(2)}) collective-permute-start(f32[5,32]{1,0:T(8,128)S(1)} %get-tuple-element.162), channel_id=1, source_target_pairs={{16,0},{24,16},{17,1},{25,17},{18,2},{26,18},{19,3},{27,19},{20,4}... | collective-permute-start | bytes 1928 | tf_op jit(solution)/shard_map/ppermute | solution.py:367
  131.5 9.9 %collective-permute-start.14 = (bf16[4608,128]{1,0:T(8,128)(2,1)}, bf16[4608,128]{1,0:T(8,128)(2,1)}, u32[]{:S(2)}, u32[]{:S(2)}) collective-permute-start(bf16[4608,128]{1,0:T(8,128)(2,1)} %get-tuple-element.136), channel_id=1, source_target_pairs={{0,8},{8,0},{16,24},{24,16},{1,9},{9,1},{17,25},{25,17},{2,10},{10... | collective-permute-start | bytes 3538952 | tf_op jit(solution)/shard_map/ppermute | solution.py:367
  132.1 9.4 %collective-permute-start.15 = (bf16[4608,128]{1,0:T(8,128)(2,1)}, bf16[4608,128]{1,0:T(8,128)(2,1)S(1)}, u32[]{:S(2)}, u32[]{:S(2)}) collective-permute-start(bf16[4608,128]{1,0:T(8,128)(2,1)} %get-tuple-element.139), channel_id=1, source_target_pairs={{0,8},{8,0},{16,24},{24,16},{1,9},{9,1},{17,25},{25,17},{2,10},{10... | collective-permute-start | bytes 3538952 | tf_op jit(solution)/shard_map/ppermute | solution.py:367
  132.1 9.3 %collective-permute-start.16 = (bf16[4608,128]{1,0:T(8,128)(2,1)}, bf16[4608,128]{1,0:T(8,128)(2,1)S(1)}, u32[]{:S(2)}, u32[]{:S(2)}) collective-permute-start(bf16[4608,128]{1,0:T(8,128)(2,1)} %get-tuple-element.140), channel_id=1, source_target_pairs={{0,8},{8,0},{16,24},{24,16},{1,9},{9,1},{17,25},{25,17},{2,10},{10... | collective-permute-start | bytes 3538952 | tf_op jit(solution)/shard_map/ppermute | solution.py:367
  132.6 8.9 %collective-permute-start.17 = (bf16[4608,128]{1,0:T(8,128)(2,1)}, bf16[4608,128]{1,0:T(8,128)(2,1)S(1)}, u32[]{:S(2)}, u32[]{:S(2)}) collective-permute-start(bf16[4608,128]{1,0:T(8,128)(2,1)} %get-tuple-element.141), channel_id=1, source_target_pairs={{0,8},{8,0},{16,24},{24,16},{1,9},{9,1},{17,25},{25,17},{2,10},{10... | collective-permute-start | bytes 3538952 | tf_op jit(solution)/shard_map/ppermute | solution.py:367
  141.4 7.6 %copy-start.8 = (bf16[4608,128]{1,0:T(8,128)(2,1)S(1)}, bf16[4608,128]{1,0:T(8,128)(2,1)}, u32[]{:S(2)}) copy-start(bf16[4608,128]{1,0:T(8,128)(2,1)} %get-tuple-element.145) | copy-start | bytes 3538948
  141.5 44.3 %copy-start.9 = (bf16[4608,128]{1,0:T(8,128)(2,1)}, bf16[4608,128]{1,0:T(8,128)(2,1)S(1)}, u32[]{:S(2)}) copy-start(bf16[4608,128]{1,0:T(8,128)(2,1)S(1)} %collective-permute-done.15) | copy-start | bytes 3538948
  141.5 9.6 %copy-start.7 = (bf16[4608,128]{1,0:T(8,128)(2,1)S(1)}, bf16[4608,128]{1,0:T(8,128)(2,1)}, u32[]{:S(2)}) copy-start(bf16[4608,128]{1,0:T(8,128)(2,1)} %get-tuple-element.147) | copy-start | bytes 3538948
  142.9 6.2 %collective-permute-start.32 = (bf16[576,128]{1,0:T(8,128)(2,1)S(1)}, bf16[576,128]{1,0:T(8,128)(2,1)S(1)}, u32[]{:S(2)}, u32[]{:S(2)}) collective-permute-start(bf16[576,128]{1,0:T(8,128)(2,1)S(1)} %add_convert_fusion.13), channel_id=1, source_target_pairs={{2,0},{4,2},{6,4},{7,6},{5,7},{3,5},{1,3},{0,1},{10,8},{12,10},{14... | collective-permute-start | bytes 442376 | tf_op jit(solution)/shard_map/ppermute | solution.py:367
  145.2 6.0 %collective-permute-start.39 = (bf16[576,128]{1,0:T(8,128)(2,1)S(1)}, bf16[576,128]{1,0:T(8,128)(2,1)S(1)}, u32[]{:S(2)}, u32[]{:S(2)}) collective-permute-start(bf16[576,128]{1,0:T(8,128)(2,1)S(1)} %add_convert_fusion.6), channel_id=1, source_target_pairs={{2,0},{4,2},{6,4},{7,6},{5,7},{3,5},{1,3},{0,1},{10,8},{12,10},{14... | collective-permute-start | bytes 442376 | tf_op jit(solution)/shard_map/ppermute | solution.py:367
  146.5 8.1 %copy-start.10 = (bf16[4608,128]{1,0:T(8,128)(2,1)S(1)}, bf16[4608,128]{1,0:T(8,128)(2,1)}, u32[]{:S(2)}) copy-start(bf16[4608,128]{1,0:T(8,128)(2,1)} %get-tuple-element.143) | copy-start | bytes 3538948
  146.5 5.9 %collective-permute-start.18 = (bf16[576,128]{1,0:T(8,128)(2,1)S(1)}, bf16[576,128]{1,0:T(8,128)(2,1)S(1)}, u32[]{:S(2)}, u32[]{:S(2)}) collective-permute-start(bf16[576,128]{1,0:T(8,128)(2,1)S(1)} %add_convert_fusion.27), channel_id=1, source_target_pairs={{0,2},{2,4},{4,6},{6,7},{7,5},{5,3},{3,1},{1,0},{8,10},{10,12},{12... | collective-permute-start | bytes 442376 | tf_op jit(solution)/shard_map/ppermute | solution.py:367
  148.7 5.9 %collective-permute-start.25 = (bf16[576,128]{1,0:T(8,128)(2,1)S(1)}, bf16[576,128]{1,0:T(8,128)(2,1)S(1)}, u32[]{:S(2)}, u32[]{:S(2)}) collective-permute-start(bf16[576,128]{1,0:T(8,128)(2,1)S(1)} %add_convert_fusion.20), channel_id=1, source_target_pairs={{0,2},{2,4},{4,6},{6,7},{7,5},{5,3},{3,1},{1,0},{8,10},{10,12},{12... | collective-permute-start | bytes 442376 | tf_op jit(solution)/shard_map/ppermute | solution.py:367
  149.1 6.2 %collective-permute-start.33 = (bf16[576,128]{1,0:T(8,128)(2,1)S(1)}, bf16[576,128]{1,0:T(8,128)(2,1)S(1)}, u32[]{:S(2)}, u32[]{:S(2)}) collective-permute-start(bf16[576,128]{1,0:T(8,128)(2,1)S(1)} %add_convert_fusion.12), channel_id=1, source_target_pairs={{2,0},{4,2},{6,4},{7,6},{5,7},{3,5},{1,3},{0,1},{10,8},{12,10},{14... | collective-permute-start | bytes 442376 | tf_op jit(solution)/shard_map/ppermute | solution.py:367
  151.2 7.1 %copy-start.11 = (bf16[4608,128]{1,0:T(8,128)(2,1)S(1)}, bf16[4608,128]{1,0:T(8,128)(2,1)}, u32[]{:S(2)}) copy-start(bf16[4608,128]{1,0:T(8,128)(2,1)} %get-tuple-element.138) | copy-start | bytes 3538948
  151.2 5.9 %collective-permute-start.40 = (bf16[576,128]{1,0:T(8,128)(2,1)S(1)}, bf16[576,128]{1,0:T(8,128)(2,1)S(1)}, u32[]{:S(2)}, u32[]{:S(2)}) collective-permute-start(bf16[576,128]{1,0:T(8,128)(2,1)S(1)} %add_convert_fusion.5), channel_id=1, source_target_pairs={{2,0},{4,2},{6,4},{7,6},{5,7},{3,5},{1,3},{0,1},{10,8},{12,10},{14... | collective-permute-start | bytes 442376 | tf_op jit(solution)/shard_map/ppermute | solution.py:367
  153.4 4.8 %collective-permute-start.19 = (bf16[576,128]{1,0:T(8,128)(2,1)S(1)}, bf16[576,128]{1,0:T(8,128)(2,1)S(1)}, u32[]{:S(2)}, u32[]{:S(2)}) collective-permute-start(bf16[576,128]{1,0:T(8,128)(2,1)S(1)} %add_convert_fusion.26), channel_id=1, source_target_pairs={{0,2},{2,4},{4,6},{6,7},{7,5},{5,3},{3,1},{1,0},{8,10},{10,12},{12... | collective-permute-start | bytes 442376 | tf_op jit(solution)/shard_map/ppermute | solution.py:367
  154.7 5.5 %collective-permute-start.26 = (bf16[576,128]{1,0:T(8,128)(2,1)S(1)}, bf16[576,128]{1,0:T(8,128)(2,1)S(1)}, u32[]{:S(2)}, u32[]{:S(2)}) collective-permute-start(bf16[576,128]{1,0:T(8,128)(2,1)S(1)} %add_convert_fusion.19), channel_id=1, source_target_pairs={{0,2},{2,4},{4,6},{6,7},{7,5},{5,3},{3,1},{1,0},{8,10},{10,12},{12... | collective-permute-start | bytes 442376 | tf_op jit(solution)/shard_map/ppermute | solution.py:367
  155.4 5.0 %collective-permute-start.34 = (bf16[576,128]{1,0:T(8,128)(2,1)S(1)}, bf16[576,128]{1,0:T(8,128)(2,1)S(1)}, u32[]{:S(2)}, u32[]{:S(2)}) collective-permute-start(bf16[576,128]{1,0:T(8,128)(2,1)S(1)} %add_convert_fusion.11), channel_id=1, source_target_pairs={{2,0},{4,2},{6,4},{7,6},{5,7},{3,5},{1,3},{0,1},{10,8},{12,10},{14... | collective-permute-start | bytes 442376 | tf_op jit(solution)/shard_map/ppermute | solution.py:367
  157.2 5.2 %collective-permute-start.41 = (bf16[576,128]{1,0:T(8,128)(2,1)S(1)}, bf16[576,128]{1,0:T(8,128)(2,1)S(1)}, u32[]{:S(2)}, u32[]{:S(2)}) collective-permute-start(bf16[576,128]{1,0:T(8,128)(2,1)S(1)} %add_convert_fusion.4), channel_id=1, source_target_pairs={{2,0},{4,2},{6,4},{7,6},{5,7},{3,5},{1,3},{0,1},{10,8},{12,10},{14... | collective-permute-start | bytes 442376 | tf_op jit(solution)/shard_map/ppermute | solution.py:367
  159.2 4.9 %collective-permute-start.20 = (bf16[576,128]{1,0:T(8,128)(2,1)S(1)}, bf16[576,128]{1,0:T(8,128)(2,1)S(1)}, u32[]{:S(2)}, u32[]{:S(2)}) collective-permute-start(bf16[576,128]{1,0:T(8,128)(2,1)S(1)} %add_convert_fusion.25), channel_id=1, source_target_pairs={{0,2},{2,4},{4,6},{6,7},{7,5},{5,3},{3,1},{1,0},{8,10},{10,12},{12... | collective-permute-start | bytes 442376 | tf_op jit(solution)/shard_map/ppermute | solution.py:367
  160.3 5.5 %collective-permute-start.27 = (bf16[576,128]{1,0:T(8,128)(2,1)S(1)}, bf16[576,128]{1,0:T(8,128)(2,1)S(1)}, u32[]{:S(2)}, u32[]{:S(2)}) collective-permute-start(bf16[576,128]{1,0:T(8,128)(2,1)S(1)} %add_convert_fusion.18), channel_id=1, source_target_pairs={{0,2},{2,4},{4,6},{6,7},{7,5},{5,3},{3,1},{1,0},{8,10},{10,12},{12... | collective-permute-start | bytes 442376 | tf_op jit(solution)/shard_map/ppermute | solution.py:367
  160.4 6.0 %collective-permute-start.35 = (bf16[576,128]{1,0:T(8,128)(2,1)S(1)}, bf16[576,128]{1,0:T(8,128)(2,1)S(1)}, u32[]{:S(2)}, u32[]{:S(2)}) collective-permute-start(bf16[576,128]{1,0:T(8,128)(2,1)S(1)} %add_convert_fusion.10), channel_id=1, source_target_pairs={{2,0},{4,2},{6,4},{7,6},{5,7},{3,5},{1,3},{0,1},{10,8},{12,10},{14... | collective-permute-start | bytes 442376 | tf_op jit(solution)/shard_map/ppermute | solution.py:367
  162.5 5.9 %collective-permute-start.42 = (bf16[576,128]{1,0:T(8,128)(2,1)S(1)}, bf16[576,128]{1,0:T(8,128)(2,1)S(1)}, u32[]{:S(2)}, u32[]{:S(2)}) collective-permute-start(bf16[576,128]{1,0:T(8,128)(2,1)S(1)} %add_convert_fusion.3), channel_id=1, source_target_pairs={{2,0},{4,2},{6,4},{7,6},{5,7},{3,5},{1,3},{0,1},{10,8},{12,10},{14... | collective-permute-start | bytes 442376 | tf_op jit(solution)/shard_map/ppermute | solution.py:367
  165.1 5.3 %collective-permute-start.21 = (bf16[576,128]{1,0:T(8,128)(2,1)S(1)}, bf16[576,128]{1,0:T(8,128)(2,1)S(1)}, u32[]{:S(2)}, u32[]{:S(2)}) collective-permute-start(bf16[576,128]{1,0:T(8,128)(2,1)S(1)} %add_convert_fusion.24), channel_id=1, source_target_pairs={{0,2},{2,4},{4,6},{6,7},{7,5},{5,3},{3,1},{1,0},{8,10},{10,12},{12... | collective-permute-start | bytes 442376 | tf_op jit(solution)/shard_map/ppermute | solution.py:367
  165.8 6.3 %collective-permute-start.28 = (bf16[576,128]{1,0:T(8,128)(2,1)S(1)}, bf16[576,128]{1,0:T(8,128)(2,1)S(1)}, u32[]{:S(2)}, u32[]{:S(2)}) collective-permute-start(bf16[576,128]{1,0:T(8,128)(2,1)S(1)} %add_convert_fusion.17), channel_id=1, source_target_pairs={{0,2},{2,4},{4,6},{6,7},{7,5},{5,3},{3,1},{1,0},{8,10},{10,12},{12... | collective-permute-start | bytes 442376 | tf_op jit(solution)/shard_map/ppermute | solution.py:367
  166.6 6.2 %collective-permute-start.36 = (bf16[576,128]{1,0:T(8,128)(2,1)S(1)}, bf16[576,128]{1,0:T(8,128)(2,1)S(1)}, u32[]{:S(2)}, u32[]{:S(2)}) collective-permute-start(bf16[576,128]{1,0:T(8,128)(2,1)S(1)} %add_convert_fusion.9), channel_id=1, source_target_pairs={{2,0},{4,2},{6,4},{7,6},{5,7},{3,5},{1,3},{0,1},{10,8},{12,10},{14... | collective-permute-start | bytes 442376 | tf_op jit(solution)/shard_map/ppermute | solution.py:367
  168.4 6.0 %collective-permute-start.43 = (bf16[576,128]{1,0:T(8,128)(2,1)S(1)}, bf16[576,128]{1,0:T(8,128)(2,1)S(1)}, u32[]{:S(2)}, u32[]{:S(2)}) collective-permute-start(bf16[576,128]{1,0:T(8,128)(2,1)S(1)} %add_convert_fusion.2), channel_id=1, source_target_pairs={{2,0},{4,2},{6,4},{7,6},{5,7},{3,5},{1,3},{0,1},{10,8},{12,10},{14... | collective-permute-start | bytes 442376 | tf_op jit(solution)/shard_map/ppermute | solution.py:367
  171.4 5.9 %collective-permute-start.22 = (bf16[576,128]{1,0:T(8,128)(2,1)S(1)}, bf16[576,128]{1,0:T(8,128)(2,1)S(1)}, u32[]{:S(2)}, u32[]{:S(2)}) collective-permute-start(bf16[576,128]{1,0:T(8,128)(2,1)S(1)} %add_convert_fusion.23), channel_id=1, source_target_pairs={{0,2},{2,4},{4,6},{6,7},{7,5},{5,3},{3,1},{1,0},{8,10},{10,12},{12... | collective-permute-start | bytes 442376 | tf_op jit(solution)/shard_map/ppermute | solution.py:367
  172.1 6.8 %collective-permute-start.29 = (bf16[576,128]{1,0:T(8,128)(2,1)S(1)}, bf16[576,128]{1,0:T(8,128)(2,1)S(1)}, u32[]{:S(2)}, u32[]{:S(2)}) collective-permute-start(bf16[576,128]{1,0:T(8,128)(2,1)S(1)} %add_convert_fusion.16), channel_id=1, source_target_pairs={{0,2},{2,4},{4,6},{6,7},{7,5},{5,3},{3,1},{1,0},{8,10},{10,12},{12... | collective-permute-start | bytes 442376 | tf_op jit(solution)/shard_map/ppermute | solution.py:367
  172.8 6.8 %collective-permute-start.37 = (bf16[576,128]{1,0:T(8,128)(2,1)S(1)}, bf16[576,128]{1,0:T(8,128)(2,1)S(1)}, u32[]{:S(2)}, u32[]{:S(2)}) collective-permute-start(bf16[576,128]{1,0:T(8,128)(2,1)S(1)} %add_convert_fusion.8), channel_id=1, source_target_pairs={{2,0},{4,2},{6,4},{7,6},{5,7},{3,5},{1,3},{0,1},{10,8},{12,10},{14... | collective-permute-start | bytes 442376 | tf_op jit(solution)/shard_map/ppermute | solution.py:367
  174.5 6.3 %collective-permute-start.44 = (bf16[576,128]{1,0:T(8,128)(2,1)S(1)}, bf16[576,128]{1,0:T(8,128)(2,1)S(1)}, u32[]{:S(2)}, u32[]{:S(2)}) collective-permute-start(bf16[576,128]{1,0:T(8,128)(2,1)S(1)} %add_convert_fusion.1), channel_id=1, source_target_pairs={{2,0},{4,2},{6,4},{7,6},{5,7},{3,5},{1,3},{0,1},{10,8},{12,10},{14... | collective-permute-start | bytes 442376 | tf_op jit(solution)/shard_map/ppermute | solution.py:367
  178.3 5.8 %collective-permute-start.23 = (bf16[576,128]{1,0:T(8,128)(2,1)S(1)}, bf16[576,128]{1,0:T(8,128)(2,1)S(1)}, u32[]{:S(2)}, u32[]{:S(2)}) collective-permute-start(bf16[576,128]{1,0:T(8,128)(2,1)S(1)} %add_convert_fusion.22), channel_id=1, source_target_pairs={{0,2},{2,4},{4,6},{6,7},{7,5},{5,3},{3,1},{1,0},{8,10},{10,12},{12... | collective-permute-start | bytes 442376 | tf_op jit(solution)/shard_map/ppermute | solution.py:367
  179.0 6.8 %collective-permute-start.30 = (bf16[576,128]{1,0:T(8,128)(2,1)S(1)}, bf16[576,128]{1,0:T(8,128)(2,1)S(1)}, u32[]{:S(2)}, u32[]{:S(2)}) collective-permute-start(bf16[576,128]{1,0:T(8,128)(2,1)S(1)} %add_convert_fusion.15), channel_id=1, source_target_pairs={{0,2},{2,4},{4,6},{6,7},{7,5},{5,3},{3,1},{1,0},{8,10},{10,12},{12... | collective-permute-start | bytes 442376 | tf_op jit(solution)/shard_map/ppermute | solution.py:367
  179.6 6.8 %collective-permute-start.38 = (bf16[576,128]{1,0:T(8,128)(2,1)S(1)}, bf16[576,128]{1,0:T(8,128)(2,1)S(1)}, u32[]{:S(2)}, u32[]{:S(2)}) collective-permute-start(bf16[576,128]{1,0:T(8,128)(2,1)S(1)} %add_convert_fusion.7), channel_id=1, source_target_pairs={{2,0},{4,2},{6,4},{7,6},{5,7},{3,5},{1,3},{0,1},{10,8},{12,10},{14... | collective-permute-start | bytes 442376 | tf_op jit(solution)/shard_map/ppermute | solution.py:367
  180.9 7.3 %collective-permute-start.45 = (bf16[576,128]{1,0:T(8,128)(2,1)S(1)}, bf16[576,128]{1,0:T(8,128)(2,1)S(1)}, u32[]{:S(2)}, u32[]{:S(2)}) collective-permute-start(bf16[576,128]{1,0:T(8,128)(2,1)S(1)} %add_convert_fusion), channel_id=1, source_target_pairs={{2,0},{4,2},{6,4},{7,6},{5,7},{3,5},{1,3},{0,1},{10,8},{12,10},{14... | collective-permute-start | bytes 442376 | tf_op jit(solution)/shard_map/ppermute | solution.py:367
  185.1 5.9 %collective-permute-start.24 = (bf16[576,128]{1,0:T(8,128)(2,1)S(1)}, bf16[576,128]{1,0:T(8,128)(2,1)S(1)}, u32[]{:S(2)}, u32[]{:S(2)}) collective-permute-start(bf16[576,128]{1,0:T(8,128)(2,1)S(1)} %add_convert_fusion.21), channel_id=1, source_target_pairs={{0,2},{2,4},{4,6},{6,7},{7,5},{5,3},{3,1},{1,0},{8,10},{10,12},{12... | collective-permute-start | bytes 442376 | tf_op jit(solution)/shard_map/ppermute | solution.py:367
  185.8 6.8 %collective-permute-start.31 = (bf16[576,128]{1,0:T(8,128)(2,1)S(1)}, bf16[576,128]{1,0:T(8,128)(2,1)S(1)}, u32[]{:S(2)}, u32[]{:S(2)}) collective-permute-start(bf16[576,128]{1,0:T(8,128)(2,1)S(1)} %add_convert_fusion.14), channel_id=1, source_target_pairs={{0,2},{2,4},{4,6},{6,7},{7,5},{5,3},{3,1},{1,0},{8,10},{10,12},{12... | collective-permute-start | bytes 442376 | tf_op jit(solution)/shard_map/ppermute | solution.py:367
  194.1 5.7 %collective-permute-start.46 = (bf16[2,576,128]{2,1,0:T(8,128)(2,1)S(1)}, bf16[2,576,128]{2,1,0:T(8,128)(2,1)S(1)}, u32[]{:S(2)}, u32[]{:S(2)}) collective-permute-start(bf16[2,576,128]{2,1,0:T(8,128)(2,1)S(1)} %get-tuple-element.153), channel_id=1, source_target_pairs={{0,2},{2,4},{4,6},{6,7},{7,5},{5,3},{3,1},{1,0},{8,10},{10,12},{12... | collective-permute-start | bytes 884744 | tf_op jit(solution)/shard_map/ppermute | solution.py:367
  194.7 5.8 %collective-permute-start.47 = (bf16[2,576,128]{2,1,0:T(8,128)(2,1)S(1)}, bf16[2,576,128]{2,1,0:T(8,128)(2,1)S(1)}, u32[]{:S(2)}, u32[]{:S(2)}) collective-permute-start(bf16[2,576,128]{2,1,0:T(8,128)(2,1)S(1)} %get-tuple-element.153), channel_id=1, source_target_pairs={{2,0},{4,2},{6,4},{7,6},{5,7},{3,5},{1,3},{0,1},{10,8},{12,10},{14... | collective-permute-start | bytes 884744 | tf_op jit(solution)/shard_map/ppermute | solution.py:367
  199.7 8.5 %collective-permute-start.48 = (bf16[2,576,128]{2,1,0:T(8,128)(2,1)S(1)}, bf16[2,576,128]{2,1,0:T(8,128)(2,1)S(1)}, u32[]{:S(2)}, u32[]{:S(2)}) collective-permute-start(bf16[2,576,128]{2,1,0:T(8,128)(2,1)S(1)} %collective-permute-done.46), channel_id=1, source_target_pairs={{0,2},{2,4},{4,6},{6,7},{7,5},{5,3},{3,1},{1,0},{8,10},{10,12},{12... | collective-permute-start | bytes 884744 | tf_op jit(solution)/shard_map/ppermute | solution.py:367
  200.5 8.3 %collective-permute-start.49 = (bf16[2,576,128]{2,1,0:T(8,128)(2,1)S(1)}, bf16[2,576,128]{2,1,0:T(8,128)(2,1)S(1)}, u32[]{:S(2)}, u32[]{:S(2)}) collective-permute-start(bf16[2,576,128]{2,1,0:T(8,128)(2,1)S(1)} %collective-permute-done.47), channel_id=1, source_target_pairs={{2,0},{4,2},{6,4},{7,6},{5,7},{3,5},{1,3},{0,1},{10,8},{12,10},{14... | collective-permute-start | bytes 884744 | tf_op jit(solution)/shard_map/ppermute | solution.py:367
  208.3 8.7 %collective-permute-start.50 = (bf16[2,576,128]{2,1,0:T(8,128)(2,1)S(1)}, bf16[2,576,128]{2,1,0:T(8,128)(2,1)S(1)}, u32[]{:S(2)}, u32[]{:S(2)}) collective-permute-start(bf16[2,576,128]{2,1,0:T(8,128)(2,1)S(1)} %collective-permute-done.48), channel_id=1, source_target_pairs={{0,2},{2,4},{4,6},{6,7},{7,5},{5,3},{3,1},{1,0},{8,10},{10,12},{12... | collective-permute-start | bytes 884744 | tf_op jit(solution)/shard_map/ppermute | solution.py:367
  208.8 8.8 %collective-permute-start.51 = (bf16[2,576,128]{2,1,0:T(8,128)(2,1)S(1)}, bf16[2,576,128]{2,1,0:T(8,128)(2,1)S(1)}, u32[]{:S(2)}, u32[]{:S(2)}) collective-permute-start(bf16[2,576,128]{2,1,0:T(8,128)(2,1)S(1)} %collective-permute-done.49), channel_id=1, source_target_pairs={{2,0},{4,2},{6,4},{7,6},{5,7},{3,5},{1,3},{0,1},{10,8},{12,10},{14... | collective-permute-start | bytes 884744 | tf_op jit(solution)/shard_map/ppermute | solution.py:367
  217.0 7.8 %collective-permute-start.52 = (bf16[2,576,128]{2,1,0:T(8,128)(2,1)S(1)}, bf16[2,576,128]{2,1,0:T(8,128)(2,1)S(1)}, u32[]{:S(2)}, u32[]{:S(2)}) collective-permute-start(bf16[2,576,128]{2,1,0:T(8,128)(2,1)S(1)} %collective-permute-done.50), channel_id=1, source_target_pairs={{0,2},{2,4},{4,6},{6,7},{7,5},{5,3},{3,1},{1,0},{8,10},{10,12},{12... | collective-permute-start | bytes 884744 | tf_op jit(solution)/shard_map/ppermute | solution.py:367
  226.3 0.7 collective-permute-start.53
  228.7 0.7 collective-permute-start.54
  231.1 27.6 %copy-start.20 = (bf16[32,4608]{1,0:T(8,128)(2,1)S(1)}, bf16[32,4608]{1,0:T(8,128)(2,1)}, u32[]{:S(2)}) copy-start(bf16[32,4608]{1,0:T(8,128)(2,1)} %fusion) | copy-start | bytes 884740
  231.1 26.4 %collective-permute-start.55 = (bf16[32,4608]{1,0:T(8,128)(2,1)}, bf16[32,4608]{1,0:T(8,128)(2,1)}, u32[]{:S(2)}, u32[]{:S(2)}) collective-permute-start(bf16[32,4608]{1,0:T(8,128)(2,1)} %fusion.2), channel_id=1, source_target_pairs={{16,24},{17,25},{18,26},{19,27},{20,28},{21,29},{22,30},{23,31}} | collective-permute-start | bytes 884744 | tf_op jit(solution)/shard_map/ppermute | solution.py:367
  (14 other events, 25.2 us)

commit v4 on v3

--- a/solution.py
+++ b/solution.py
@@ -412,23 +412,20 @@
 
 
 def ring_gather(own, spot, axis):
-    count, ahead, back = ring_routes(axis)
-    kinds, rows, rank = own.shape
+    count, *routes = ring_routes(axis)
+    rows, rank = own[0].shape
 
     def put(whole, piece, offset):
-        return lax.dynamic_update_slice(whole, piece, (0, block_at(spot, offset, count) * rows, 0))
-
-    whole = put(jnp.zeros((kinds, count * rows, rank), own.dtype), own, 0)
-    down = up = own
-    placed = 1
+        return lax.dynamic_update_slice(whole, piece, (block_at(spot, offset, count) * rows, 0))
+
+    whole = [put(jnp.zeros((count * rows, rank), piece.dtype), piece, 0) for piece in own]
+    moving = {(way, kind): piece for kind, piece in enumerate(own) for way in range(2)}
     for step in range(1, count // 2 + 1):
-        down = send(down, axis, ahead)
-        whole = put(whole, down, -step)
-        placed += 1
-        if placed < count:
-            up = send(up, axis, back)
-            whole = put(whole, up, step)
-            placed += 1
+        for way, kind in moving:
+            if 2 * step == count and way != kind % 2:
+                continue
+            moving[way, kind] = send(moving[way, kind], axis, routes[way])
+            whole[kind] = put(whole[kind], moving[way, kind], step if way else -step)
     return whole
 
 
@@ -447,11 +444,7 @@
     label_count = label_rows.shape[0]
     total_rows, halves = micro * rows, 2
     chunks = tasks * halves
-    small = max(total_rows * 2 // 5 // 16 * 16, 16)
-    parts = []
-    for task in range(tasks):
-        sizes = (small, total_rows - small) if task == 0 else (total_rows - small, small)
-        parts += [(0, sizes[0]), (sizes[0], sizes[1])]
+    parts = [(half * (total_rows // halves), total_rows // halves) for _ in range(tasks) for half in range(halves)]
     spot = spot_of(lax.axis_index("dp"), lax.axis_size("dp"))
     place = jnp.stack([stage, member, section, spot]).astype(jnp.int32)
     sections = range(section_count)
@@ -600,8 +593,6 @@
         return [made[:2], made[2:]]
 
     for turn in range(chunks):
-        if turn == 2:
-            token = after(token, crossing[0])
         first_forward(turn)
         if turn == 0:
             token = after(token, others)
@@ -627,7 +618,7 @@
     shares = ring_scatter(sums, other_sums, spot, "dp")
     numerator, denominator = shares
     merged_part = (numerator / (denominator + merge_eps)).astype(bf16)
-    merged = ring_gather(merged_part, spot, "dp")
+    merged = ring_gather([merged_part[0], merged_part[1]], spot, "dp")
     fisher_log = jnp.log(denominator + merge_eps)
 
     current, result = eval_states, eval_states

time: 263 us -> 259 us (0.985)
  waiting for transfers between devices: 85.5 us -> 75.7 us
  other arithmetic: 16.8 us -> 22.1 us
    ppermute x56 -> x63, waiting for transfers between devices: 85.5 us -> 75.7 us  [send(): return lax.ppermute(block, axis, route)]
    convert_element_type x24, other arithmetic: 7.04 us -> 12.6 us  [ring_scatter(): moving[stream] = total if step == count - 1 else total.astype(bf16)]
    ppermute x56 -> x63, starting transfers between devices: 60.4 us -> 60.2 us  [send(): return lax.ppermute(block, axis, route)]
  transfers between devices with their start and end apart: 56 -> 63, of which waited for: 28 -> 28; matrix products, arithmetic and copies ran while one was open for 7% -> 10% of each run, Pallas kernels for 24% -> 24%
where the time goes in v4:
time: 259 us; the launch traced here: 258 us
  waiting for transfers between devices  75.7 us (29%)
  Pallas kernels  72.9 us (28%)
  starting transfers between devices  60.2 us (23%)
  other arithmetic  22.1 us (9%)
  local copies, waits for them, and re-layouts  18.1 us (7%)
  matrix products  7.18 us (3%)
    ppermute x63, waiting for transfers between devices, send(): return lax.ppermute(block, axis, route)  75.7 us
    ppermute x63, starting transfers between devices, send(): return lax.ppermute(block, axis, route)  60.2 us
    pallas_call x4, Pallas kernels, last_stage(): call(token, crossing[turn], label_columns, label_rows, *weights(turn))  48.8 us
    pallas_call x2, Pallas kernels, fisher(): call(token, *[wide for wide, _ in pairs], *[narrow for _, narrow in pairs...  17.7 us
    convert_element_type x24, other arithmetic, ring_scatter(): moving[stream] = total if step == count - 1 else total.astype(bf16)  12.6 us
    unnamed x45, local copies, waits for them, and re-layouts  8.79 us
    dot_general x4, matrix products, block_forward(): jnp.einsum('nr,dr->nd', gelu_value(hidden).astype(bf16), w_up, preferred_...  7.18 us
  transfers between devices with their start and end apart: 63, of which 28 were waited for; matrix products, arithmetic and copies ran while one was open for 10% of the time, Pallas kernels for 24%

profile of v4, /device:TPU:23, one launch (start us, length us, event | category | flops | bytes accessed | tf_op | source)
XLA Modules:
  0.0 257.7 jit_solution(5470107154957051705)
XLA Ops:
  0.7 3.4 %dynamic-slice_bitcast_fusion.1 = (bf16[4608,128]{1,0:T(8,128)(2,1)}, bf16[4608,128]{1,0:T(8,128)(2,1)}) fusion(bf16[1,4,4608,128]{3,2,1,0:T(8,128)(2,1)} %param.7, s32[]{:T(128)S(6)} %select_n.271, s32[]{:T(128)S(6)} %select_n.270), kind=kLoop, calls=%fused_computation.11 | loop fusion | bytes 4718600 | tf_op jit(solution)/shard_map/jit(dynamic_index_in_dim)/squeeze | solution.py:457
  4.8 1.6 dynamic-slice_bitcast_fusion
  7.5 1.9 collective-permute-done.1.up_other.refs_9_
  9.4 1.0 copy-done.4
  11.2 1.6 collective-permute-done.2.down_other.refs_10_
  12.9 1.3 collective-permute-start.4
  15.0 1.3 collective-permute-start.5
  18.7 17.7 %collective-permute-done.4.states = bf16[80,4608]{1,0:T(8,128)(2,1)S(1)} collective-permute-done((bf16[80,4608]{1,0:T(8,128)(2,1)}, bf16[80,4608]{1,0:T(8,128)(2,1)S(1)}, u32[]{:S(2)}, u32[]{:S(2)}) %collective-permute-start.4) | collective-permute-done | bytes 737312 | tf_op jit(solution)/shard_map/ppermute | solution.py:367
  37.3 11.8 %last_stage.4 = (bf16[80,4608]{1,0:T(8,128)(2,1)}, f32[8,128]{1,0:T(8,128)}, bf16[2,2,80,4608]{3,2,1,0:T(8,128)(2,1)}, bf16[2,2,80,128]{3,2,1,0:T(8,128)(2,1)}) custom-call(s32[4]{0:T(128)} %pad_add_fusion.place, bf16[80,4608]{1,0:T(8,128)(2,1)} %copy-done.18, s32[2,160,1]{2,1,0:T(8,128)} %reshape.92.labels, bf16[256,4608]{1,0:T(8,128)(2,1)} %label_rows.7, ...), custom_call_target="tpu_custom_call" | custom-call | flops 1132462080 | bytes 4718592 | tf_op jit(solution)/shard_map/last_stage/pallas_call | solution.py:542
  49.1 1.3 collective-permute-start.6
  50.5 1.3 collective-permute-start.7
  53.0 11.9 %last_stage.5 = (bf16[80,4608]{1,0:T(8,128)(2,1)}, f32[8,128]{1,0:T(8,128)}, bf16[2,2,80,4608]{3,2,1,0:T(8,128)(2,1)}, bf16[2,2,80,128]{3,2,1,0:T(8,128)(2,1)}) custom-call(s32[4]{0:T(128)} %pad_add_fusion.place, bf16[80,4608]{1,0:T(8,128)(2,1)} %copy-done.16, s32[2,160,1]{2,1,0:T(8,128)} %reshape.92.labels, bf16[256,4608]{1,0:T(8,128)(2,1)} %label_rows.7, ...), custom_call_target="tpu_custom_call" | custom-call | flops 1132462080 | bytes 4718592 | tf_op jit(solution)/shard_map/last_stage/pallas_call | solution.py:542
  64.9 1.3 collective-permute-start.8
  66.3 1.3 collective-permute-start.9
  71.1 12.5 %last_stage.6 = (bf16[80,4608]{1,0:T(8,128)(2,1)}, f32[8,128]{1,0:T(8,128)}, bf16[2,2,80,4608]{3,2,1,0:T(8,128)(2,1)}, bf16[2,2,80,128]{3,2,1,0:T(8,128)(2,1)}) custom-call(s32[4]{0:T(128)} %pad_add_fusion.place, bf16[80,4608]{1,0:T(8,128)(2,1)} %copy-done.17, s32[2,160,1]{2,1,0:T(8,128)} %reshape.92.labels, bf16[256,4608]{1,0:T(8,128)(2,1)} %label_rows.7, ...), custom_call_target="tpu_custom_call" | custom-call | flops 1132462080 | bytes 4718592 | tf_op jit(solution)/shard_map/last_stage/pallas_call | solution.py:542
  83.6 1.3 collective-permute-start.10
  88.3 12.5 %last_stage.7 = (bf16[80,4608]{1,0:T(8,128)(2,1)}, f32[8,128]{1,0:T(8,128)}, bf16[2,2,80,4608]{3,2,1,0:T(8,128)(2,1)}, bf16[2,2,80,128]{3,2,1,0:T(8,128)(2,1)}) custom-call(s32[4]{0:T(128)} %pad_add_fusion.place, bf16[80,4608]{1,0:T(8,128)(2,1)} %copy-done.13, s32[2,160,1]{2,1,0:T(8,128)} %reshape.92.labels, bf16[256,4608]{1,0:T(8,128)(2,1)} %label_rows.7, ...), custom_call_target="tpu_custom_call" | custom-call | flops 1132462080 | bytes 4718592 | tf_op jit(solution)/shard_map/last_stage/pallas_call | solution.py:542
  100.8 1.3 collective-permute-start.13
  106.1 8.3 %collective-permute-start.12 = (f32[5,32]{1,0:T(8,128)S(1)}, f32[5,32]{1,0:T(8,128)S(1)}, u32[]{:S(2)}, u32[]{:S(2)}) collective-permute-start(f32[5,32]{1,0:T(8,128)S(1)} %get-tuple-element.160), channel_id=1, source_target_pairs={{16,0},{24,16},{17,1},{25,17},{18,2},{26,18},{19,3},{27,19},{20,4}... | collective-permute-start | bytes 1928 | tf_op jit(solution)/shard_map/ppermute | solution.py:367
  115.2 3.0 %collective-permute-done.13.grad = bf16[80,4608]{1,0:T(8,128)(2,1)S(1)} collective-permute-done((bf16[80,4608]{1,0:T(8,128)(2,1)}, bf16[80,4608]{1,0:T(8,128)(2,1)S(1)}, u32[]{:S(2)}, u32[]{:S(2)}) %collective-permute-start.13) | collective-permute-done | bytes 737312 | tf_op jit(solution)/shard_map/ppermute | solution.py:367
  119.1 1.0 first_backward.7
  120.1 8.9 %fisher_away.1 = (bf16[4608,128]{1,0:T(8,128)(2,1)}, bf16[4608,128]{1,0:T(8,128)(2,1)}, bf16[4608,128]{1,0:T(8,128)(2,1)}, bf16[4608,128]{1,0:T(8,128)(2,1)}) custom-call(s32[4]{0:T(128)} %pad_add_fusion.place, bf16[2,2,80,4608]{3,2,1,0:T(8,128)(2,1)} %get-tuple-element.130.refs_0_, bf16[2,2,80,4608]{3,2,1,0:T(8,128)(2,1)} %get-tuple-element.131.refs_1_, ...), custom_call_target="tpu_custom_call" | custom-call | flops 754974720 | bytes 11796480 | tf_op jit(solution)/shard_map/fisher_away/pallas_call | solution.py:592
  130.7 8.8 %fisher_own.1 = (bf16[4608,128]{1,0:T(8,128)(2,1)}, bf16[4608,128]{1,0:T(8,128)(2,1)}, bf16[4608,128]{1,0:T(8,128)(2,1)}, bf16[4608,128]{1,0:T(8,128)(2,1)}) custom-call(s32[4]{0:T(128)} %pad_add_fusion.place, bf16[2,2,80,4608]{3,2,1,0:T(8,128)(2,1)} %get-tuple-element.130.refs_0_, bf16[2,2,80,4608]{3,2,1,0:T(8,128)(2,1)} %get-tuple-element.131.refs_1_, ...), custom_call_target="tpu_custom_call" | custom-call | flops 754974720 | bytes 11796480 | tf_op jit(solution)/shard_map/fisher_own/pallas_call | solution.py:592
  139.6 1.1 add_convert_fusion.13
  140.7 1.4 collective-permute-start.32
  143.3 1.0 add_convert_fusion.27
  144.4 1.3 collective-permute-start.18
  145.6 1.0 add_convert_fusion.20
  147.1 1.2 collective-permute-start.33
  149.1 1.2 collective-permute-start.40
  150.2 1.0 add_convert_fusion.26
  152.4 1.0 add_convert_fusion.19
  156.0 1.0 add_convert_fusion.25
  157.7 1.6 collective-permute-done.26
  159.3 1.0 add_convert_fusion.18
  160.4 1.5 collective-permute-start.35
  163.5 1.1 collective-permute-start.21
  166.5 1.5 collective-permute-start.36
  170.0 1.3 collective-permute-start.22
  171.4 1.0 add_convert_fusion.16
  174.9 1.0 add_convert_fusion.22
  175.9 1.7 collective-permute-start.23
  178.5 1.3 collective-permute-start.30
  180.2 1.4 collective-permute-done.44
  182.6 1.0 add_convert_fusion.21
  185.3 1.5 collective-permute-start.31
  186.8 1.9 collective-permute-done.45
  189.9 2.2 collective-permute-done.31
  196.5 1.8 collective-permute-done.46
  198.3 1.1 collective-permute-start.48
  202.3 1.1 collective-permute-start.50
  204.6 1.2 collective-permute-start.57
  206.6 1.5 collective-permute-done.50
  208.0 1.2 collective-permute-start.52
  209.2 3.1 %collective-permute-done.58 = bf16[576,128]{1,0:T(8,128)(2,1)S(1)} collective-permute-done((bf16[576,128]{1,0:T(8,128)(2,1)S(1)}, bf16[576,128]{1,0:T(8,128)(2,1)S(1)}, u32[]{:S(2)}, u32[]{:S(2)}) %collective-permute-start.58) | collective-permute-done | bytes 147488 | tf_op jit(solution)/shard_map/ppermute | solution.py:367
  212.7 1.2 collective-permute-done.52
  213.9 3.5 %collective-permute-done.59 = bf16[576,128]{1,0:T(8,128)(2,1)S(1)} collective-permute-done((bf16[576,128]{1,0:T(8,128)(2,1)S(1)}, bf16[576,128]{1,0:T(8,128)(2,1)S(1)}, u32[]{:S(2)}, u32[]{:S(2)}) %collective-permute-start.59) | collective-permute-done | bytes 147488 | tf_op jit(solution)/shard_map/ppermute | solution.py:367
  217.5 1.5 fusion
  219.9 1.5 fusion.1
  222.3 1.5 fusion.2
  223.8 1.4 collective-permute-start.62
  226.7 27.2 %collective-permute-done.62 = bf16[32,4608]{1,0:T(8,128)(2,1)} collective-permute-done((bf16[32,4608]{1,0:T(8,128)(2,1)}, bf16[32,4608]{1,0:T(8,128)(2,1)}, u32[]{:S(2)}, u32[]{:S(2)}) %collective-permute-start.62) | collective-permute-done | bytes 294944 | tf_op jit(solution)/shard_map/ppermute | solution.py:367
  254.0 1.1 fusion.10
  255.1 2.6 %fusion.5 = bf16[1,32,4608]{2,1,0:T(8,128)(2,1)} fusion(bf16[4608,128]{1,0:T(8,128)(2,1)S(1)} %constant_dynamic-update-slice_fusion, bf16[32,4608]{1,0:T(8,128)(2,1)} %collective-permute-done.62, bf16[32,4608]{1,0:T(8,128)(2,1)} %fusion.2, bf16[32,4608]{1,0:T(8,128)(2,1)} %fusion.1, bf16[32,4608]{1,0:T(8,128)(2,1)S(1)} %copy-done.11, ...), kind=kOutput, calls=%fused_computation.9 | convolution fusion | flops 76570624 | bytes 4128900 | tf_op jit(solution)/shard_map/nr,dr->nd/dot_general | solution.py:334
  (200 shorter events, 55.0 us)
Async XLA Ops:
  4.1 3.4 %collective-permute-start = (bf16[4608,128]{1,0:T(8,128)(2,1)}, bf16[4608,128]{1,0:T(8,128)(2,1)S(1)}, u32[]{:S(2)}, u32[]{:S(2)}) collective-permute-start(bf16[4608,128]{1,0:T(8,128)(2,1)} %get-tuple-element.153), channel_id=1, source_target_pairs={{0,8},{8,0},{16,24},{24,16},{1,9},{9,1},{17,25},{25,17},{2,10},{10... | collective-permute-start | bytes 3538952 | tf_op jit(solution)/shard_map/ppermute | solution.py:367
  6.4 3.1 %collective-permute-start.1 = (bf16[4608,128]{1,0:T(8,128)(2,1)}, bf16[4608,128]{1,0:T(8,128)(2,1)S(1)}, u32[]{:S(2)}, u32[]{:S(2)}) collective-permute-start(bf16[4608,128]{1,0:T(8,128)(2,1)} %get-tuple-element.151), channel_id=1, source_target_pairs={{0,8},{8,0},{16,24},{24,16},{1,9},{9,1},{17,25},{25,17},{2,10},{10... | collective-permute-start | bytes 3538952 | tf_op jit(solution)/shard_map/ppermute | solution.py:367
  6.4 6.4 %collective-permute-start.2 = (bf16[4608,128]{1,0:T(8,128)(2,1)}, bf16[4608,128]{1,0:T(8,128)(2,1)S(1)}, u32[]{:S(2)}, u32[]{:S(2)}) collective-permute-start(bf16[4608,128]{1,0:T(8,128)(2,1)} %get-tuple-element.152), channel_id=1, source_target_pairs={{0,8},{8,0},{16,24},{24,16},{1,9},{9,1},{17,25},{25,17},{2,10},{10... | collective-permute-start | bytes 3538952 | tf_op jit(solution)/shard_map/ppermute | solution.py:367
  6.9 6.1 %collective-permute-start.3 = (bf16[4608,128]{1,0:T(8,128)(2,1)}, bf16[4608,128]{1,0:T(8,128)(2,1)}, u32[]{:S(2)}, u32[]{:S(2)}) collective-permute-start(bf16[4608,128]{1,0:T(8,128)(2,1)} %get-tuple-element.150), channel_id=1, source_target_pairs={{0,8},{8,0},{16,24},{24,16},{1,9},{9,1},{17,25},{25,17},{2,10},{10... | collective-permute-start | bytes 3538952 | tf_op jit(solution)/shard_map/ppermute | solution.py:367
  12.9 23.5 %collective-permute-start.4 = (bf16[80,4608]{1,0:T(8,128)(2,1)}, bf16[80,4608]{1,0:T(8,128)(2,1)S(1)}, u32[]{:S(2)}, u32[]{:S(2)}) collective-permute-start(bf16[80,4608]{1,0:T(8,128)(2,1)} %get-tuple-element.85), channel_id=1, source_target_pairs={{0,16},{8,24},{1,17},{9,25},{2,18},{10,26},{3,19},{11,27},{4,20},{... | collective-permute-start | bytes 2211848 | tf_op jit(solution)/shard_map/ppermute | solution.py:367
  15.0 37.1 %collective-permute-start.5 = (bf16[80,4608]{1,0:T(8,128)(2,1)}, bf16[80,4608]{1,0:T(8,128)(2,1)S(1)}, u32[]{:S(2)}, u32[]{:S(2)}) collective-permute-start(bf16[80,4608]{1,0:T(8,128)(2,1)} %get-tuple-element.89), channel_id=1, source_target_pairs={{0,16},{8,24},{1,17},{9,25},{2,18},{10,26},{3,19},{11,27},{4,20},{... | collective-permute-start | bytes 2211848 | tf_op jit(solution)/shard_map/ppermute | solution.py:367
  18.7 31.8 %copy-start.21 = (bf16[80,4608]{1,0:T(8,128)(2,1)S(1)}, bf16[80,4608]{1,0:T(8,128)(2,1)}, u32[]{:S(2)}) copy-start(bf16[80,4608]{1,0:T(8,128)(2,1)} %get-tuple-element.100) | copy-start | bytes 2211844
  49.1 19.1 %collective-permute-start.6 = (bf16[80,4608]{1,0:T(8,128)(2,1)}, bf16[80,4608]{1,0:T(8,128)(2,1)S(1)}, u32[]{:S(2)}, u32[]{:S(2)}) collective-permute-start(bf16[80,4608]{1,0:T(8,128)(2,1)} %get-tuple-element.92), channel_id=1, source_target_pairs={{16,0},{24,8},{17,1},{25,9},{18,2},{26,10},{19,3},{27,11},{20,4},{... | collective-permute-start | bytes 2211848 | tf_op jit(solution)/shard_map/ppermute | solution.py:367
  50.5 19.7 %collective-permute-start.7 = (bf16[80,4608]{1,0:T(8,128)(2,1)S(1)}, bf16[80,4608]{1,0:T(8,128)(2,1)S(1)}, u32[]{:S(2)}, u32[]{:S(2)}) collective-permute-start(bf16[80,4608]{1,0:T(8,128)(2,1)S(1)} %copy-done.21), channel_id=1, source_target_pairs={{0,16},{8,24},{1,17},{9,25},{2,18},{10,26},{3,19},{11,27},{4,20},{... | collective-permute-start | bytes 2211848 | tf_op jit(solution)/shard_map/ppermute | solution.py:367
  64.9 20.7 %collective-permute-start.8 = (bf16[80,4608]{1,0:T(8,128)(2,1)}, bf16[80,4608]{1,0:T(8,128)(2,1)S(1)}, u32[]{:S(2)}, u32[]{:S(2)}) collective-permute-start(bf16[80,4608]{1,0:T(8,128)(2,1)} %get-tuple-element.103), channel_id=1, source_target_pairs={{16,0},{24,8},{17,1},{25,9},{18,2},{26,10},{19,3},{27,11},{20,4},{... | collective-permute-start | bytes 2211848 | tf_op jit(solution)/shard_map/ppermute | solution.py:367
  66.3 21.1 %collective-permute-start.9 = (bf16[80,4608]{1,0:T(8,128)(2,1)S(1)}, bf16[80,4608]{1,0:T(8,128)(2,1)S(1)}, u32[]{:S(2)}, u32[]{:S(2)}) collective-permute-start(bf16[80,4608]{1,0:T(8,128)(2,1)S(1)} %copy-done.20), channel_id=1, source_target_pairs={{0,16},{8,24},{1,17},{9,25},{2,18},{10,26},{3,19},{11,27},{4,20},{... | collective-permute-start | bytes 2211848 | tf_op jit(solution)/shard_map/ppermute | solution.py:367
  83.6 20.1 %collective-permute-start.10 = (bf16[80,4608]{1,0:T(8,128)(2,1)}, bf16[80,4608]{1,0:T(8,128)(2,1)S(1)}, u32[]{:S(2)}, u32[]{:S(2)}) collective-permute-start(bf16[80,4608]{1,0:T(8,128)(2,1)} %get-tuple-element.114), channel_id=1, source_target_pairs={{16,0},{24,8},{17,1},{25,9},{18,2},{26,10},{19,3},{27,11},{20,4},{... | collective-permute-start | bytes 2211848 | tf_op jit(solution)/shard_map/ppermute | solution.py:367
  100.8 17.4 %collective-permute-start.13 = (bf16[80,4608]{1,0:T(8,128)(2,1)}, bf16[80,4608]{1,0:T(8,128)(2,1)S(1)}, u32[]{:S(2)}, u32[]{:S(2)}) collective-permute-start(bf16[80,4608]{1,0:T(8,128)(2,1)} %get-tuple-element.123), channel_id=1, source_target_pairs={{16,0},{24,8},{17,1},{25,9},{18,2},{26,10},{19,3},{27,11},{20,4},{... | collective-permute-start | bytes 2211848 | tf_op jit(solution)/shard_map/ppermute | solution.py:367
  105.4 9.0 %collective-permute-start.11 = (f32[5,32]{1,0:T(8,128)S(1)}, f32[5,32]{1,0:T(8,128)S(1)}, u32[]{:S(2)}, u32[]{:S(2)}) collective-permute-start(f32[5,32]{1,0:T(8,128)S(1)} %get-tuple-element.161), channel_id=1, source_target_pairs={{16,8},{24,24},{17,9},{25,25},{18,10},{26,26},{19,11},{27,27},{20,... | collective-permute-start | bytes 1928 | tf_op jit(solution)/shard_map/ppermute | solution.py:367
  106.1 9.1 %collective-permute-start.12 = (f32[5,32]{1,0:T(8,128)S(1)}, f32[5,32]{1,0:T(8,128)S(1)}, u32[]{:S(2)}, u32[]{:S(2)}) collective-permute-start(f32[5,32]{1,0:T(8,128)S(1)} %get-tuple-element.160), channel_id=1, source_target_pairs={{16,0},{24,16},{17,1},{25,17},{18,2},{26,18},{19,3},{27,19},{20,4}... | collective-permute-start | bytes 1928 | tf_op jit(solution)/shard_map/ppermute | solution.py:367
  129.0 10.5 %collective-permute-start.14 = (bf16[4608,128]{1,0:T(8,128)(2,1)}, bf16[4608,128]{1,0:T(8,128)(2,1)}, u32[]{:S(2)}, u32[]{:S(2)}) collective-permute-start(bf16[4608,128]{1,0:T(8,128)(2,1)} %get-tuple-element.134), channel_id=1, source_target_pairs={{0,8},{8,0},{16,24},{24,16},{1,9},{9,1},{17,25},{25,17},{2,10},{10... | collective-permute-start | bytes 3538952 | tf_op jit(solution)/shard_map/ppermute | solution.py:367
  130.0 9.6 %collective-permute-start.15 = (bf16[4608,128]{1,0:T(8,128)(2,1)}, bf16[4608,128]{1,0:T(8,128)(2,1)}, u32[]{:S(2)}, u32[]{:S(2)}) collective-permute-start(bf16[4608,128]{1,0:T(8,128)(2,1)} %get-tuple-element.137), channel_id=1, source_target_pairs={{0,8},{8,0},{16,24},{24,16},{1,9},{9,1},{17,25},{25,17},{2,10},{10... | collective-permute-start | bytes 3538952 | tf_op jit(solution)/shard_map/ppermute | solution.py:367
  130.0 9.5 %collective-permute-start.16 = (bf16[4608,128]{1,0:T(8,128)(2,1)}, bf16[4608,128]{1,0:T(8,128)(2,1)S(1)}, u32[]{:S(2)}, u32[]{:S(2)}) collective-permute-start(bf16[4608,128]{1,0:T(8,128)(2,1)} %get-tuple-element.138), channel_id=1, source_target_pairs={{0,8},{8,0},{16,24},{24,16},{1,9},{9,1},{17,25},{25,17},{2,10},{10... | collective-permute-start | bytes 3538952 | tf_op jit(solution)/shard_map/ppermute | solution.py:367
  130.5 9.1 %collective-permute-start.17 = (bf16[4608,128]{1,0:T(8,128)(2,1)}, bf16[4608,128]{1,0:T(8,128)(2,1)S(1)}, u32[]{:S(2)}, u32[]{:S(2)}) collective-permute-start(bf16[4608,128]{1,0:T(8,128)(2,1)} %get-tuple-element.139), channel_id=1, source_target_pairs={{0,8},{8,0},{16,24},{24,16},{1,9},{9,1},{17,25},{25,17},{2,10},{10... | collective-permute-start | bytes 3538952 | tf_op jit(solution)/shard_map/ppermute | solution.py:367
  140.7 6.3 %collective-permute-start.32 = (bf16[576,128]{1,0:T(8,128)(2,1)S(1)}, bf16[576,128]{1,0:T(8,128)(2,1)S(1)}, u32[]{:S(2)}, u32[]{:S(2)}) collective-permute-start(bf16[576,128]{1,0:T(8,128)(2,1)S(1)} %add_convert_fusion.13), channel_id=1, source_target_pairs={{2,0},{4,2},{6,4},{7,6},{5,7},{3,5},{1,3},{0,1},{10,8},{12,10},{14... | collective-permute-start | bytes 442376 | tf_op jit(solution)/shard_map/ppermute | solution.py:367
  143.0 6.0 %collective-permute-start.39 = (bf16[576,128]{1,0:T(8,128)(2,1)S(1)}, bf16[576,128]{1,0:T(8,128)(2,1)S(1)}, u32[]{:S(2)}, u32[]{:S(2)}) collective-permute-start(bf16[576,128]{1,0:T(8,128)(2,1)S(1)} %add_convert_fusion.6), channel_id=1, source_target_pairs={{2,0},{4,2},{6,4},{7,6},{5,7},{3,5},{1,3},{0,1},{10,8},{12,10},{14... | collective-permute-start | bytes 442376 | tf_op jit(solution)/shard_map/ppermute | solution.py:367
  144.4 5.9 %collective-permute-start.18 = (bf16[576,128]{1,0:T(8,128)(2,1)S(1)}, bf16[576,128]{1,0:T(8,128)(2,1)S(1)}, u32[]{:S(2)}, u32[]{:S(2)}) collective-permute-start(bf16[576,128]{1,0:T(8,128)(2,1)S(1)} %add_convert_fusion.27), channel_id=1, source_target_pairs={{0,2},{2,4},{4,6},{6,7},{7,5},{5,3},{3,1},{1,0},{8,10},{10,12},{12... | collective-permute-start | bytes 442376 | tf_op jit(solution)/shard_map/ppermute | solution.py:367
  146.7 5.8 %collective-permute-start.25 = (bf16[576,128]{1,0:T(8,128)(2,1)S(1)}, bf16[576,128]{1,0:T(8,128)(2,1)S(1)}, u32[]{:S(2)}, u32[]{:S(2)}) collective-permute-start(bf16[576,128]{1,0:T(8,128)(2,1)S(1)} %add_convert_fusion.20), channel_id=1, source_target_pairs={{0,2},{2,4},{4,6},{6,7},{7,5},{5,3},{3,1},{1,0},{8,10},{10,12},{12... | collective-permute-start | bytes 442376 | tf_op jit(solution)/shard_map/ppermute | solution.py:367
  147.1 7.0 %collective-permute-start.33 = (bf16[576,128]{1,0:T(8,128)(2,1)S(1)}, bf16[576,128]{1,0:T(8,128)(2,1)S(1)}, u32[]{:S(2)}, u32[]{:S(2)}) collective-permute-start(bf16[576,128]{1,0:T(8,128)(2,1)S(1)} %add_convert_fusion.12), channel_id=1, source_target_pairs={{2,0},{4,2},{6,4},{7,6},{5,7},{3,5},{1,3},{0,1},{10,8},{12,10},{14... | collective-permute-start | bytes 442376 | tf_op jit(solution)/shard_map/ppermute | solution.py:367
  149.1 6.0 %collective-permute-start.40 = (bf16[576,128]{1,0:T(8,128)(2,1)S(1)}, bf16[576,128]{1,0:T(8,128)(2,1)S(1)}, u32[]{:S(2)}, u32[]{:S(2)}) collective-permute-start(bf16[576,128]{1,0:T(8,128)(2,1)S(1)} %add_convert_fusion.5), channel_id=1, source_target_pairs={{2,0},{4,2},{6,4},{7,6},{5,7},{3,5},{1,3},{0,1},{10,8},{12,10},{14... | collective-permute-start | bytes 442376 | tf_op jit(solution)/shard_map/ppermute | solution.py:367
  151.3 4.8 %collective-permute-start.19 = (bf16[576,128]{1,0:T(8,128)(2,1)S(1)}, bf16[576,128]{1,0:T(8,128)(2,1)S(1)}, u32[]{:S(2)}, u32[]{:S(2)}) collective-permute-start(bf16[576,128]{1,0:T(8,128)(2,1)S(1)} %add_convert_fusion.26), channel_id=1, source_target_pairs={{0,2},{2,4},{4,6},{6,7},{7,5},{5,3},{3,1},{1,0},{8,10},{10,12},{12... | collective-permute-start | bytes 442376 | tf_op jit(solution)/shard_map/ppermute | solution.py:367
  153.4 5.9 %collective-permute-start.26 = (bf16[576,128]{1,0:T(8,128)(2,1)S(1)}, bf16[576,128]{1,0:T(8,128)(2,1)S(1)}, u32[]{:S(2)}, u32[]{:S(2)}) collective-permute-start(bf16[576,128]{1,0:T(8,128)(2,1)S(1)} %add_convert_fusion.19), channel_id=1, source_target_pairs={{0,2},{2,4},{4,6},{6,7},{7,5},{5,3},{3,1},{1,0},{8,10},{10,12},{12... | collective-permute-start | bytes 442376 | tf_op jit(solution)/shard_map/ppermute | solution.py:367
  154.1 6.2 %collective-permute-start.34 = (bf16[576,128]{1,0:T(8,128)(2,1)S(1)}, bf16[576,128]{1,0:T(8,128)(2,1)S(1)}, u32[]{:S(2)}, u32[]{:S(2)}) collective-permute-start(bf16[576,128]{1,0:T(8,128)(2,1)S(1)} %add_convert_fusion.11), channel_id=1, source_target_pairs={{2,0},{4,2},{6,4},{7,6},{5,7},{3,5},{1,3},{0,1},{10,8},{12,10},{14... | collective-permute-start | bytes 442376 | tf_op jit(solution)/shard_map/ppermute | solution.py:367
  155.1 6.8 %collective-permute-start.41 = (bf16[576,128]{1,0:T(8,128)(2,1)S(1)}, bf16[576,128]{1,0:T(8,128)(2,1)S(1)}, u32[]{:S(2)}, u32[]{:S(2)}) collective-permute-start(bf16[576,128]{1,0:T(8,128)(2,1)S(1)} %add_convert_fusion.4), channel_id=1, source_target_pairs={{2,0},{4,2},{6,4},{7,6},{5,7},{3,5},{1,3},{0,1},{10,8},{12,10},{14... | collective-permute-start | bytes 442376 | tf_op jit(solution)/shard_map/ppermute | solution.py:367
  157.0 5.5 %collective-permute-start.20 = (bf16[576,128]{1,0:T(8,128)(2,1)S(1)}, bf16[576,128]{1,0:T(8,128)(2,1)S(1)}, u32[]{:S(2)}, u32[]{:S(2)}) collective-permute-start(bf16[576,128]{1,0:T(8,128)(2,1)S(1)} %add_convert_fusion.25), channel_id=1, source_target_pairs={{0,2},{2,4},{4,6},{6,7},{7,5},{5,3},{3,1},{1,0},{8,10},{10,12},{12... | collective-permute-start | bytes 442376 | tf_op jit(solution)/shard_map/ppermute | solution.py:367
  160.3 5.0 %collective-permute-start.27 = (bf16[576,128]{1,0:T(8,128)(2,1)S(1)}, bf16[576,128]{1,0:T(8,128)(2,1)S(1)}, u32[]{:S(2)}, u32[]{:S(2)}) collective-permute-start(bf16[576,128]{1,0:T(8,128)(2,1)S(1)} %add_convert_fusion.18), channel_id=1, source_target_pairs={{0,2},{2,4},{4,6},{6,7},{7,5},{5,3},{3,1},{1,0},{8,10},{10,12},{12... | collective-permute-start | bytes 442376 | tf_op jit(solution)/shard_map/ppermute | solution.py:367
  160.4 5.9 %collective-permute-start.35 = (bf16[576,128]{1,0:T(8,128)(2,1)S(1)}, bf16[576,128]{1,0:T(8,128)(2,1)S(1)}, u32[]{:S(2)}, u32[]{:S(2)}) collective-permute-start(bf16[576,128]{1,0:T(8,128)(2,1)S(1)} %add_convert_fusion.10), channel_id=1, source_target_pairs={{2,0},{4,2},{6,4},{7,6},{5,7},{3,5},{1,3},{0,1},{10,8},{12,10},{14... | collective-permute-start | bytes 442376 | tf_op jit(solution)/shard_map/ppermute | solution.py:367
  162.0 6.0 %collective-permute-start.42 = (bf16[576,128]{1,0:T(8,128)(2,1)S(1)}, bf16[576,128]{1,0:T(8,128)(2,1)S(1)}, u32[]{:S(2)}, u32[]{:S(2)}) collective-permute-start(bf16[576,128]{1,0:T(8,128)(2,1)S(1)} %add_convert_fusion.3), channel_id=1, source_target_pairs={{2,0},{4,2},{6,4},{7,6},{5,7},{3,5},{1,3},{0,1},{10,8},{12,10},{14... | collective-permute-start | bytes 442376 | tf_op jit(solution)/shard_map/ppermute | solution.py:367
  163.5 5.6 %collective-permute-start.21 = (bf16[576,128]{1,0:T(8,128)(2,1)S(1)}, bf16[576,128]{1,0:T(8,128)(2,1)S(1)}, u32[]{:S(2)}, u32[]{:S(2)}) collective-permute-start(bf16[576,128]{1,0:T(8,128)(2,1)S(1)} %add_convert_fusion.24), channel_id=1, source_target_pairs={{0,2},{2,4},{4,6},{6,7},{7,5},{5,3},{3,1},{1,0},{8,10},{10,12},{12... | collective-permute-start | bytes 442376 | tf_op jit(solution)/shard_map/ppermute | solution.py:367
  166.3 5.1 %collective-permute-start.28 = (bf16[576,128]{1,0:T(8,128)(2,1)S(1)}, bf16[576,128]{1,0:T(8,128)(2,1)S(1)}, u32[]{:S(2)}, u32[]{:S(2)}) collective-permute-start(bf16[576,128]{1,0:T(8,128)(2,1)S(1)} %add_convert_fusion.17), channel_id=1, source_target_pairs={{0,2},{2,4},{4,6},{6,7},{7,5},{5,3},{3,1},{1,0},{8,10},{10,12},{12... | collective-permute-start | bytes 442376 | tf_op jit(solution)/shard_map/ppermute | solution.py:367
  166.5 6.7 %collective-permute-start.36 = (bf16[576,128]{1,0:T(8,128)(2,1)S(1)}, bf16[576,128]{1,0:T(8,128)(2,1)S(1)}, u32[]{:S(2)}, u32[]{:S(2)}) collective-permute-start(bf16[576,128]{1,0:T(8,128)(2,1)S(1)} %add_convert_fusion.9), channel_id=1, source_target_pairs={{2,0},{4,2},{6,4},{7,6},{5,7},{3,5},{1,3},{0,1},{10,8},{12,10},{14... | collective-permute-start | bytes 442376 | tf_op jit(solution)/shard_map/ppermute | solution.py:367
  168.0 6.0 %collective-permute-start.43 = (bf16[576,128]{1,0:T(8,128)(2,1)S(1)}, bf16[576,128]{1,0:T(8,128)(2,1)S(1)}, u32[]{:S(2)}, u32[]{:S(2)}) collective-permute-start(bf16[576,128]{1,0:T(8,128)(2,1)S(1)} %add_convert_fusion.2), channel_id=1, source_target_pairs={{2,0},{4,2},{6,4},{7,6},{5,7},{3,5},{1,3},{0,1},{10,8},{12,10},{14... | collective-permute-start | bytes 442376 | tf_op jit(solution)/shard_map/ppermute | solution.py:367
  170.0 4.8 %collective-permute-start.22 = (bf16[576,128]{1,0:T(8,128)(2,1)S(1)}, bf16[576,128]{1,0:T(8,128)(2,1)S(1)}, u32[]{:S(2)}, u32[]{:S(2)}) collective-permute-start(bf16[576,128]{1,0:T(8,128)(2,1)S(1)} %add_convert_fusion.23), channel_id=1, source_target_pairs={{0,2},{2,4},{4,6},{6,7},{7,5},{5,3},{3,1},{1,0},{8,10},{10,12},{12... | collective-permute-start | bytes 442376 | tf_op jit(solution)/shard_map/ppermute | solution.py:367
  172.4 5.2 %collective-permute-start.29 = (bf16[576,128]{1,0:T(8,128)(2,1)S(1)}, bf16[576,128]{1,0:T(8,128)(2,1)S(1)}, u32[]{:S(2)}, u32[]{:S(2)}) collective-permute-start(bf16[576,128]{1,0:T(8,128)(2,1)S(1)} %add_convert_fusion.16), channel_id=1, source_target_pairs={{0,2},{2,4},{4,6},{6,7},{7,5},{5,3},{3,1},{1,0},{8,10},{10,12},{12... | collective-permute-start | bytes 442376 | tf_op jit(solution)/shard_map/ppermute | solution.py:367
  173.3 6.6 %collective-permute-start.37 = (bf16[576,128]{1,0:T(8,128)(2,1)S(1)}, bf16[576,128]{1,0:T(8,128)(2,1)S(1)}, u32[]{:S(2)}, u32[]{:S(2)}) collective-permute-start(bf16[576,128]{1,0:T(8,128)(2,1)S(1)} %add_convert_fusion.8), channel_id=1, source_target_pairs={{2,0},{4,2},{6,4},{7,6},{5,7},{3,5},{1,3},{0,1},{10,8},{12,10},{14... | collective-permute-start | bytes 442376 | tf_op jit(solution)/shard_map/ppermute | solution.py:367
  174.1 7.5 %collective-permute-start.44 = (bf16[576,128]{1,0:T(8,128)(2,1)S(1)}, bf16[576,128]{1,0:T(8,128)(2,1)S(1)}, u32[]{:S(2)}, u32[]{:S(2)}) collective-permute-start(bf16[576,128]{1,0:T(8,128)(2,1)S(1)} %add_convert_fusion.1), channel_id=1, source_target_pairs={{2,0},{4,2},{6,4},{7,6},{5,7},{3,5},{1,3},{0,1},{10,8},{12,10},{14... | collective-permute-start | bytes 442376 | tf_op jit(solution)/shard_map/ppermute | solution.py:367
  175.9 6.7 %collective-permute-start.23 = (bf16[576,128]{1,0:T(8,128)(2,1)S(1)}, bf16[576,128]{1,0:T(8,128)(2,1)S(1)}, u32[]{:S(2)}, u32[]{:S(2)}) collective-permute-start(bf16[576,128]{1,0:T(8,128)(2,1)S(1)} %add_convert_fusion.22), channel_id=1, source_target_pairs={{0,2},{2,4},{4,6},{6,7},{7,5},{5,3},{3,1},{1,0},{8,10},{10,12},{12... | collective-permute-start | bytes 442376 | tf_op jit(solution)/shard_map/ppermute | solution.py:367
  178.5 5.8 %collective-permute-start.30 = (bf16[576,128]{1,0:T(8,128)(2,1)S(1)}, bf16[576,128]{1,0:T(8,128)(2,1)S(1)}, u32[]{:S(2)}, u32[]{:S(2)}) collective-permute-start(bf16[576,128]{1,0:T(8,128)(2,1)S(1)} %add_convert_fusion.15), channel_id=1, source_target_pairs={{0,2},{2,4},{4,6},{6,7},{7,5},{5,3},{3,1},{1,0},{8,10},{10,12},{12... | collective-permute-start | bytes 442376 | tf_op jit(solution)/shard_map/ppermute | solution.py:367
  179.9 6.8 %collective-permute-start.38 = (bf16[576,128]{1,0:T(8,128)(2,1)S(1)}, bf16[576,128]{1,0:T(8,128)(2,1)S(1)}, u32[]{:S(2)}, u32[]{:S(2)}) collective-permute-start(bf16[576,128]{1,0:T(8,128)(2,1)S(1)} %add_convert_fusion.7), channel_id=1, source_target_pairs={{2,0},{4,2},{6,4},{7,6},{5,7},{3,5},{1,3},{0,1},{10,8},{12,10},{14... | collective-permute-start | bytes 442376 | tf_op jit(solution)/shard_map/ppermute | solution.py:367
  181.6 7.1 %collective-permute-start.45 = (bf16[576,128]{1,0:T(8,128)(2,1)S(1)}, bf16[576,128]{1,0:T(8,128)(2,1)S(1)}, u32[]{:S(2)}, u32[]{:S(2)}) collective-permute-start(bf16[576,128]{1,0:T(8,128)(2,1)S(1)} %add_convert_fusion), channel_id=1, source_target_pairs={{2,0},{4,2},{6,4},{7,6},{5,7},{3,5},{1,3},{0,1},{10,8},{12,10},{14... | collective-permute-start | bytes 442376 | tf_op jit(solution)/shard_map/ppermute | solution.py:367
  183.5 5.4 %collective-permute-start.24 = (bf16[576,128]{1,0:T(8,128)(2,1)S(1)}, bf16[576,128]{1,0:T(8,128)(2,1)S(1)}, u32[]{:S(2)}, u32[]{:S(2)}) collective-permute-start(bf16[576,128]{1,0:T(8,128)(2,1)S(1)} %add_convert_fusion.21), channel_id=1, source_target_pairs={{0,2},{2,4},{4,6},{6,7},{7,5},{5,3},{3,1},{1,0},{8,10},{10,12},{12... | collective-permute-start | bytes 442376 | tf_op jit(solution)/shard_map/ppermute | solution.py:367
  185.3 6.8 %collective-permute-start.31 = (bf16[576,128]{1,0:T(8,128)(2,1)S(1)}, bf16[576,128]{1,0:T(8,128)(2,1)S(1)}, u32[]{:S(2)}, u32[]{:S(2)}) collective-permute-start(bf16[576,128]{1,0:T(8,128)(2,1)S(1)} %add_convert_fusion.14), channel_id=1, source_target_pairs={{0,2},{2,4},{4,6},{6,7},{7,5},{5,3},{3,1},{1,0},{8,10},{10,12},{12... | collective-permute-start | bytes 442376 | tf_op jit(solution)/shard_map/ppermute | solution.py:367
  193.2 5.1 %collective-permute-start.46 = (bf16[576,128]{1,0:T(8,128)(2,1)S(1)}, bf16[576,128]{1,0:T(8,128)(2,1)S(1)}, u32[]{:S(2)}, u32[]{:S(2)}) collective-permute-start(bf16[576,128]{1,0:T(8,128)(2,1)S(1)} %get-tuple-element.158), channel_id=1, source_target_pairs={{0,2},{2,4},{4,6},{6,7},{7,5},{5,3},{3,1},{1,0},{8,10},{10,12},{12... | collective-permute-start | bytes 442376 | tf_op jit(solution)/shard_map/ppermute | solution.py:367
  194.1 5.4 %collective-permute-start.47 = (bf16[576,128]{1,0:T(8,128)(2,1)S(1)}, bf16[576,128]{1,0:T(8,128)(2,1)S(1)}, u32[]{:S(2)}, u32[]{:S(2)}) collective-permute-start(bf16[576,128]{1,0:T(8,128)(2,1)S(1)} %get-tuple-element.158), channel_id=1, source_target_pairs={{2,0},{4,2},{6,4},{7,6},{5,7},{3,5},{1,3},{0,1},{10,8},{12,10},{14... | collective-permute-start | bytes 442376 | tf_op jit(solution)/shard_map/ppermute | solution.py:367
  194.7 6.0 %collective-permute-start.53 = (bf16[576,128]{1,0:T(8,128)(2,1)S(1)}, bf16[576,128]{1,0:T(8,128)(2,1)S(1)}, u32[]{:S(2)}, u32[]{:S(2)}) collective-permute-start(bf16[576,128]{1,0:T(8,128)(2,1)S(1)} %get-tuple-element.159), channel_id=1, source_target_pairs={{0,2},{2,4},{4,6},{6,7},{7,5},{5,3},{3,1},{1,0},{8,10},{10,12},{12... | collective-permute-start | bytes 442376 | tf_op jit(solution)/shard_map/ppermute | solution.py:367
  195.5 6.0 %collective-permute-start.54 = (bf16[576,128]{1,0:T(8,128)(2,1)S(1)}, bf16[576,128]{1,0:T(8,128)(2,1)S(1)}, u32[]{:S(2)}, u32[]{:S(2)}) collective-permute-start(bf16[576,128]{1,0:T(8,128)(2,1)S(1)} %get-tuple-element.159), channel_id=1, source_target_pairs={{2,0},{4,2},{6,4},{7,6},{5,7},{3,5},{1,3},{0,1},{10,8},{12,10},{14... | collective-permute-start | bytes 442376 | tf_op jit(solution)/shard_map/ppermute | solution.py:367
  198.3 4.0 %collective-permute-start.48 = (bf16[576,128]{1,0:T(8,128)(2,1)S(1)}, bf16[576,128]{1,0:T(8,128)(2,1)S(1)}, u32[]{:S(2)}, u32[]{:S(2)}) collective-permute-start(bf16[576,128]{1,0:T(8,128)(2,1)S(1)} %collective-permute-done.46), channel_id=1, source_target_pairs={{0,2},{2,4},{4,6},{6,7},{7,5},{5,3},{3,1},{1,0},{8,10},{10,12},{12... | collective-permute-start | bytes 442376 | tf_op jit(solution)/shard_map/ppermute | solution.py:367
  199.5 4.0 %collective-permute-start.49 = (bf16[576,128]{1,0:T(8,128)(2,1)S(1)}, bf16[576,128]{1,0:T(8,128)(2,1)S(1)}, u32[]{:S(2)}, u32[]{:S(2)}) collective-permute-start(bf16[576,128]{1,0:T(8,128)(2,1)S(1)} %collective-permute-done.47), channel_id=1, source_target_pairs={{2,0},{4,2},{6,4},{7,6},{5,7},{3,5},{1,3},{0,1},{10,8},{12,10},{14... | collective-permute-start | bytes 442376 | tf_op jit(solution)/shard_map/ppermute | solution.py:367
  200.7 4.0 %collective-permute-start.55 = (bf16[576,128]{1,0:T(8,128)(2,1)S(1)}, bf16[576,128]{1,0:T(8,128)(2,1)S(1)}, u32[]{:S(2)}, u32[]{:S(2)}) collective-permute-start(bf16[576,128]{1,0:T(8,128)(2,1)S(1)} %collective-permute-done.53), channel_id=1, source_target_pairs={{0,2},{2,4},{4,6},{6,7},{7,5},{5,3},{3,1},{1,0},{8,10},{10,12},{12... | collective-permute-start | bytes 442376 | tf_op jit(solution)/shard_map/ppermute | solution.py:367
  201.5 4.3 %collective-permute-start.56 = (bf16[576,128]{1,0:T(8,128)(2,1)S(1)}, bf16[576,128]{1,0:T(8,128)(2,1)S(1)}, u32[]{:S(2)}, u32[]{:S(2)}) collective-permute-start(bf16[576,128]{1,0:T(8,128)(2,1)S(1)} %collective-permute-done.54), channel_id=1, source_target_pairs={{2,0},{4,2},{6,4},{7,6},{5,7},{3,5},{1,3},{0,1},{10,8},{12,10},{14... | collective-permute-start | bytes 442376 | tf_op jit(solution)/shard_map/ppermute | solution.py:367
  202.3 5.7 %collective-permute-start.50 = (bf16[576,128]{1,0:T(8,128)(2,1)S(1)}, bf16[576,128]{1,0:T(8,128)(2,1)S(1)}, u32[]{:S(2)}, u32[]{:S(2)}) collective-permute-start(bf16[576,128]{1,0:T(8,128)(2,1)S(1)} %collective-permute-done.48), channel_id=1, source_target_pairs={{0,2},{2,4},{4,6},{6,7},{7,5},{5,3},{3,1},{1,0},{8,10},{10,12},{12... | collective-permute-start | bytes 442376 | tf_op jit(solution)/shard_map/ppermute | solution.py:367
  203.5 9.2 %collective-permute-start.51 = (bf16[576,128]{1,0:T(8,128)(2,1)S(1)}, bf16[576,128]{1,0:T(8,128)(2,1)S(1)}, u32[]{:S(2)}, u32[]{:S(2)}) collective-permute-start(bf16[576,128]{1,0:T(8,128)(2,1)S(1)} %collective-permute-done.49), channel_id=1, source_target_pairs={{2,0},{4,2},{6,4},{7,6},{5,7},{3,5},{1,3},{0,1},{10,8},{12,10},{14... | collective-permute-start | bytes 442376 | tf_op jit(solution)/shard_map/ppermute | solution.py:367
  204.6 7.9 %collective-permute-start.57 = (bf16[576,128]{1,0:T(8,128)(2,1)S(1)}, bf16[576,128]{1,0:T(8,128)(2,1)S(1)}, u32[]{:S(2)}, u32[]{:S(2)}) collective-permute-start(bf16[576,128]{1,0:T(8,128)(2,1)S(1)} %collective-permute-done.55), channel_id=1, source_target_pairs={{0,2},{2,4},{4,6},{6,7},{7,5},{5,3},{3,1},{1,0},{8,10},{10,12},{12... | collective-permute-start | bytes 442376 | tf_op jit(solution)/shard_map/ppermute | solution.py:367
  205.9 6.4 %collective-permute-start.58 = (bf16[576,128]{1,0:T(8,128)(2,1)S(1)}, bf16[576,128]{1,0:T(8,128)(2,1)S(1)}, u32[]{:S(2)}, u32[]{:S(2)}) collective-permute-start(bf16[576,128]{1,0:T(8,128)(2,1)S(1)} %collective-permute-done.56), channel_id=1, source_target_pairs={{2,0},{4,2},{6,4},{7,6},{5,7},{3,5},{1,3},{0,1},{10,8},{12,10},{14... | collective-permute-start | bytes 442376 | tf_op jit(solution)/shard_map/ppermute | solution.py:367
  208.0 5.9 %collective-permute-start.52 = (bf16[576,128]{1,0:T(8,128)(2,1)S(1)}, bf16[576,128]{1,0:T(8,128)(2,1)S(1)}, u32[]{:S(2)}, u32[]{:S(2)}) collective-permute-start(bf16[576,128]{1,0:T(8,128)(2,1)S(1)} %collective-permute-done.50), channel_id=1, source_target_pairs={{0,2},{2,4},{4,6},{6,7},{7,5},{5,3},{3,1},{1,0},{8,10},{10,12},{12... | collective-permute-start | bytes 442376 | tf_op jit(solution)/shard_map/ppermute | solution.py:367
  212.3 5.1 %collective-permute-start.59 = (bf16[576,128]{1,0:T(8,128)(2,1)S(1)}, bf16[576,128]{1,0:T(8,128)(2,1)S(1)}, u32[]{:S(2)}, u32[]{:S(2)}) collective-permute-start(bf16[576,128]{1,0:T(8,128)(2,1)S(1)} %collective-permute-done.58), channel_id=1, source_target_pairs={{2,0},{4,2},{6,4},{7,6},{5,7},{3,5},{1,3},{0,1},{10,8},{12,10},{14... | collective-permute-start | bytes 442376 | tf_op jit(solution)/shard_map/ppermute | solution.py:367
  219.0 0.7 collective-permute-start.60
  221.4 0.7 collective-permute-start.61
  223.8 30.1 %collective-permute-start.62 = (bf16[32,4608]{1,0:T(8,128)(2,1)}, bf16[32,4608]{1,0:T(8,128)(2,1)}, u32[]{:S(2)}, u32[]{:S(2)}) collective-permute-start(bf16[32,4608]{1,0:T(8,128)(2,1)} %fusion.2), channel_id=1, source_target_pairs={{16,24},{17,25},{18,26},{19,27},{20,28},{21,29},{22,30},{23,31}} | collective-permute-start | bytes 884744 | tf_op jit(solution)/shard_map/ppermute | solution.py:367
  (21 other events, 122.8 us)
